TPU v7x, 128 devices: a whole 4x4x4 slice. The times are simulated.
128 devices in a mesh: aa: 16 (over y, x), ba: 8 (over z, core).
Axes of the slice: x: 4, y: 4, z: 4, core: 2. Of those that a mesh axis runs over, the one named last changes fastest.
Arguments:
- bricks: bfloat16 [16384, 4096], P(('aa', 'ba')), may hold values from -6 to 6
- transfer: float32 [2, 4], replicated, may hold values from -1.5 to 1.5
- assignment: int32 [16384, 1], replicated, may hold values from 0 to 127; in each aligned block of 128 rows (0 to 127, 128 to 255, ...) at most 2 rows name the same one
- brick_cell: int32 [16384], replicated, may hold values from 0 to 16383, each once
- depth_rank: int32 [2, 16384], replicated, may hold values from 0 to 16383, each once within a row
Outputs:
- frame_z: float32 [4, 128, 2048], P(None, 'ba', 'aa')
- frame_x: float32 [4, 128, 2048], P(None, 'ba', 'aa')
Inputs may be any that keep to these rules, and one draw needn't show every extreme that they name: `assignment`: within each aligned block of 128 rows (the bricks stored on one device) no renderer is named by more than 2 rows; every renderer is named by some row. `brick_cell`: each grid cell holds exactly one brick. `depth_rank`: each row names every brick once.
All inputs are finite; a program needn't handle non-finite values.
Results may differ from a plain program's by a relative error of at most 0.0003.
Values may be sent and summed in bfloat16 or wider, within the bound.
No kernel may reach another device: no remote copies, remote signals or barrier semaphores. Data moves between devices by JAX's collectives and lax.ppermute only.
A program may use at most 128 MiB of HBM per device.

v0:
```python
import math

import jax
import jax.numpy as jnp
from jax import lax
from jax.sharding import PartitionSpec as P

SIDE = 1024
EDGE = 16


def swapped(block, axis, apart):
    count = lax.axis_size(axis)
    route = []
    for low in range(count):
        high = low | 1 << apart
        if high != low and high < count:
            route += [(low, high), (high, low)]
    return lax.ppermute(block, axis, route)


def upsample_matrix(brick_edge):
    row_ids = jnp.arange(2 * brick_edge)[:, None]
    col_ids = jnp.arange(brick_edge)[None, :]
    centre = row_ids // 2
    beside = jnp.clip(jnp.where(row_ids % 2 == 0, centre - 1, centre + 1), 0, brick_edge - 1)
    return 0.75 * (col_ids == centre).astype(jnp.float32) + 0.25 * (col_ids == beside).astype(
        jnp.float32
    )


def classify(samples, transfer):
    slopes = transfer[0]
    offsets = transfer[1]
    density = 2.0 * jax.nn.softplus(slopes[0] * samples + offsets[0]) / SIDE
    colours = [
        jax.nn.sigmoid(slopes[channel] * samples + offsets[channel]) for channel in (1, 2, 3)
    ]
    return (density, colours)


def march_slices(density, colours):
    length = density.shape[1]
    lower_part = (jnp.arange(length)[None, :] < jnp.arange(length)[:, None]).astype(jnp.float32)
    before = jnp.einsum("ab,nbp->nap", lower_part, density, precision=lax.Precision.HIGHEST)
    weight = -jnp.expm1(-density) * jnp.exp(-before)
    pieces = [jnp.sum(colour * weight, axis=1) for colour in colours] + [jnp.sum(density, axis=1)]
    return jnp.stack(pieces, axis=1)


def render_cells(cells, transfer):
    number = cells.shape[0]
    matrix = upsample_matrix(EDGE)
    plane_weights = jnp.kron(matrix, matrix).astype(jnp.bfloat16)
    volume = cells.reshape(number, EDGE, EDGE, EDGE)
    facing_z = jnp.einsum(
        "nxyz,pyx->nzp",
        volume,
        plane_weights.reshape(-1, EDGE, EDGE),
        preferred_element_type=jnp.float32,
    )
    facing_x = jnp.einsum(
        "nxq,pq->nxp",
        cells.reshape(number, EDGE, EDGE * EDGE),
        plane_weights,
        preferred_element_type=jnp.float32,
    )
    results = []
    for facing in (facing_z, facing_x):
        samples = jnp.einsum("ak,nkp->nap", matrix, facing, precision=lax.Precision.HIGHEST)
        density, colours = classify(samples, transfer)
        results.append(march_slices(density, colours))
    return (results[0], results[1])


def render_all(cells, transfer):
    brick_total = cells.shape[0]
    group_size = math.gcd(brick_total, 16)
    grouped = cells.reshape(brick_total // group_size, group_size, cells.shape[1])
    tiles_z, tiles_x = lax.map(lambda members: render_cells(members, transfer), grouped)
    return (tiles_z.reshape(brick_total, 4, -1), tiles_x.reshape(brick_total, 4, -1))


def partial_picture(tile_data, footprint, ranks, filled, footprints):
    slots = tile_data.shape[0]
    live_mask = filled.astype(jnp.float32)
    tile_data = tile_data * live_mask[:, None, None]
    optical = tile_data[:, 3]
    ahead_mask = (
        (footprint[:, None] == footprint[None, :])
        & (ranks[None, :] < ranks[:, None])
        & filled[None, :]
    )
    in_front = jnp.dot(ahead_mask.astype(jnp.float32), optical, precision=lax.Precision.HIGHEST)
    shaded = jnp.concatenate(
        [tile_data[:, :3] * jnp.exp(-in_front)[:, None], optical[:, None]], axis=1
    )
    scatter_rows = (
        (jnp.arange(footprints)[:, None] == footprint[None, :]) & filled[None, :]
    ).astype(jnp.float32)
    placed = jnp.dot(scatter_rows, shaded.reshape(slots, -1), precision=lax.Precision.HIGHEST)
    tile_side = 2 * EDGE
    across = SIDE // EDGE
    layers = footprints // across
    placed = placed.reshape(layers, across, 4, tile_side, tile_side).transpose(2, 0, 3, 1, 4)
    return placed.reshape(4, layers * tile_side, across * tile_side)


def over_merge(nearer, farther):
    shading = jnp.exp(-nearer[3:4])
    return jnp.concatenate([nearer[:3] + shading * farther[:3], nearer[3:4] + farther[3:4]], axis=0)


def split_half(values, split_dim, my_bit):
    dims_now = values.shape
    paired = values.reshape(
        dims_now[:split_dim] + (dims_now[split_dim] // 2, 2) + dims_now[split_dim + 1 :]
    )
    lower_half = lax.index_in_dim(paired, 0, split_dim + 1, keepdims=False)
    upper_half = lax.index_in_dim(paired, 1, split_dim + 1, keepdims=False)
    retain = jnp.where(my_bit == 1, upper_half, lower_half)
    handed = jnp.where(my_bit == 1, lower_half, upper_half)
    return (retain, handed)


def merge_pair(retain, arrived, my_bit):
    return jnp.where(my_bit == 0, over_merge(retain, arrived), over_merge(arrived, retain))


def finish(merged):
    return jnp.concatenate([merged[:3], -jnp.expm1(-merged[3:4])], axis=0)


def body(bricks, transfer, assignment, brick_cell, depth_rank):
    aa_count = lax.axis_size("aa")
    ba_count = lax.axis_size("ba")
    devices = aa_count * ba_count
    aa_index = lax.axis_index("aa")
    ba_index = lax.axis_index("ba")
    device_index = aa_index * ba_count + ba_index
    per_device = bricks.shape[0]
    brick_total = brick_cell.shape[0]
    capacity = max(2, 2 * per_device // devices)
    renderer = assignment[:, 0]
    target = renderer % aa_count * ba_count + renderer // aa_count
    own_target = lax.dynamic_slice_in_dim(target, device_index * per_device, per_device)
    positions = jnp.arange(per_device)
    earlier = (positions[None, :] < positions[:, None]) & (
        own_target[None, :] == own_target[:, None]
    )
    slot_of = own_target * capacity + jnp.sum(earlier.astype(jnp.int32), axis=1)
    targets_grid = target.reshape(devices, per_device)
    for_me = (targets_grid == device_index).astype(jnp.int32)
    standing = jnp.cumsum(for_me, axis=1) - 1
    matches = (for_me[:, :, None] == 1) & (
        standing[:, :, None] == jnp.arange(capacity)[None, None, :]
    )
    filled = jnp.any(matches, axis=1).reshape(-1)
    global_ids = jnp.arange(brick_total).reshape(devices, per_device)
    brick_ids = jnp.sum(matches.astype(jnp.int32) * global_ids[:, :, None], axis=1).reshape(-1)
    across = SIDE // EDGE
    cells_here = brick_cell[brick_ids]
    column_x = cells_here % across
    column_z = cells_here // across % across
    layer_index = cells_here // (across * across)
    foot_z = layer_index * across + column_x
    foot_x = layer_index * across + column_z
    rank_z = depth_rank[0][brick_ids]
    rank_x = depth_rank[1][brick_ids]
    slot_total = devices * capacity
    outbox = jnp.zeros((slot_total, bricks.shape[1]), jnp.bfloat16).at[slot_of].set(bricks)
    received = lax.all_to_all(
        outbox.reshape(devices, capacity, bricks.shape[1]),
        ("aa", "ba"),
        split_axis=0,
        concat_axis=0,
        tiled=True,
    )
    tiles_z, tiles_x = render_all(received.reshape(slot_total, bricks.shape[1]), transfer)
    footprints = brick_total // across
    picture_z = partial_picture(tiles_z, foot_z, rank_z, filled, footprints)
    picture_x = partial_picture(tiles_x, foot_x, rank_x, filled, footprints)
    row_total = picture_z.shape[1]
    col_total = picture_z.shape[2]
    row_part = row_total // ba_count
    col_part = col_total // aa_count
    current = [
        picture.reshape(4, row_total, aa_count, col_part) for picture in (picture_z, picture_x)
    ]
    for level_bit in range(aa_count.bit_length() - 1):
        my_bit = aa_index >> level_bit & 1
        halves = [split_half(values, 2, my_bit) for values in current]
        arrived = swapped((halves[0][1], halves[1][1]), "aa", level_bit)
        current = [merge_pair(pair[0], landed, my_bit) for pair, landed in zip(halves, arrived)]
    current = [values.reshape(4, ba_count, row_part, col_part) for values in current]
    for level_bit in range(ba_count.bit_length() - 1):
        my_bit = ba_index >> level_bit & 1
        halves = [split_half(values, 1, my_bit) for values in current]
        arrived = swapped((halves[0][1], halves[1][1]), "ba", level_bit)
        current = [merge_pair(pair[0], landed, my_bit) for pair, landed in zip(halves, arrived)]
    result_z = current[0].reshape(4, row_part, col_part)
    result_x = current[1].reshape(4, row_part, col_part)
    return (finish(result_z), finish(result_x))


def solution(mesh):
    in_specs = (P(("aa", "ba"), None), P(), P(), P(), P())
    out_specs = (P(None, "ba", "aa"), P(None, "ba", "aa"))
    return jax.shard_map(body, mesh=mesh, in_specs=in_specs, out_specs=out_specs, check_vma=False)
```

profile of v0, /device:TPU:0, one launch (start us, length us, event | category | flops | bytes accessed | tf_op | source)
XLA Modules:
  0.0 881.1 jit_solution(4411816079871706596)
XLA Ops:
  9.5 11.1 %all-to-all-start = ((bf16[128,2,4096]{2,1,0:T(2,128)(2,1)}), bf16[128,2,4096]{2,1,0:T(2,128)(2,1)S(1)}, u32[]{:S(2)}, u32[]{:S(2)}) async-start(bf16[128,2,4096]{2,1,0:T(2,128)(2,1)} %reshape.1251), calls=%async_computation | async-start | bytes 4194304 | tf_op jit(solution)/shard_map/all_to_all | solution.py:172
  30.3 20.8 %all-to-all-done = bf16[128,2,4096]{2,1,0:T(2,128)(2,1)S(1)} async-done(((bf16[128,2,4096]{2,1,0:T(2,128)(2,1)}), bf16[128,2,4096]{2,1,0:T(2,128)(2,1)S(1)}, u32[]{:S(2)}, u32[]{:S(2)}) %all-to-all-start) | async-done | bytes 2097184 | tf_op jit(solution)/shard_map/all_to_all | solution.py:172
  53.3 579.2 %while.15 = (s32[]{:T(128)}, f32[16,16,4,1024]{3,2,1,0:T(4,128)}, f32[16,16,4,1024]{3,2,1,0:T(4,128)}, f32[2,4]{1,0:T(2,128)S(1)}, bf16[16,16,4096]{2,1,0:T(8,128)(2,1)}, /*index=5*/s32[]{:T(128)}) while((s32[]{:T(128)}, f32[16,16,4,1024]{3,2,1,0:T(4,128)}, f32[16,16,4,1024]{3,2,1,0:T(4,128)}, f32[2,4]{1,0:T(2,128)S(1)}, ...), condition=%wide.region_14.15_spmd, body=%wide.region_5.14_spmd.sunk | while | flops 919873792 | bytes 18884296 | solution.py:80
  60.1 12.0 %fusion.179 = (f32[16,1024]{1,0:T(8,128)S(1)}, f32[16,1024]{1,0:T(8,128)S(1)}, f32[16,1024]{1,0:T(8,128)S(1)}, f32[16,1024]{1,0:T(8,128)S(1)}) fusion(f32[16,1024,32]{1,2,0:T(8,128)S(1)} %fusion.178, f32[]{:T(128)} %bitcast.620, f32[]{:T(128)} %bitcast.621, f32[]{:T(128)} %bitcast.622, f32[]{:T(128)} %bitcast.623, f32[]{:T(128)} %bitcast.624, ...), kind=kOutput, calls=%fused_computation.21.clone.1 | convolution fusion | flops 224330752 | bytes 2359328 | tf_op jit(solution)/shard_map/while/body/eval_jaxpr/ab,nbp->nap/dot_general | solution.py:45
  76.2 12.0 %fusion.176 = (f32[16,1024]{1,0:T(8,128)S(1)}, f32[16,1024]{1,0:T(8,128)S(1)}, f32[16,1024]{1,0:T(8,128)S(1)}, f32[16,1024]{1,0:T(8,128)S(1)}) fusion(f32[16,1024,32]{1,2,0:T(8,128)S(1)} %fusion.174, f32[]{:T(128)} %bitcast.620, f32[]{:T(128)} %bitcast.621, f32[]{:T(128)} %bitcast.622, f32[]{:T(128)} %bitcast.623, f32[]{:T(128)} %bitcast.624, ...), kind=kOutput, calls=%fused_computation.34.clone.1 | convolution fusion | flops 224330752 | bytes 2359328 | tf_op jit(solution)/shard_map/while/body/eval_jaxpr/ab,nbp->nap/dot_general | solution.py:45
  96.3 12.0 %fusion.179 = (f32[16,1024]{1,0:T(8,128)S(1)}, f32[16,1024]{1,0:T(8,128)S(1)}, f32[16,1024]{1,0:T(8,128)S(1)}, f32[16,1024]{1,0:T(8,128)S(1)}) fusion(f32[16,1024,32]{1,2,0:T(8,128)S(1)} %fusion.178, f32[]{:T(128)} %bitcast.620, f32[]{:T(128)} %bitcast.621, f32[]{:T(128)} %bitcast.622, f32[]{:T(128)} %bitcast.623, f32[]{:T(128)} %bitcast.624, ...), kind=kOutput, calls=%fused_computation.21.clone.1 | convolution fusion | flops 224330752 | bytes 2359328 | tf_op jit(solution)/shard_map/while/body/eval_jaxpr/ab,nbp->nap/dot_general | solution.py:45
  112.3 12.0 %fusion.176 = (f32[16,1024]{1,0:T(8,128)S(1)}, f32[16,1024]{1,0:T(8,128)S(1)}, f32[16,1024]{1,0:T(8,128)S(1)}, f32[16,1024]{1,0:T(8,128)S(1)}) fusion(f32[16,1024,32]{1,2,0:T(8,128)S(1)} %fusion.174, f32[]{:T(128)} %bitcast.620, f32[]{:T(128)} %bitcast.621, f32[]{:T(128)} %bitcast.622, f32[]{:T(128)} %bitcast.623, f32[]{:T(128)} %bitcast.624, ...), kind=kOutput, calls=%fused_computation.34.clone.1 | convolution fusion | flops 224330752 | bytes 2359328 | tf_op jit(solution)/shard_map/while/body/eval_jaxpr/ab,nbp->nap/dot_general | solution.py:45
  132.4 12.0 %fusion.179 = (f32[16,1024]{1,0:T(8,128)S(1)}, f32[16,1024]{1,0:T(8,128)S(1)}, f32[16,1024]{1,0:T(8,128)S(1)}, f32[16,1024]{1,0:T(8,128)S(1)}) fusion(f32[16,1024,32]{1,2,0:T(8,128)S(1)} %fusion.178, f32[]{:T(128)} %bitcast.620, f32[]{:T(128)} %bitcast.621, f32[]{:T(128)} %bitcast.622, f32[]{:T(128)} %bitcast.623, f32[]{:T(128)} %bitcast.624, ...), kind=kOutput, calls=%fused_computation.21.clone.1 | convolution fusion | flops 224330752 | bytes 2359328 | tf_op jit(solution)/shard_map/while/body/eval_jaxpr/ab,nbp->nap/dot_general | solution.py:45
  148.5 12.0 %fusion.176 = (f32[16,1024]{1,0:T(8,128)S(1)}, f32[16,1024]{1,0:T(8,128)S(1)}, f32[16,1024]{1,0:T(8,128)S(1)}, f32[16,1024]{1,0:T(8,128)S(1)}) fusion(f32[16,1024,32]{1,2,0:T(8,128)S(1)} %fusion.174, f32[]{:T(128)} %bitcast.620, f32[]{:T(128)} %bitcast.621, f32[]{:T(128)} %bitcast.622, f32[]{:T(128)} %bitcast.623, f32[]{:T(128)} %bitcast.624, ...), kind=kOutput, calls=%fused_computation.34.clone.1 | convolution fusion | flops 224330752 | bytes 2359328 | tf_op jit(solution)/shard_map/while/body/eval_jaxpr/ab,nbp->nap/dot_general | solution.py:45
  168.6 12.0 %fusion.179 = (f32[16,1024]{1,0:T(8,128)S(1)}, f32[16,1024]{1,0:T(8,128)S(1)}, f32[16,1024]{1,0:T(8,128)S(1)}, f32[16,1024]{1,0:T(8,128)S(1)}) fusion(f32[16,1024,32]{1,2,0:T(8,128)S(1)} %fusion.178, f32[]{:T(128)} %bitcast.620, f32[]{:T(128)} %bitcast.621, f32[]{:T(128)} %bitcast.622, f32[]{:T(128)} %bitcast.623, f32[]{:T(128)} %bitcast.624, ...), kind=kOutput, calls=%fused_computation.21.clone.1 | convolution fusion | flops 224330752 | bytes 2359328 | tf_op jit(solution)/shard_map/while/body/eval_jaxpr/ab,nbp->nap/dot_general | solution.py:45
  184.6 12.0 %fusion.176 = (f32[16,1024]{1,0:T(8,128)S(1)}, f32[16,1024]{1,0:T(8,128)S(1)}, f32[16,1024]{1,0:T(8,128)S(1)}, f32[16,1024]{1,0:T(8,128)S(1)}) fusion(f32[16,1024,32]{1,2,0:T(8,128)S(1)} %fusion.174, f32[]{:T(128)} %bitcast.620, f32[]{:T(128)} %bitcast.621, f32[]{:T(128)} %bitcast.622, f32[]{:T(128)} %bitcast.623, f32[]{:T(128)} %bitcast.624, ...), kind=kOutput, calls=%fused_computation.34.clone.1 | convolution fusion | flops 224330752 | bytes 2359328 | tf_op jit(solution)/shard_map/while/body/eval_jaxpr/ab,nbp->nap/dot_general | solution.py:45
  204.8 12.0 %fusion.179 = (f32[16,1024]{1,0:T(8,128)S(1)}, f32[16,1024]{1,0:T(8,128)S(1)}, f32[16,1024]{1,0:T(8,128)S(1)}, f32[16,1024]{1,0:T(8,128)S(1)}) fusion(f32[16,1024,32]{1,2,0:T(8,128)S(1)} %fusion.178, f32[]{:T(128)} %bitcast.620, f32[]{:T(128)} %bitcast.621, f32[]{:T(128)} %bitcast.622, f32[]{:T(128)} %bitcast.623, f32[]{:T(128)} %bitcast.624, ...), kind=kOutput, calls=%fused_computation.21.clone.1 | convolution fusion | flops 224330752 | bytes 2359328 | tf_op jit(solution)/shard_map/while/body/eval_jaxpr/ab,nbp->nap/dot_general | solution.py:45
  220.8 12.0 %fusion.176 = (f32[16,1024]{1,0:T(8,128)S(1)}, f32[16,1024]{1,0:T(8,128)S(1)}, f32[16,1024]{1,0:T(8,128)S(1)}, f32[16,1024]{1,0:T(8,128)S(1)}) fusion(f32[16,1024,32]{1,2,0:T(8,128)S(1)} %fusion.174, f32[]{:T(128)} %bitcast.620, f32[]{:T(128)} %bitcast.621, f32[]{:T(128)} %bitcast.622, f32[]{:T(128)} %bitcast.623, f32[]{:T(128)} %bitcast.624, ...), kind=kOutput, calls=%fused_computation.34.clone.1 | convolution fusion | flops 224330752 | bytes 2359328 | tf_op jit(solution)/shard_map/while/body/eval_jaxpr/ab,nbp->nap/dot_general | solution.py:45
  240.9 12.0 %fusion.179 = (f32[16,1024]{1,0:T(8,128)S(1)}, f32[16,1024]{1,0:T(8,128)S(1)}, f32[16,1024]{1,0:T(8,128)S(1)}, f32[16,1024]{1,0:T(8,128)S(1)}) fusion(f32[16,1024,32]{1,2,0:T(8,128)S(1)} %fusion.178, f32[]{:T(128)} %bitcast.620, f32[]{:T(128)} %bitcast.621, f32[]{:T(128)} %bitcast.622, f32[]{:T(128)} %bitcast.623, f32[]{:T(128)} %bitcast.624, ...), kind=kOutput, calls=%fused_computation.21.clone.1 | convolution fusion | flops 224330752 | bytes 2359328 | tf_op jit(solution)/shard_map/while/body/eval_jaxpr/ab,nbp->nap/dot_general | solution.py:45
  256.9 12.0 %fusion.176 = (f32[16,1024]{1,0:T(8,128)S(1)}, f32[16,1024]{1,0:T(8,128)S(1)}, f32[16,1024]{1,0:T(8,128)S(1)}, f32[16,1024]{1,0:T(8,128)S(1)}) fusion(f32[16,1024,32]{1,2,0:T(8,128)S(1)} %fusion.174, f32[]{:T(128)} %bitcast.620, f32[]{:T(128)} %bitcast.621, f32[]{:T(128)} %bitcast.622, f32[]{:T(128)} %bitcast.623, f32[]{:T(128)} %bitcast.624, ...), kind=kOutput, calls=%fused_computation.34.clone.1 | convolution fusion | flops 224330752 | bytes 2359328 | tf_op jit(solution)/shard_map/while/body/eval_jaxpr/ab,nbp->nap/dot_general | solution.py:45
  277.1 12.0 %fusion.179 = (f32[16,1024]{1,0:T(8,128)S(1)}, f32[16,1024]{1,0:T(8,128)S(1)}, f32[16,1024]{1,0:T(8,128)S(1)}, f32[16,1024]{1,0:T(8,128)S(1)}) fusion(f32[16,1024,32]{1,2,0:T(8,128)S(1)} %fusion.178, f32[]{:T(128)} %bitcast.620, f32[]{:T(128)} %bitcast.621, f32[]{:T(128)} %bitcast.622, f32[]{:T(128)} %bitcast.623, f32[]{:T(128)} %bitcast.624, ...), kind=kOutput, calls=%fused_computation.21.clone.1 | convolution fusion | flops 224330752 | bytes 2359328 | tf_op jit(solution)/shard_map/while/body/eval_jaxpr/ab,nbp->nap/dot_general | solution.py:45
  293.1 12.0 %fusion.176 = (f32[16,1024]{1,0:T(8,128)S(1)}, f32[16,1024]{1,0:T(8,128)S(1)}, f32[16,1024]{1,0:T(8,128)S(1)}, f32[16,1024]{1,0:T(8,128)S(1)}) fusion(f32[16,1024,32]{1,2,0:T(8,128)S(1)} %fusion.174, f32[]{:T(128)} %bitcast.620, f32[]{:T(128)} %bitcast.621, f32[]{:T(128)} %bitcast.622, f32[]{:T(128)} %bitcast.623, f32[]{:T(128)} %bitcast.624, ...), kind=kOutput, calls=%fused_computation.34.clone.1 | convolution fusion | flops 224330752 | bytes 2359328 | tf_op jit(solution)/shard_map/while/body/eval_jaxpr/ab,nbp->nap/dot_general | solution.py:45
  313.2 12.0 %fusion.179 = (f32[16,1024]{1,0:T(8,128)S(1)}, f32[16,1024]{1,0:T(8,128)S(1)}, f32[16,1024]{1,0:T(8,128)S(1)}, f32[16,1024]{1,0:T(8,128)S(1)}) fusion(f32[16,1024,32]{1,2,0:T(8,128)S(1)} %fusion.178, f32[]{:T(128)} %bitcast.620, f32[]{:T(128)} %bitcast.621, f32[]{:T(128)} %bitcast.622, f32[]{:T(128)} %bitcast.623, f32[]{:T(128)} %bitcast.624, ...), kind=kOutput, calls=%fused_computation.21.clone.1 | convolution fusion | flops 224330752 | bytes 2359328 | tf_op jit(solution)/shard_map/while/body/eval_jaxpr/ab,nbp->nap/dot_general | solution.py:45
  329.2 12.0 %fusion.176 = (f32[16,1024]{1,0:T(8,128)S(1)}, f32[16,1024]{1,0:T(8,128)S(1)}, f32[16,1024]{1,0:T(8,128)S(1)}, f32[16,1024]{1,0:T(8,128)S(1)}) fusion(f32[16,1024,32]{1,2,0:T(8,128)S(1)} %fusion.174, f32[]{:T(128)} %bitcast.620, f32[]{:T(128)} %bitcast.621, f32[]{:T(128)} %bitcast.622, f32[]{:T(128)} %bitcast.623, f32[]{:T(128)} %bitcast.624, ...), kind=kOutput, calls=%fused_computation.34.clone.1 | convolution fusion | flops 224330752 | bytes 2359328 | tf_op jit(solution)/shard_map/while/body/eval_jaxpr/ab,nbp->nap/dot_general | solution.py:45
  349.4 12.0 %fusion.179 = (f32[16,1024]{1,0:T(8,128)S(1)}, f32[16,1024]{1,0:T(8,128)S(1)}, f32[16,1024]{1,0:T(8,128)S(1)}, f32[16,1024]{1,0:T(8,128)S(1)}) fusion(f32[16,1024,32]{1,2,0:T(8,128)S(1)} %fusion.178, f32[]{:T(128)} %bitcast.620, f32[]{:T(128)} %bitcast.621, f32[]{:T(128)} %bitcast.622, f32[]{:T(128)} %bitcast.623, f32[]{:T(128)} %bitcast.624, ...), kind=kOutput, calls=%fused_computation.21.clone.1 | convolution fusion | flops 224330752 | bytes 2359328 | tf_op jit(solution)/shard_map/while/body/eval_jaxpr/ab,nbp->nap/dot_general | solution.py:45
  365.4 12.0 %fusion.176 = (f32[16,1024]{1,0:T(8,128)S(1)}, f32[16,1024]{1,0:T(8,128)S(1)}, f32[16,1024]{1,0:T(8,128)S(1)}, f32[16,1024]{1,0:T(8,128)S(1)}) fusion(f32[16,1024,32]{1,2,0:T(8,128)S(1)} %fusion.174, f32[]{:T(128)} %bitcast.620, f32[]{:T(128)} %bitcast.621, f32[]{:T(128)} %bitcast.622, f32[]{:T(128)} %bitcast.623, f32[]{:T(128)} %bitcast.624, ...), kind=kOutput, calls=%fused_computation.34.clone.1 | convolution fusion | flops 224330752 | bytes 2359328 | tf_op jit(solution)/shard_map/while/body/eval_jaxpr/ab,nbp->nap/dot_general | solution.py:45
  385.5 12.0 %fusion.179 = (f32[16,1024]{1,0:T(8,128)S(1)}, f32[16,1024]{1,0:T(8,128)S(1)}, f32[16,1024]{1,0:T(8,128)S(1)}, f32[16,1024]{1,0:T(8,128)S(1)}) fusion(f32[16,1024,32]{1,2,0:T(8,128)S(1)} %fusion.178, f32[]{:T(128)} %bitcast.620, f32[]{:T(128)} %bitcast.621, f32[]{:T(128)} %bitcast.622, f32[]{:T(128)} %bitcast.623, f32[]{:T(128)} %bitcast.624, ...), kind=kOutput, calls=%fused_computation.21.clone.1 | convolution fusion | flops 224330752 | bytes 2359328 | tf_op jit(solution)/shard_map/while/body/eval_jaxpr/ab,nbp->nap/dot_general | solution.py:45
  401.5 12.0 %fusion.176 = (f32[16,1024]{1,0:T(8,128)S(1)}, f32[16,1024]{1,0:T(8,128)S(1)}, f32[16,1024]{1,0:T(8,128)S(1)}, f32[16,1024]{1,0:T(8,128)S(1)}) fusion(f32[16,1024,32]{1,2,0:T(8,128)S(1)} %fusion.174, f32[]{:T(128)} %bitcast.620, f32[]{:T(128)} %bitcast.621, f32[]{:T(128)} %bitcast.622, f32[]{:T(128)} %bitcast.623, f32[]{:T(128)} %bitcast.624, ...), kind=kOutput, calls=%fused_computation.34.clone.1 | convolution fusion | flops 224330752 | bytes 2359328 | tf_op jit(solution)/shard_map/while/body/eval_jaxpr/ab,nbp->nap/dot_general | solution.py:45
  421.7 12.0 %fusion.179 = (f32[16,1024]{1,0:T(8,128)S(1)}, f32[16,1024]{1,0:T(8,128)S(1)}, f32[16,1024]{1,0:T(8,128)S(1)}, f32[16,1024]{1,0:T(8,128)S(1)}) fusion(f32[16,1024,32]{1,2,0:T(8,128)S(1)} %fusion.178, f32[]{:T(128)} %bitcast.620, f32[]{:T(128)} %bitcast.621, f32[]{:T(128)} %bitcast.622, f32[]{:T(128)} %bitcast.623, f32[]{:T(128)} %bitcast.624, ...), kind=kOutput, calls=%fused_computation.21.clone.1 | convolution fusion | flops 224330752 | bytes 2359328 | tf_op jit(solution)/shard_map/while/body/eval_jaxpr/ab,nbp->nap/dot_general | solution.py:45
  437.7 12.0 %fusion.176 = (f32[16,1024]{1,0:T(8,128)S(1)}, f32[16,1024]{1,0:T(8,128)S(1)}, f32[16,1024]{1,0:T(8,128)S(1)}, f32[16,1024]{1,0:T(8,128)S(1)}) fusion(f32[16,1024,32]{1,2,0:T(8,128)S(1)} %fusion.174, f32[]{:T(128)} %bitcast.620, f32[]{:T(128)} %bitcast.621, f32[]{:T(128)} %bitcast.622, f32[]{:T(128)} %bitcast.623, f32[]{:T(128)} %bitcast.624, ...), kind=kOutput, calls=%fused_computation.34.clone.1 | convolution fusion | flops 224330752 | bytes 2359328 | tf_op jit(solution)/shard_map/while/body/eval_jaxpr/ab,nbp->nap/dot_general | solution.py:45
  457.8 12.0 %fusion.179 = (f32[16,1024]{1,0:T(8,128)S(1)}, f32[16,1024]{1,0:T(8,128)S(1)}, f32[16,1024]{1,0:T(8,128)S(1)}, f32[16,1024]{1,0:T(8,128)S(1)}) fusion(f32[16,1024,32]{1,2,0:T(8,128)S(1)} %fusion.178, f32[]{:T(128)} %bitcast.620, f32[]{:T(128)} %bitcast.621, f32[]{:T(128)} %bitcast.622, f32[]{:T(128)} %bitcast.623, f32[]{:T(128)} %bitcast.624, ...), kind=kOutput, calls=%fused_computation.21.clone.1 | convolution fusion | flops 224330752 | bytes 2359328 | tf_op jit(solution)/shard_map/while/body/eval_jaxpr/ab,nbp->nap/dot_general | solution.py:45
  473.8 12.0 %fusion.176 = (f32[16,1024]{1,0:T(8,128)S(1)}, f32[16,1024]{1,0:T(8,128)S(1)}, f32[16,1024]{1,0:T(8,128)S(1)}, f32[16,1024]{1,0:T(8,128)S(1)}) fusion(f32[16,1024,32]{1,2,0:T(8,128)S(1)} %fusion.174, f32[]{:T(128)} %bitcast.620, f32[]{:T(128)} %bitcast.621, f32[]{:T(128)} %bitcast.622, f32[]{:T(128)} %bitcast.623, f32[]{:T(128)} %bitcast.624, ...), kind=kOutput, calls=%fused_computation.34.clone.1 | convolution fusion | flops 224330752 | bytes 2359328 | tf_op jit(solution)/shard_map/while/body/eval_jaxpr/ab,nbp->nap/dot_general | solution.py:45
  494.0 12.0 %fusion.179 = (f32[16,1024]{1,0:T(8,128)S(1)}, f32[16,1024]{1,0:T(8,128)S(1)}, f32[16,1024]{1,0:T(8,128)S(1)}, f32[16,1024]{1,0:T(8,128)S(1)}) fusion(f32[16,1024,32]{1,2,0:T(8,128)S(1)} %fusion.178, f32[]{:T(128)} %bitcast.620, f32[]{:T(128)} %bitcast.621, f32[]{:T(128)} %bitcast.622, f32[]{:T(128)} %bitcast.623, f32[]{:T(128)} %bitcast.624, ...), kind=kOutput, calls=%fused_computation.21.clone.1 | convolution fusion | flops 224330752 | bytes 2359328 | tf_op jit(solution)/shard_map/while/body/eval_jaxpr/ab,nbp->nap/dot_general | solution.py:45
  510.0 12.0 %fusion.176 = (f32[16,1024]{1,0:T(8,128)S(1)}, f32[16,1024]{1,0:T(8,128)S(1)}, f32[16,1024]{1,0:T(8,128)S(1)}, f32[16,1024]{1,0:T(8,128)S(1)}) fusion(f32[16,1024,32]{1,2,0:T(8,128)S(1)} %fusion.174, f32[]{:T(128)} %bitcast.620, f32[]{:T(128)} %bitcast.621, f32[]{:T(128)} %bitcast.622, f32[]{:T(128)} %bitcast.623, f32[]{:T(128)} %bitcast.624, ...), kind=kOutput, calls=%fused_computation.34.clone.1 | convolution fusion | flops 224330752 | bytes 2359328 | tf_op jit(solution)/shard_map/while/body/eval_jaxpr/ab,nbp->nap/dot_general | solution.py:45
  530.1 12.0 %fusion.179 = (f32[16,1024]{1,0:T(8,128)S(1)}, f32[16,1024]{1,0:T(8,128)S(1)}, f32[16,1024]{1,0:T(8,128)S(1)}, f32[16,1024]{1,0:T(8,128)S(1)}) fusion(f32[16,1024,32]{1,2,0:T(8,128)S(1)} %fusion.178, f32[]{:T(128)} %bitcast.620, f32[]{:T(128)} %bitcast.621, f32[]{:T(128)} %bitcast.622, f32[]{:T(128)} %bitcast.623, f32[]{:T(128)} %bitcast.624, ...), kind=kOutput, calls=%fused_computation.21.clone.1 | convolution fusion | flops 224330752 | bytes 2359328 | tf_op jit(solution)/shard_map/while/body/eval_jaxpr/ab,nbp->nap/dot_general | solution.py:45
  546.1 12.0 %fusion.176 = (f32[16,1024]{1,0:T(8,128)S(1)}, f32[16,1024]{1,0:T(8,128)S(1)}, f32[16,1024]{1,0:T(8,128)S(1)}, f32[16,1024]{1,0:T(8,128)S(1)}) fusion(f32[16,1024,32]{1,2,0:T(8,128)S(1)} %fusion.174, f32[]{:T(128)} %bitcast.620, f32[]{:T(128)} %bitcast.621, f32[]{:T(128)} %bitcast.622, f32[]{:T(128)} %bitcast.623, f32[]{:T(128)} %bitcast.624, ...), kind=kOutput, calls=%fused_computation.34.clone.1 | convolution fusion | flops 224330752 | bytes 2359328 | tf_op jit(solution)/shard_map/while/body/eval_jaxpr/ab,nbp->nap/dot_general | solution.py:45
  566.3 12.0 %fusion.179 = (f32[16,1024]{1,0:T(8,128)S(1)}, f32[16,1024]{1,0:T(8,128)S(1)}, f32[16,1024]{1,0:T(8,128)S(1)}, f32[16,1024]{1,0:T(8,128)S(1)}) fusion(f32[16,1024,32]{1,2,0:T(8,128)S(1)} %fusion.178, f32[]{:T(128)} %bitcast.620, f32[]{:T(128)} %bitcast.621, f32[]{:T(128)} %bitcast.622, f32[]{:T(128)} %bitcast.623, f32[]{:T(128)} %bitcast.624, ...), kind=kOutput, calls=%fused_computation.21.clone.1 | convolution fusion | flops 224330752 | bytes 2359328 | tf_op jit(solution)/shard_map/while/body/eval_jaxpr/ab,nbp->nap/dot_general | solution.py:45
  582.4 12.0 %fusion.176 = (f32[16,1024]{1,0:T(8,128)S(1)}, f32[16,1024]{1,0:T(8,128)S(1)}, f32[16,1024]{1,0:T(8,128)S(1)}, f32[16,1024]{1,0:T(8,128)S(1)}) fusion(f32[16,1024,32]{1,2,0:T(8,128)S(1)} %fusion.174, f32[]{:T(128)} %bitcast.620, f32[]{:T(128)} %bitcast.621, f32[]{:T(128)} %bitcast.622, f32[]{:T(128)} %bitcast.623, f32[]{:T(128)} %bitcast.624, ...), kind=kOutput, calls=%fused_computation.34.clone.1 | convolution fusion | flops 224330752 | bytes 2359328 | tf_op jit(solution)/shard_map/while/body/eval_jaxpr/ab,nbp->nap/dot_general | solution.py:45
  602.5 12.0 %fusion.179 = (f32[16,1024]{1,0:T(8,128)S(1)}, f32[16,1024]{1,0:T(8,128)S(1)}, f32[16,1024]{1,0:T(8,128)S(1)}, f32[16,1024]{1,0:T(8,128)S(1)}) fusion(f32[16,1024,32]{1,2,0:T(8,128)S(1)} %fusion.178, f32[]{:T(128)} %bitcast.620, f32[]{:T(128)} %bitcast.621, f32[]{:T(128)} %bitcast.622, f32[]{:T(128)} %bitcast.623, f32[]{:T(128)} %bitcast.624, ...), kind=kOutput, calls=%fused_computation.21.clone.1 | convolution fusion | flops 224330752 | bytes 2359328 | tf_op jit(solution)/shard_map/while/body/eval_jaxpr/ab,nbp->nap/dot_general | solution.py:45
  618.6 12.0 %fusion.176 = (f32[16,1024]{1,0:T(8,128)S(1)}, f32[16,1024]{1,0:T(8,128)S(1)}, f32[16,1024]{1,0:T(8,128)S(1)}, f32[16,1024]{1,0:T(8,128)S(1)}) fusion(f32[16,1024,32]{1,2,0:T(8,128)S(1)} %fusion.174, f32[]{:T(128)} %bitcast.620, f32[]{:T(128)} %bitcast.621, f32[]{:T(128)} %bitcast.622, f32[]{:T(128)} %bitcast.623, f32[]{:T(128)} %bitcast.624, ...), kind=kOutput, calls=%fused_computation.34.clone.1 | convolution fusion | flops 224330752 | bytes 2359328 | tf_op jit(solution)/shard_map/while/body/eval_jaxpr/ab,nbp->nap/dot_general | solution.py:45
  648.8 5.3 copy.296
  654.0 7.6 convolution_bitcast_fusion.1
  661.6 12.3 %copy.297 = f32[4,4,32,64,32]{4,3,2,1,0:T(8,128)} copy(f32[4,4,32,64,32]{3,4,2,0,1:T(8,128)} %convolution_bitcast_fusion.1) | data formatting | bytes 8388608 | tf_op jit(solution)/shard_map/transpose | solution.py:105
  673.9 12.9 %reshape_reshape_reshape.7 = f32[4,128,8,2,128]{4,3,2,1,0:T(2,128)} reshape(f32[4,4,32,64,32]{4,3,2,1,0:T(8,128)} %copy.297) | data formatting | bytes 8388608 | tf_op jit(solution)/shard_map/reshape;reshape;reshape | solution.py:116
  686.8 7.2 fusion.139
  706.2 7.6 convolution_bitcast_fusion.2
  713.8 12.3 %copy.251 = f32[4,4,32,64,32]{4,3,2,1,0:T(8,128)} copy(f32[4,4,32,64,32]{3,4,2,0,1:T(8,128)} %convolution_bitcast_fusion.2) | data formatting | bytes 8388608 | tf_op jit(solution)/shard_map/transpose | solution.py:105
  726.1 12.7 %reshape_reshape_reshape.6 = f32[4,128,8,2,128]{4,3,2,1,0:T(2,128)} reshape(f32[4,4,32,64,32]{4,3,2,1,0:T(8,128)} %copy.251) | data formatting | bytes 8388608 | tf_op jit(solution)/shard_map/reshape;reshape;reshape | solution.py:116
  738.8 9.4 %broadcast_select_fusion = (f32[4,128,8,1,128]{4,3,2,1,0:T(1,128)}, f32[4,128,8,1,128]{4,3,2,1,0:T(1,128)}, f32[4,128,8,1,128]{4,3,2,1,0:T(1,128)}) fusion(pred[]{:T(512)S(6)} %eq.337, f32[4,128,8,2,128]{4,3,2,1,0:T(2,128)} %reshape_reshape_reshape.6), kind=kLoop, calls=%fused_computation.81 | loop fusion | flops 524288 | bytes 10485761 | tf_op jit(solution)/shard_map/jit(_where)/select_n | solution.py:122
  757.1 40.3 %collective-permute-done = f32[4,128,8,128]{3,2,1,0:T(8,128)} collective-permute-done((f32[4,128,8,128]{3,2,1,0:T(8,128)}, f32[4,128,8,128]{3,2,1,0:T(8,128)}, u32[]{:S(2)}, u32[]{:S(2)}) %collective-permute-start) | collective-permute-done | bytes 2097184 | tf_op jit(solution)/shard_map/ppermute | solution.py:19
  802.9 17.4 %collective-permute-done.8 = f32[4,128,4,128]{3,1,2,0:T(8,128)S(1)} collective-permute-done((f32[4,128,4,128]{3,1,2,0:T(8,128)S(1)}, f32[4,128,4,128]{3,1,2,0:T(8,128)S(1)}, u32[]{:S(2)}, u32[]{:S(2)}) %collective-permute-start.8) | collective-permute-done | bytes 1048608 | tf_op jit(solution)/shard_map/ppermute | solution.py:19
  821.2 19.9 %collective-permute-done.1 = f32[4,128,4,128]{3,1,2,0:T(8,128)S(1)} collective-permute-done((f32[4,128,4,128]{3,1,2,0:T(8,128)S(1)}, f32[4,128,4,128]{3,1,2,0:T(8,128)S(1)}, u32[]{:S(2)}, u32[]{:S(2)}) %collective-permute-start.1) | collective-permute-done | bytes 1048608 | tf_op jit(solution)/shard_map/ppermute | solution.py:19
  844.3 12.2 %collective-permute-done.2 = f32[4,128,2,128]{3,1,2,0:T(8,128)S(1)} collective-permute-done((f32[4,128,2,128]{3,1,2,0:T(8,128)S(1)}, f32[4,128,2,128]{3,1,2,0:T(8,128)S(1)}, u32[]{:S(2)}, u32[]{:S(2)}) %collective-permute-start.2) | collective-permute-done | bytes 524320 | tf_op jit(solution)/shard_map/ppermute | solution.py:19
  (587 shorter events, 283.6 us)
Async XLA Ops:
  0.6 22.1 %copy-start = (s32[16384]{0:T(1024)S(1)}, s32[16384]{0:T(1024)}, u32[]{:S(2)}) copy-start(s32[16384]{0:T(1024)} %param.10) | copy-start | bytes 196612
  9.5 11.2 %copy-start.6 = (s32[2,16384]{1,0:T(2,128)S(1)}, s32[2,16384]{1,0:T(2,128)}, u32[]{:S(2)}) copy-start(s32[2,16384]{1,0:T(2,128)} %param.11) | copy-start | bytes 393220
  9.5 11.3 %copy-start.3 = (s32[16384,1]{0,1:T(1,128)S(1)}, s32[16384,1]{0,1:T(1,128)}, u32[]{:S(2)}) copy-start(s32[16384,1]{0,1:T(1,128)} %param.9) | copy-start | bytes 196612
  9.5 41.6 %all-to-all-start = ((bf16[128,2,4096]{2,1,0:T(2,128)(2,1)}), bf16[128,2,4096]{2,1,0:T(2,128)(2,1)S(1)}, u32[]{:S(2)}, u32[]{:S(2)}) async-start(bf16[128,2,4096]{2,1,0:T(2,128)(2,1)} %reshape.1251), calls=%async_computation | async-start | bytes 4194304 | tf_op jit(solution)/shard_map/all_to_all | solution.py:172
  21.8 31.5 %copy-start.7 = (pred[256]{0:T(512)(128)(4,1)}, pred[256]{0:T(512)(128)(4,1)S(1)}, u32[]{:S(2)}) copy-start(pred[256]{0:T(512)(128)(4,1)S(1)} %and.294) | copy-start | bytes 772
  30.3 23.0 %copy-start.4 = (f32[2,4]{1,0:T(2,128)S(1)}, f32[2,4]{1,0:T(2,128)}, u32[]{:S(2)}) copy-start(f32[2,4]{1,0:T(2,128)} %param.8) | copy-start | bytes 100
  53.3 579.2 %copy-start.13 = (f32[256]{0:T(256)S(1)}, f32[256]{0:T(256)}, u32[]{:S(2)}) copy-start(f32[256]{0:T(256)} %convert_element_type.56) | copy-start | bytes 3076
  636.9 2.2 copy-start.8
  637.0 2.2 copy-start.9
  637.0 2.2 copy-start.11
  638.1 2.0 copy-start.10
  638.1 2.0 copy-start.12
  648.8 5.3 copy-start.5
  694.0 2.9 copy-start.2
  695.7 55.4 %collective-permute-start.7 = (f32[4,128,8,128]{3,2,1,0:T(8,128)}, f32[4,128,8,128]{3,2,1,0:T(8,128)}, u32[]{:S(2)}, u32[]{:S(2)}) collective-permute-start(f32[4,128,8,128]{3,2,1,0:T(8,128)} %get-tuple-element.133), channel_id=1, source_target_pairs={{0,8},{8,0},{16,24},{24,16},{32,40},{40,32},{48,56},{56,48},{64,72... | collective-permute-start | bytes 6291464 | tf_op jit(solution)/shard_map/ppermute | solution.py:19
  748.3 49.1 %collective-permute-start = (f32[4,128,8,128]{3,2,1,0:T(8,128)}, f32[4,128,8,128]{3,2,1,0:T(8,128)}, u32[]{:S(2)}, u32[]{:S(2)}) collective-permute-start(f32[4,128,8,128]{3,2,1,0:T(8,128)} %bitcast.47), channel_id=1, source_target_pairs={{0,8},{8,0},{16,24},{24,16},{32,40},{40,32},{48,56},{56,48},{64,72... | collective-permute-start | bytes 6291464 | tf_op jit(solution)/shard_map/ppermute | solution.py:19
  755.1 65.3 %collective-permute-start.8 = (f32[4,128,4,128]{3,1,2,0:T(8,128)S(1)}, f32[4,128,4,128]{3,1,2,0:T(8,128)S(1)}, u32[]{:S(2)}, u32[]{:S(2)}) collective-permute-start(f32[4,128,4,128]{3,1,2,0:T(8,128)S(1)} %get-tuple-element.144), channel_id=1, source_target_pairs={{0,16},{16,0},{8,24},{24,8},{32,48},{48,32},{40,56},{56,40},{64,80... | collective-permute-start | bytes 3145736 | tf_op jit(solution)/shard_map/ppermute | solution.py:19
  801.4 39.7 %collective-permute-start.1 = (f32[4,128,4,128]{3,1,2,0:T(8,128)S(1)}, f32[4,128,4,128]{3,1,2,0:T(8,128)S(1)}, u32[]{:S(2)}, u32[]{:S(2)}) collective-permute-start(f32[4,128,4,128]{3,1,2,0:T(8,128)S(1)} %select_bitcast_fusion.2), channel_id=1, source_target_pairs={{0,16},{16,0},{8,24},{24,8},{32,48},{48,32},{40,56},{56,40},{64,80... | collective-permute-start | bytes 3145736 | tf_op jit(solution)/shard_map/ppermute | solution.py:19
  821.1 20.7 %collective-permute-start.9 = (f32[4,128,2,128]{3,1,2,0:T(8,128)S(1)}, f32[4,128,2,128]{3,1,2,0:T(8,128)S(1)}, u32[]{:S(2)}, u32[]{:S(2)}) collective-permute-start(f32[4,128,2,128]{3,1,2,0:T(8,128)S(1)} %get-tuple-element.159), channel_id=1, source_target_pairs={{0,32},{32,0},{8,40},{40,8},{16,48},{48,16},{24,56},{56,24},{64,96... | collective-permute-start | bytes 1572872 | tf_op jit(solution)/shard_map/ppermute | solution.py:19
  841.5 14.9 %collective-permute-start.2 = (f32[4,128,2,128]{3,1,2,0:T(8,128)S(1)}, f32[4,128,2,128]{3,1,2,0:T(8,128)S(1)}, u32[]{:S(2)}, u32[]{:S(2)}) collective-permute-start(f32[4,128,2,128]{3,1,2,0:T(8,128)S(1)} %select_bitcast_fusion.4), channel_id=1, source_target_pairs={{0,32},{32,0},{8,40},{40,8},{16,48},{48,16},{24,56},{56,24},{64,96... | collective-permute-start | bytes 1572872 | tf_op jit(solution)/shard_map/ppermute | solution.py:19
  842.1 20.2 %collective-permute-start.10 = (f32[4,128,1,128]{3,1,0,2:T(8,128)S(1)}, f32[4,128,1,128]{3,1,0,2:T(8,128)S(1)}, u32[]{:S(2)}, u32[]{:S(2)}) collective-permute-start(f32[4,128,1,128]{3,1,0,2:T(8,128)S(1)} %get-tuple-element.170), channel_id=1, source_target_pairs={{0,64},{64,0},{8,72},{72,8},{16,80},{80,16},{24,88},{88,24},{32,96... | collective-permute-start | bytes 786440 | tf_op jit(solution)/shard_map/ppermute | solution.py:19
  856.6 8.7 collective-permute-start.3
  862.5 5.7 collective-permute-start.11
  865.5 1.4 collective-permute-start.4
  867.0 13.9 %copy-start.1 = (s32[16384]{0:T(1024)S(1)}, s32[16384]{0:T(1024)}, u32[]{:S(2)}) copy-start(s32[16384]{0:T(1024)} %param.10) | copy-start | bytes 196612
  867.0 4.8 collective-permute-start.5
  868.3 4.4 collective-permute-start.12
  872.8 5.5 collective-permute-start.13
  874.1 5.4 collective-permute-start.6
where the time goes:
time: 890 us; the launch traced here: 881 us
  matrix products  478 us (54%)
  local copies, waits for them, and re-layouts  175 us (20%)
  waiting for transfers between devices  125 us (14%)
  other arithmetic  71.8 us (8%)
  starting transfers between devices  25.9 us (3%)
    dot_general x32, matrix products, march_slices(): jnp.einsum('ab,nbp->nap', lower_part, density, precision=lax.Precision.HI...  384 us
    ppermute x14, waiting for transfers between devices, swapped(): return lax.ppermute(block, axis, route)  105 us
    dot_general x32, matrix products, render_cells(): jnp.einsum('ak,nkp->nap', matrix, facing, precision=lax.Precision.HIGHEST)  64 us
    convert_element_type x16, local copies, waits for them, and re-layouts, render_cells(): plane_weights = jnp.kron(matrix, matrix).astype(jnp.bfloat16)  35.6 us
    another operation x2, local copies, waits for them, and re-layouts, split_half(): values.reshape(dims_now[:split_dim] + (dims_now[split_dim] // 2, 2) + dim...  25.6 us
    transpose x2, local copies, waits for them, and re-layouts, partial_picture(): placed.reshape(layers, across, 4, tile_side, tile_side)  24.5 us
    all_to_all x1, waiting for transfers between devices, body(): lax.all_to_all(outbox.reshape(devices, capacity, bricks.shape[1]), ('aa',...  20.8 us
    dynamic_update_slice x16, other arithmetic, render_all(): lax.map(lambda members: render_cells(members, transfer), grouped)  20.6 us
  transfers between devices with their start and end apart: 15, of which 12 were waited for; matrix products, arithmetic and copies ran while one was open for 8% of the time, Pallas kernels for 0%

commit v1 on v0

v1 whole, which is shorter than its diff:
```python
import functools

import jax
import jax.numpy as jnp
import numpy as np
from jax import lax
from jax.experimental import pallas as pl
from jax.experimental.pallas import tpu as pltpu
from jax.sharding import Mesh
from jax.sharding import PartitionSpec as P

SIDE = 1024
EDGE = 16
CAP = 16
CHIPS = 64
LOCAL = 256
HALF = EDGE * EDGE * EDGE // 2
F32 = jnp.float32
BF16 = jnp.bfloat16
I32 = jnp.int32
LOG2E = 1.4426950408889634
KAPPA = 2.0 * 0.6931471805599453 / SIDE
PLANE = ("y", "x")
CHIP = ("y", "x", "z")


def iota(shape, axis):
    return lax.broadcasted_iota(I32, shape, axis)


def ones_where(mask):
    return jnp.where(mask, 1.0, 0.0).astype(BF16)


def nt_dot(left, right):
    return lax.dot_general(left, right, (((1,), (1,)), ((), ())), preferred_element_type=F32)


def nn_dot(left, right):
    return jnp.dot(left, right, preferred_element_type=F32)


def parts_of(values, count):
    pieces = []
    rest = values
    for _ in range(count - 1):
        piece = rest.astype(BF16)
        pieces.append(piece)
        rest = rest - piece.astype(F32)
    return pieces + [rest.astype(BF16)]


def params(mib=48, semantics=None):
    return pltpu.CompilerParams(vmem_limit_bytes=mib * 1024 * 1024, dimension_semantics=semantics)


def upsample_np():
    matrix = np.zeros((2 * EDGE, EDGE), np.float32)
    for row in range(2 * EDGE):
        centre = row // 2
        beside = min(max(centre - 1 if row % 2 == 0 else centre + 1, 0), EDGE - 1)
        matrix[row, centre] += 0.75
        matrix[row, beside] += 0.25
    return matrix


def plane_weights(parity):
    up = upsample_np()
    out = np.zeros((2, 8, 32, 8, 2, 8, 16), np.float32)
    for core in range(2):
        for yc in range(8):
            row = up[16 * core + 2 * yc + parity]
            for y in range(8):
                out[core, :, :, yc, 0, y, :] = row[8 * core + y] * up[None]
            for x in range(8):
                out[core, x, :, yc, 1, x, :] = row[8 if core == 0 else 7] * up
    return jnp.asarray(out.reshape(2, 8, 256, 256), BF16)


def split_kernel(pos_ref, bricks_ref, send_ref):
    other = 1 - pos_ref[2]
    for x in range(EDGE):
        start = pl.multiple_of(x * 256 + other * 128, 128)
        send_ref[:, x * 128 : x * 128 + 128] = bricks_ref[:, pl.ds(start, 128)]


def split_halves(pos, bricks):
    return pl.pallas_call(
        split_kernel,
        out_shape=jax.ShapeDtypeStruct((128, HALF), BF16),
        in_specs=[pl.BlockSpec(memory_space=pltpu.SMEM), pl.BlockSpec(memory_space=pltpu.VMEM)],
        out_specs=pl.BlockSpec(memory_space=pltpu.VMEM),
        compiler_params=params(),
        name="split_halves",
    )(pos, bricks)


def chip_of(cell):
    return (cell % 64) // 4 * 4 + cell // 4096


def pack_kernel(pos_ref, cell_ref, bricks_ref, other_ref, out_ref, slot_ref, full_ref):
    step = pl.program_id(0)

    @pl.when(step == 0)
    def _():
        core = pos_ref[2]
        dest = chip_of(cell_ref[...])
        across = jnp.broadcast_to(dest, (LOCAL, LOCAL))
        down = across.astype(F32).T.astype(I32)
        earlier = (down == across) & (iota((LOCAL, LOCAL), 0) < iota((LOCAL, LOCAL), 1))
        rank = jnp.sum(earlier.astype(I32), axis=0, keepdims=True) - pos_ref[3] * CAP
        slot_ref[...] = jnp.where((rank >= 0) & (rank < CAP), dest * CAP + rank, -1)
        mine = pl.multiple_of(core * 128, 128)
        theirs = pl.multiple_of(128 - core * 128, 128)
        for x in range(EDGE):
            start = pl.multiple_of(x * 256 + core * 128, 128)
            full_ref[pl.ds(mine, 128), x * 128 : x * 128 + 128] = bricks_ref[:, pl.ds(start, 128)]
        full_ref[pl.ds(theirs, 128), :] = other_ref[...]

    pick = ones_where(iota((128, LOCAL), 0) + step * 128 == slot_ref[...])
    out_ref[...] = nn_dot(pick, full_ref[...]).astype(BF16)


def pack(pos, cell_row, bricks, other):
    rows = CHIPS * CAP
    whole = lambda shape: pl.BlockSpec(shape, lambda s: (0, 0))
    return pl.pallas_call(
        pack_kernel,
        grid=(rows // 128,),
        out_shape=jax.ShapeDtypeStruct((rows, HALF), BF16),
        in_specs=[
            pl.BlockSpec(memory_space=pltpu.SMEM),
            whole((1, LOCAL)),
            whole((128, 2 * HALF)),
            whole((128, HALF)),
        ],
        out_specs=pl.BlockSpec((128, HALF), lambda s: (s, 0)),
        scratch_shapes=[pltpu.VMEM((1, LOCAL), I32), pltpu.VMEM((LOCAL, HALF), BF16)],
        compiler_params=params(semantics=("arbitrary",)),
        name="pack_outbox",
    )(pos, cell_row, bricks, other)


def index_kernel(
    pos_ref, cell_ref, key_z_ref, key_x_ref, place_ref, kz_col_ref, kz_row_ref, kx_col_ref, kx_row_ref, most_ref,
    here_ref, there_ref, slot_ref, dest_ref
):
    plane, z = pos_ref[0], pos_ref[1]
    cell = cell_ref[...]
    gx, gz, gy = cell % 64, cell // 64 % 64, cell // 4096
    dest = chip_of(cell)
    dest_ref[...] = dest
    for_me = dest == plane * 4 + z
    before = ones_where(iota((LOCAL, LOCAL), 0) < iota((LOCAL, LOCAL), 1))
    rank = nn_dot(ones_where(for_me), before).astype(I32) - pos_ref[3] * CAP
    group = iota((CHIPS, LOCAL), 0) % 8
    slot_ref[...] = jnp.where(for_me & (rank >= 0) & (rank < CAP), rank + group * CAP, -1)
    here_ref[...] = jnp.where(for_me, gz * 4 + gx % 4, -1)
    there_ref[...] = jnp.where((gy == z) & (gz // 4 == plane), gx // 4 * 16 + gz % 4 * 4 + gx % 4, -1)
    down = iota((LOCAL, LOCAL), 0)
    down_slot = iota((128, LOCAL), 0)
    down_chip = iota((CHIPS, LOCAL), 0)
    units = jnp.ones((LOCAL, 128), BF16)
    byte = iota((8, LOCAL), 0)

    def key_bytes(row):
        return jnp.where(
            byte == 0, row % 256, jnp.where(byte == 1, row // 256 % 256, jnp.where(byte == 2, row // 65536, 0))
        ).astype(F32).astype(BF16)

    key_z_sum = jnp.zeros((LOCAL, 8), F32)
    key_x_sum = jnp.zeros((LOCAL, 8), F32)
    most = jnp.zeros((CHIPS, 128), F32)
    for part in range(8):

        def source(index, carry):
            place, key_z_sum, key_x_sum, most = carry
            row = pl.ds(part * 8 + index, 1)
            here = ones_where(down == here_ref[row, :])
            there = ones_where(down == there_ref[row, :])
            place = place + nt_dot(here, ones_where(down_slot == slot_ref[row, :]))
            key_z_sum = key_z_sum + nt_dot(here, key_bytes(key_z_ref[row, :]))
            key_x_sum = key_x_sum + nt_dot(there, key_bytes(key_x_ref[row, :]))
            most = jnp.maximum(most, nn_dot(ones_where(down_chip == dest_ref[row, :]), units))
            return place, key_z_sum, key_x_sum, most

        place, key_z_sum, key_x_sum, most = lax.fori_loop(
            0, 8, source, (jnp.zeros((LOCAL, 128), F32), key_z_sum, key_x_sum, most)
        )
        place_ref[:, part * 128 : part * 128 + 128] = place.astype(BF16)
    most_ref[...] = most
    for sums, col_ref, row_ref in ((key_z_sum, kz_col_ref, kz_row_ref), (key_x_sum, kx_col_ref, kx_row_ref)):
        col = sums[:, 0:1] + 256.0 * sums[:, 1:2] + 65536.0 * sums[:, 2:3]
        wide = jnp.broadcast_to(col, (LOCAL, 128))
        col_ref[...] = wide
        row_ref[...] = wide.T[0:8]


def index_maps(pos, cell, key_z, key_x):
    vmem = pl.BlockSpec(memory_space=pltpu.VMEM)
    col = jax.ShapeDtypeStruct((LOCAL, 128), F32)
    row = jax.ShapeDtypeStruct((8, LOCAL), F32)
    return pl.pallas_call(
        index_kernel,
        out_shape=(
            jax.ShapeDtypeStruct((LOCAL, CHIPS * CAP), BF16),
            col,
            row,
            col,
            row,
            jax.ShapeDtypeStruct((CHIPS, 128), F32),
        ),
        in_specs=[pl.BlockSpec(memory_space=pltpu.SMEM), vmem, vmem, vmem],
        out_specs=(vmem,) * 6,
        scratch_shapes=[pltpu.VMEM((CHIPS, LOCAL), I32)] * 4,
        compiler_params=params(),
        cost_estimate=pl.CostEstimate(flops=10**10, bytes_accessed=10**6, transcendentals=0),
        name="index_maps",
    )(pos, cell, key_z, key_x)


def unpack_kernel(pos_ref, place_ref, recv_ref, cells_ref, edge_ref):
    step = pl.program_id(0)
    cells = nn_dot(place_ref[...], recv_ref[...]).astype(BF16)
    cells_ref[...] = cells
    width = cells.shape[1]
    row = iota((width, 256), 0)
    lane = iota((width, 256), 1)
    first = jnp.where(pos_ref[2] == 0, 112, 0)
    x = row // 128 + step * (width // 128)
    pick = ones_where((row % 128 - first == lane % 16) & (x == lane // 16))
    edge = nn_dot(cells, pick).astype(BF16)

    @pl.when(step == 0)
    def _():
        edge_ref[...] = edge

    @pl.when(step > 0)
    def _():
        edge_ref[...] += edge


def unpack(pos, place, received):
    rows = CHIPS * CAP
    width = 512
    return pl.pallas_call(
        unpack_kernel,
        grid=(HALF // width,),
        out_shape=(jax.ShapeDtypeStruct((LOCAL, HALF), BF16), jax.ShapeDtypeStruct((LOCAL, 256), BF16)),
        in_specs=[
            pl.BlockSpec(memory_space=pltpu.SMEM),
            pl.BlockSpec((LOCAL, rows), lambda s: (0, 0)),
            pl.BlockSpec((rows, width), lambda s: (0, s)),
        ],
        out_specs=(pl.BlockSpec((LOCAL, width), lambda s: (0, s)), pl.BlockSpec((LOCAL, 256), lambda s: (0, 0))),
        compiler_params=params(semantics=("arbitrary",)),
        name="unpack_inbox",
    )(pos, place, received)


def render_kernel(pos_ref, transfer_ref, cells_ref, edge_ref, weights_ref, tile_x_ref, tile_z_ref, plane_ref, state_ref):
    for x in range(EDGE):
        side = x // 8 * 128
        operand = jnp.concatenate([cells_ref[:, x * 128 : x * 128 + 128], edge_ref[:, side : side + 128]], axis=1)
        plane_ref[x] = nt_dot(weights_ref[0, x % 8], operand).reshape(32, 8, 128)
    slope = [transfer_ref[0, 0] * LOG2E] + [0.5 * transfer_ref[0, c] for c in (1, 2, 3)]
    offset = [transfer_ref[1, 0] * LOG2E] + [0.5 * transfer_ref[1, c] for c in (1, 2, 3)]
    zero = jnp.zeros((8, 128), F32)
    one = jnp.ones((8, 128), F32)
    state_ref[0] = jnp.ones((32, 8, 128), F32)
    for n in range(1, 5):
        state_ref[n] = jnp.zeros((32, 8, 128), F32)

    def classify(sample):
        grown = jnp.exp2(slope[0] * sample + offset[0])
        above = 1.0 + grown
        lost = jnp.minimum(grown, 1.0) - (jnp.minimum(above, 2.0) - 1.0)
        dense = jnp.log2(above) + LOG2E * lost
        alpha = dense * (KAPPA - dense * (KAPPA * KAPPA / 2 - dense * (KAPPA * KAPPA * KAPPA / 6)))
        return dense, alpha, [jnp.tanh(slope[c] * sample + offset[c]) for c in (1, 2, 3)]

    def advance(state, values):
        dense, alpha, colours = values
        weight = alpha * state[0]
        return (
            state[0] - weight,
            state[1] + colours[0] * weight,
            state[2] + colours[1] * weight,
            state[3] + colours[2] * weight,
            state[4] + dense,
        )

    def result(state):
        depth = KAPPA * state[4]
        half = jnp.tanh(0.5 * depth)
        total = half / (1.0 + half)
        return [total + 0.5 * state[1], total + 0.5 * state[2], total + 0.5 * state[3], depth]

    unroll = 8

    def slab(x, carry):
        left = jnp.maximum(x - 1, 0)
        right = jnp.minimum(x + 1, EDGE - 1)

        def columns(block, views):
            view_even, view_odd = views
            for step in range(unroll):
                k = block * unroll + step
                centre = 0.75 * plane_ref[x, k]
                even = classify(centre + 0.25 * plane_ref[left, k])
                odd = classify(centre + 0.25 * plane_ref[right, k])
                view_even = advance(view_even, even)
                view_odd = advance(view_odd, odd)
                state = tuple(state_ref[n, k] for n in range(5))
                state = advance(advance(state, even), odd)
                for n in range(5):
                    state_ref[n, k] = state[n]
            return view_even, view_odd

        start = (one, zero, zero, zero, zero)
        views = lax.fori_loop(0, 32 // unroll, columns, (start, start))
        for odd in range(2):
            values = result(views[odd])
            for c in range(4):
                tile_z_ref[c, 2 * x + odd] = values[c]
        return carry

    lax.fori_loop(0, EDGE, slab, 0)
    values = result([state_ref[n] for n in range(5)])
    for c in range(4):
        tile_x_ref[:, c * 256 : c * 256 + 256] = values[c].reshape(256, 128).T


def render(pos, transfer, cells, edge, weights):
    smem = pl.BlockSpec(memory_space=pltpu.SMEM)
    grid_spec = pltpu.PrefetchScalarGridSpec(
        num_scalar_prefetch=1,
        grid=(2,),
        in_specs=[
            smem,
            pl.BlockSpec((128, HALF), lambda g, pos: (g, 0)),
            pl.BlockSpec((128, 256), lambda g, pos: (g, 0)),
            pl.BlockSpec((1, 8, 256, 256), lambda g, pos: (pos[2], 0, 0, 0)),
        ],
        out_specs=(
            pl.BlockSpec((128, 1024), lambda g, pos: (g, 0)),
            pl.BlockSpec((4, 32, 8, 128), lambda g, pos: (0, 0, 0, g)),
        ),
        scratch_shapes=[pltpu.VMEM((EDGE, 32, 8, 128), F32), pltpu.VMEM((5, 32, 8, 128), F32)],
    )
    return pl.pallas_call(
        render_kernel,
        grid_spec=grid_spec,
        out_shape=(jax.ShapeDtypeStruct((LOCAL, 1024), F32), jax.ShapeDtypeStruct((4, 32, 8, LOCAL), F32)),
        compiler_params=params(semantics=("arbitrary",)),
        cost_estimate=pl.CostEstimate(flops=10**10, bytes_accessed=10**7, transcendentals=10**7),
        name="render_bricks",
    )(pos, transfer, cells, edge, weights)


def compose_z_kernel(col_ref, row_ref, first_ref, second_ref, out_ref):
    here = iota((LOCAL, LOCAL), 0)
    there = iota((LOCAL, LOCAL), 1)
    col = jnp.concatenate([col_ref[...], col_ref[...]], axis=1)
    ahead = ones_where((col < row_ref[0:1, :]) & (here % 4 == there % 4))
    group = ones_where(iota((8, LOCAL), 0) == iota((8, LOCAL), 1) % 4)
    for parity, tile_ref in enumerate((first_ref, second_ref)):
        depth = tile_ref[3].reshape(256, LOCAL)
        pieces = parts_of(depth, 3)
        through = jnp.exp(-sum(nn_dot(piece, ahead) for piece in pieces))
        for c in range(4):
            values = depth if c == 3 else tile_ref[c].reshape(256, LOCAL) * through
            out_ref[:, parity * 1024 + c * 256 : parity * 1024 + c * 256 + 256] = sum(
                nt_dot(group, piece) for piece in (pieces if c == 3 else parts_of(values, 3))
            )


def compose_z(col, row, first, second):
    return pl.pallas_call(
        compose_z_kernel,
        out_shape=jax.ShapeDtypeStruct((8, 2048), F32),
        in_specs=[pl.BlockSpec(memory_space=pltpu.VMEM)] * 4,
        out_specs=pl.BlockSpec(memory_space=pltpu.VMEM),
        compiler_params=params(),
        cost_estimate=pl.CostEstimate(flops=10**9, bytes_accessed=4 * 10**6, transcendentals=10**5),
        name="compose_z",
    )(col, row, first, second)


def compose_x_kernel(col_ref, row_ref, tile_ref, out_ref):
    here = iota((LOCAL, LOCAL), 0)
    there = iota((LOCAL, LOCAL), 1)
    col = jnp.concatenate([col_ref[...], col_ref[...]], axis=1)
    ahead = ones_where((row_ref[0:1, :] < col) & (here // 4 % 4 == there // 4 % 4))
    group = ones_where(iota((8, LOCAL), 0) == iota((8, LOCAL), 1) // 4 % 4)
    depth = tile_ref[:, 768:1024]
    pieces = parts_of(depth, 3)
    through = jnp.exp(-sum(nn_dot(ahead, piece) for piece in pieces))
    for c in range(4):
        values = depth if c == 3 else tile_ref[:, c * 256 : c * 256 + 256] * through
        out_ref[:, c * 256 : c * 256 + 256] = sum(
            nn_dot(group, piece) for piece in (pieces if c == 3 else parts_of(values, 3))
        )


def compose_x(col, row, tiles):
    return pl.pallas_call(
        compose_x_kernel,
        out_shape=jax.ShapeDtypeStruct((8, 1024), F32),
        in_specs=[pl.BlockSpec(memory_space=pltpu.VMEM)] * 3,
        out_specs=pl.BlockSpec(memory_space=pltpu.VMEM),
        compiler_params=params(),
        cost_estimate=pl.CostEstimate(flops=10**9, bytes_accessed=10**6, transcendentals=10**5),
        name="compose_x",
    )(col, row, tiles)


def to_frame(sums):
    picture = sums[:4].reshape(4, 2, 4, 32, 8).transpose(2, 4, 1, 0, 3).reshape(4, 16, 128)
    return jnp.concatenate([picture[:3], -jnp.expm1(-picture[3:])], axis=0)


def swap_cores(values):
    return lax.ppermute(values, "c", [(0, 1), (1, 0)])


def body(bricks, transfer, assignment, brick_cell, depth_rank):
    plane = lax.axis_index(PLANE)
    z = lax.axis_index("z")
    core = lax.axis_index("c")
    chip = plane * 4 + z

    def position(turn):
        return jnp.stack([plane, z, core, turn]).astype(I32)

    start = position(jnp.int32(0))
    cell = brick_cell.reshape(CHIPS, LOCAL)
    cell_row = lax.dynamic_slice_in_dim(cell, chip, 1)
    major = assignment.reshape(CHIPS, LOCAL) * 16384
    key_z = major + depth_rank[0].reshape(CHIPS, LOCAL)
    key_x = major + depth_rank[1].reshape(CHIPS, LOCAL)

    other = swap_cores(split_halves(start, bricks))

    def deliver(pos, place):
        outbox = pack(pos, cell_row, bricks, other).reshape(CHIPS, CAP, HALF)
        received = lax.all_to_all(outbox, CHIP, split_axis=0, concat_axis=0, tiled=True)
        return unpack(pos, place, received.reshape(CHIPS * CAP, HALF))

    place, kz_col, kz_row, kx_col, kx_row, most = index_maps(start, cell, key_z, key_x)
    cells, edge = deliver(start, place)
    rounds = (jnp.max(most).astype(I32) + CAP - 1) // CAP

    def next_round(carry):
        turn, cells, edge = carry
        pos = position(turn)
        more_cells, more_edge = deliver(pos, index_maps(pos, cell, key_z, key_x)[0])
        return turn + 1, cells + more_cells, edge + more_edge

    _, cells, edge = lax.while_loop(lambda carry: carry[0] < rounds, next_round, (jnp.int32(1), cells, edge))

    edge = swap_cores(edge)
    tiles_z = []
    sums_x = []
    for parity in range(2):
        tile_x, tile_z = render(start, transfer, cells, edge, plane_weights(parity))
        tiles_z.append(tile_z)
        landed = lax.all_to_all(tile_x.reshape(16, 16, 1024), PLANE, split_axis=0, concat_axis=0, tiled=True)
        sums_x.append(compose_x(kx_col, kx_row, landed.reshape(LOCAL, 1024)))
    sums_z = compose_z(kz_col, kz_row, tiles_z[0], tiles_z[1])
    return to_frame(sums_z), to_frame(jnp.concatenate(sums_x, axis=1))


def solution(mesh):
    fine = Mesh(mesh.devices.reshape(4, 4, 4, 2), ("y", "x", "z", "c"))
    in_specs = (P(("y", "x", "z", "c"), None), P(), P(), P(), P())
    out_specs = (P(None, ("z", "c"), PLANE), P(None, ("z", "c"), PLANE))
    return jax.shard_map(body, mesh=fine, in_specs=in_specs, out_specs=out_specs, check_vma=False)
```

time: 890 us -> 159 us (0.18)
  matrix products: 478 us -> 0 us
  local copies, waits for them, and re-layouts: 175 us -> 10.7 us
  waiting for transfers between devices: 125 us -> 43.1 us
  Pallas kernels: 0 us -> 72.9 us
  other arithmetic: 71.8 us -> 1.57 us
    dot_general x100 -> x0, matrix products: 478 us -> none  [the longest x32 384 us: march_slices(): jnp.einsum('ab,nbp->nap', lower_part, density, precision=lax.Precision.HI...]
    ppermute x14 -> x2, waiting for transfers between devices: 105 us -> 2.35 us  [swap_cores(): return lax.ppermute(values, 'c', [(0, 1), (1, 0)])]
    pallas_call x0 -> x9, Pallas kernels: none -> 72.9 us  [the longest x2 38.3 us: render(): pl.pallas_call(render_kernel, grid_spec=grid_spec, out_shape=(jax.ShapeDt...]
    convert_element_type x16 -> x0, local copies, waits for them, and re-layouts: 35.6 us -> none  [render_cells(): plane_weights = jnp.kron(matrix, matrix).astype(jnp.bfloat16)]
    another operation x131 -> x2, local copies, waits for them, and re-layouts: 33.9 us -> 0.04 us  [the longest x1 0.02 us: body(): key_z = major + depth_rank[0].reshape(CHIPS, LOCAL)]
    transpose x2 -> x0, local copies, waits for them, and re-layouts: 24.5 us -> none  [partial_picture(): placed.reshape(layers, across, 4, tile_side, tile_side)]
    dynamic_update_slice x16 -> x0, other arithmetic: 20.6 us -> none  [render_all(): lax.map(lambda members: render_cells(members, transfer), grouped)]
    all_to_all x1 -> x3, waiting for transfers between devices: 20.8 us -> 40.8 us  [the longest x1 29.1 us: deliver(): lax.all_to_all(outbox, CHIP, split_axis=0, concat_axis=0, tiled=True)]
  transfers between devices with their start and end apart: 15 -> 5, of which waited for: 12 -> 4; matrix products, arithmetic and copies ran while one was open for 8% -> 2% of each run, Pallas kernels for 0% -> 27%
where the time goes in v1:
time: 159 us; the launch traced here: 158 us
  Pallas kernels  72.9 us (46%)
  waiting for transfers between devices  43.1 us (27%)
  starting transfers between devices  28.2 us (18%)
  local copies, waits for them, and re-layouts  10.7 us (7%)
  between operations  1.59 us (1%)
    pallas_call x2, Pallas kernels, render(): pl.pallas_call(render_kernel, grid_spec=grid_spec, out_shape=(jax.ShapeDt...  38.3 us
    all_to_all x1, waiting for transfers between devices, deliver(): lax.all_to_all(outbox, CHIP, split_axis=0, concat_axis=0, tiled=True)  29.1 us
    pallas_call x1, Pallas kernels, index_maps(): pl.pallas_call(index_kernel, out_shape=(jax.ShapeDtypeStruct((LOCAL, CHIP...  20.5 us
    all_to_all x2, starting transfers between devices, body(): lax.all_to_all(tile_x.reshape(16, 16, 1024), PLANE, split_axis=0, concat_...  16 us
    all_to_all x1, starting transfers between devices, deliver(): lax.all_to_all(outbox, CHIP, split_axis=0, concat_axis=0, tiled=True)  11.9 us
    all_to_all x2, waiting for transfers between devices, body(): lax.all_to_all(tile_x.reshape(16, 16, 1024), PLANE, split_axis=0, concat_...  11.7 us
    unnamed x26, local copies, waits for them, and re-layouts  8 us
    pallas_call x1, Pallas kernels, unpack(): pl.pallas_call(unpack_kernel, grid=(HALF // width,), out_shape=(jax.Shape...  5.34 us
  transfers between devices with their start and end apart: 5, of which 4 were waited for; matrix products, arithmetic and copies ran while one was open for 2% of the time, Pallas kernels for 27%

profile of v1, /device:TPU:0, one launch (start us, length us, event | category | flops | bytes accessed | tf_op | source)
XLA Modules:
  0.0 158.2 jit_solution(6354190772452299421)
XLA Ops:
  0.6 0.1 pad_add_fusion.1.pos_ref
  0.7 1.4 split_halves.1
  2.1 0.1 collective-permute-start
  2.2 0.9 reshape.92.cell_ref
  3.1 1.0 collective-permute-done.other_ref
  4.1 4.1 %pack_outbox.2 = bf16[1024,2048]{1,0:T(8,128)(2,1)S(1)} custom-call(s32[4]{0:T(128)S(1)} %pad_add_fusion.1.pos_ref, s32[1,256]{1,0:T(1,128)S(1)} %constant_dynamic-slice_fusion.cell_ref, bf16[128,4096]{1,0:T(8,128)(2,1)} %bricks_ref.3, bf16[128,2048]{1,0:T(8,128)(2,1)S(1)} %collective-permute-done.other_ref), custom_call_target="tpu_custom_call" | custom-call | tf_op jit(solution)/shard_map/pack_outbox/pallas_call | solution.py:128
  8.2 0.0 copy-start.1
  8.2 2.0 %copy-done.1 = bf16[1024,2048]{1,0:T(8,128)(2,1)} copy-done((bf16[1024,2048]{1,0:T(8,128)(2,1)}, bf16[1024,2048]{1,0:T(8,128)(2,1)S(1)}, u32[]{:S(2)}) %copy-start.1) | copy-done | bytes 4194328
  10.2 11.9 %all-to-all-start.1 = ((bf16[64,16,2048]{2,1,0:T(8,128)(2,1)}), bf16[64,16,2048]{2,1,0:T(8,128)(2,1)}, u32[]{:S(2)}, u32[]{:S(2)}) async-start(bf16[64,16,2048]{2,1,0:T(8,128)(2,1)} %bitcast.30), calls=%async_computation.1 | async-start | bytes 8388608 | tf_op jit(solution)/shard_map/all_to_all | solution.py:448
  22.1 0.0 copy-done.12
  22.1 0.3 slice_reduce_fusion
  22.5 0.0 copy-done.13
  22.5 0.2 multiply_reduce_fusion
  22.7 20.5 %index_maps.2 = (bf16[256,1024]{1,0:T(8,128)(2,1)S(1)}, f32[256,128]{1,0:T(8,128)S(1)}, f32[8,256]{1,0:T(8,128)S(1)}, f32[256,128]{1,0:T(8,128)S(1)}, f32[8,256]{1,0:T(8,128)S(1)}, /*index=5*/f32[64,128]{1,0:T(8,128)S(1)}) custom-call(s32[4]{0:T(128)S(1)} %pad_add_fusion.1.pos_ref, s32[64,256]{1,0:T(8,128)S(1)} %reshape.92.cell_ref, ...), custom_call_target="tpu_custom_call" | custom-call | flops 10000000000 | bytes 1000000 | tf_op jit(solution)/shard_map/index_maps/pallas_call | solution.py:204
  43.3 0.6 reduce_max.9
  44.6 29.1 %all-to-all-done.1 = bf16[64,16,2048]{2,1,0:T(8,128)(2,1)} async-done(((bf16[64,16,2048]{2,1,0:T(8,128)(2,1)}), bf16[64,16,2048]{2,1,0:T(8,128)(2,1)}, u32[]{:S(2)}, u32[]{:S(2)}) %all-to-all-start.1) | async-done | bytes 4194336 | tf_op jit(solution)/shard_map/all_to_all | solution.py:448
  73.6 5.3 %unpack_inbox.2 = (bf16[256,2048]{1,0:T(8,128)(2,1)}, bf16[256,256]{1,0:T(8,128)(2,1)S(1)}) custom-call(s32[4]{0:T(128)S(1)} %pad_add_fusion.1.pos_ref, bf16[256,1024]{1,0:T(8,128)(2,1)S(1)} %get-tuple-element.88.place_ref, bf16[1024,2048]{1,0:T(8,128)(2,1)} %bitcast.10.recv_ref), custom_call_target="tpu_custom_call" | custom-call | tf_op jit(solution)/shard_map/unpack_inbox/pallas_call | solution.py:247
  79.0 0.0 copy-done.11
  79.0 0.0 copy-done.9
  79.0 0.3 collective-permute-start.1
  79.3 1.3 collective-permute-done.1.edge_ref
  80.6 0.0 copy-done.2
  80.6 1.6 %copy-done.4 = bf16[2,8,256,256]{3,2,1,0:T(8,128)(2,1)S(1)} copy-done((bf16[2,8,256,256]{3,2,1,0:T(8,128)(2,1)S(1)}, bf16[2,8,256,256]{3,2,1,0:T(8,128)(2,1)}, u32[]{:S(2)}) %copy-start.4) | copy-done | bytes 2097176
  82.2 19.2 %render_bricks.3 = (f32[256,1024]{1,0:T(8,128)}, f32[4,32,8,256]{3,2,1,0:T(8,128)S(1)}) custom-call(s32[4]{0:T(128)S(1)} %pad_add_fusion.1.pos_ref, f32[2,4]{1,0:T(2,128)S(1)} %copy-done.2, bf16[256,2048]{1,0:T(8,128)(2,1)} %get-tuple-element.92.cells_ref, bf16[256,256]{1,0:T(8,128)(2,1)S(1)} %collective-permute-done.1.edge_ref, ...), custom_call_target="tpu_custom_call" | custom-call | flops 10000000000 | bytes 10000000 | tf_op jit(solution)/shard_map/render_bricks/pallas_call | solution.py:352
  101.4 1.0 copy-done.5
  102.4 8.7 %all-to-all-start.3 = ((f32[16,16,1024]{2,1,0:T(8,128)}), f32[16,16,1024]{2,1,0:T(8,128)S(1)}, u32[]{:S(2)}, u32[]{:S(2)}) async-start(f32[16,16,1024]{2,1,0:T(8,128)} %bitcast.14), calls=%async_computation.3 | async-start | bytes 2097152 | tf_op jit(solution)/shard_map/all_to_all | solution.py:469
  111.1 0.0 copy-done.3
  111.1 19.1 %render_bricks.2 = (f32[256,1024]{1,0:T(8,128)}, f32[4,32,8,256]{3,2,1,0:T(8,128)S(1)}) custom-call(s32[4]{0:T(128)S(1)} %pad_add_fusion.1.pos_ref, f32[2,4]{1,0:T(2,128)S(1)} %copy-done.2, bf16[256,2048]{1,0:T(8,128)(2,1)} %get-tuple-element.92.cells_ref, bf16[256,256]{1,0:T(8,128)(2,1)S(1)} %collective-permute-done.1.edge_ref, ...), custom_call_target="tpu_custom_call" | custom-call | flops 10000000000 | bytes 10000000 | tf_op jit(solution)/shard_map/render_bricks/pallas_call | solution.py:352
  130.2 1.0 copy-done.7
  131.2 0.0 all-to-all-done.3
  131.2 7.3 %all-to-all-start.2 = ((f32[16,16,1024]{2,1,0:T(8,128)}), f32[16,16,1024]{2,1,0:T(8,128)S(1)}, u32[]{:S(2)}, u32[]{:S(2)}) async-start(f32[16,16,1024]{2,1,0:T(8,128)} %bitcast.12), calls=%async_computation.2 | async-start | bytes 2097152 | tf_op jit(solution)/shard_map/all_to_all | solution.py:469
  138.5 0.0 copy-start.6
  138.6 1.2 copy-done.6
  139.8 1.2 copy-done.8
  141.0 1.6 %compose_z.1 = f32[8,2048]{1,0:T(8,128)S(1)} custom-call(f32[256,128]{1,0:T(8,128)S(1)} %get-tuple-element.86.col_ref, f32[8,256]{1,0:T(8,128)S(1)} %get-tuple-element.87.row_ref, f32[4,32,8,256]{3,2,1,0:T(8,128)S(1)} %copy-done.8, f32[4,32,8,256]{3,2,1,0:T(8,128)S(1)} %copy-done.6), custom_call_target="tpu_custom_call" | custom-call | flops 1000000000 | bytes 4000000 | tf_op jit(solution)/shard_map/compose_z/pallas_call | solution.py:380
  142.6 0.3 reshape.95
  142.9 0.2 copy.17
  143.2 0.1 slice.36
  143.3 0.1 neg.54
  143.4 0.0 copy-done.10
  143.4 0.8 compose_x.3
  144.2 11.7 %all-to-all-done.2 = f32[16,16,1024]{2,1,0:T(8,128)S(1)} async-done(((f32[16,16,1024]{2,1,0:T(8,128)}), f32[16,16,1024]{2,1,0:T(8,128)S(1)}, u32[]{:S(2)}, u32[]{:S(2)}) %all-to-all-start.2) | async-done | bytes 1048608 | tf_op jit(solution)/shard_map/all_to_all | solution.py:469
  155.9 0.8 compose_x.2
  156.7 0.3 reshape.100
  157.1 0.2 copy.20
  157.3 0.1 slice.40
  157.5 0.1 neg.57
  157.5 0.6 pad_maximum_fusion.1
  (27 shorter events, 0.3 us)
Async XLA Ops:
  2.1 2.0 %collective-permute-start = (bf16[128,2048]{1,0:T(8,128)(2,1)S(1)}, bf16[128,2048]{1,0:T(8,128)(2,1)S(1)}, u32[]{:S(2)}, u32[]{:S(2)}) collective-permute-start(bf16[128,2048]{1,0:T(8,128)(2,1)S(1)} %split_halves.1), channel_id=1, source_target_pairs={{0,1},{1,0},{2,3},{3,2},{4,5},{5,4},{6,7},{7,6},{8,9},{9,8},{10,11... | collective-permute-start | bytes 1572872 | tf_op jit(solution)/shard_map/ppermute | solution.py:425
  8.2 2.0 %copy-start.1 = (bf16[1024,2048]{1,0:T(8,128)(2,1)}, bf16[1024,2048]{1,0:T(8,128)(2,1)S(1)}, u32[]{:S(2)}) copy-start(bf16[1024,2048]{1,0:T(8,128)(2,1)S(1)} %pack_outbox.2) | copy-start | bytes 12582916
  10.2 11.9 %copy-start.12 = (s32[2,16384]{1,0:T(2,128)S(1)}, s32[2,16384]{1,0:T(2,128)}, u32[]{:S(2)}) copy-start(s32[2,16384]{1,0:T(2,128)} %param.13) | copy-start | bytes 393220
  10.2 12.3 %copy-start.13 = (s32[16384,1]{0,1:T(1,128)S(1)}, s32[16384,1]{0,1:T(1,128)}, u32[]{:S(2)}) copy-start(s32[16384,1]{0,1:T(1,128)} %param.11) | copy-start | bytes 196612
  10.2 63.4 %all-to-all-start.1 = ((bf16[64,16,2048]{2,1,0:T(8,128)(2,1)}), bf16[64,16,2048]{2,1,0:T(8,128)(2,1)}, u32[]{:S(2)}, u32[]{:S(2)}) async-start(bf16[64,16,2048]{2,1,0:T(8,128)(2,1)} %bitcast.30), calls=%async_computation.1 | async-start | bytes 8388608 | tf_op jit(solution)/shard_map/all_to_all | solution.py:448
  43.3 35.7 %copy-start.9 = (f32[8,256]{1,0:T(8,128)}, f32[8,256]{1,0:T(8,128)S(1)}, u32[]{:S(2)}) copy-start(f32[8,256]{1,0:T(8,128)S(1)} %get-tuple-element.97.row_ref) | copy-start | bytes 24580
  43.3 35.7 %copy-start.11 = (bf16[128,4096]{1,0:T(8,128)(2,1)S(1)}, bf16[128,4096]{1,0:T(8,128)(2,1)}, u32[]{:S(2)}) copy-start(bf16[128,4096]{1,0:T(8,128)(2,1)} %bricks_ref.3) | copy-start | bytes 3145732
  79.0 1.6 %copy-start.2 = (f32[2,4]{1,0:T(2,128)S(1)}, f32[2,4]{1,0:T(2,128)}, u32[]{:S(2)}) copy-start(f32[2,4]{1,0:T(2,128)} %transfer_ref.3) | copy-start | bytes 100
  79.0 1.6 %collective-permute-start.1 = (bf16[256,256]{1,0:T(8,128)(2,1)S(1)}, bf16[256,256]{1,0:T(8,128)(2,1)S(1)}, u32[]{:S(2)}, u32[]{:S(2)}) collective-permute-start(bf16[256,256]{1,0:T(8,128)(2,1)S(1)} %get-tuple-element.93), channel_id=1, source_target_pairs={{0,1},{1,0},{2,3},{3,2},{4,5},{5,4},{6,7},{7,6},{8,9},{9,8},{10,11... | collective-permute-start | bytes 393224 | tf_op jit(solution)/shard_map/ppermute | solution.py:425
  80.6 1.6 %copy-start.4 = (bf16[2,8,256,256]{3,2,1,0:T(8,128)(2,1)S(1)}, bf16[2,8,256,256]{3,2,1,0:T(8,128)(2,1)}, u32[]{:S(2)}) copy-start(bf16[2,8,256,256]{3,2,1,0:T(8,128)(2,1)} %constant.51.clone.weights_ref) | copy-start | bytes 6291460
  82.2 28.9 %copy-start.3 = (bf16[2,8,256,256]{3,2,1,0:T(8,128)(2,1)S(1)}, bf16[2,8,256,256]{3,2,1,0:T(8,128)(2,1)}, u32[]{:S(2)}) copy-start(bf16[2,8,256,256]{3,2,1,0:T(8,128)(2,1)} %constant.50.clone.weights_ref) | copy-start | bytes 6291460
  101.4 1.0 copy-start.5
  102.4 28.8 %all-to-all-start.3 = ((f32[16,16,1024]{2,1,0:T(8,128)}), f32[16,16,1024]{2,1,0:T(8,128)S(1)}, u32[]{:S(2)}, u32[]{:S(2)}) async-start(f32[16,16,1024]{2,1,0:T(8,128)} %bitcast.14), calls=%async_computation.3 | async-start | bytes 2097152 | tf_op jit(solution)/shard_map/all_to_all | solution.py:469
  130.2 1.0 copy-start.7
  131.2 12.2 %copy-start.10 = (f32[8,256]{1,0:T(8,128)S(1)}, f32[8,256]{1,0:T(8,128)}, u32[]{:S(2)}) copy-start(f32[8,256]{1,0:T(8,128)} %copy-done.9) | copy-start | bytes 24580
  131.2 24.7 %all-to-all-start.2 = ((f32[16,16,1024]{2,1,0:T(8,128)}), f32[16,16,1024]{2,1,0:T(8,128)S(1)}, u32[]{:S(2)}, u32[]{:S(2)}) async-start(f32[16,16,1024]{2,1,0:T(8,128)} %bitcast.12), calls=%async_computation.2 | async-start | bytes 2097152 | tf_op jit(solution)/shard_map/all_to_all | solution.py:469
  138.5 1.2 copy-start.6
  139.8 1.2 copy-start.8

commit v2 on v1

v2 whole, which is shorter than its diff:
```python
import functools

import jax
import jax.numpy as jnp
import numpy as np
from jax import lax
from jax.experimental import pallas as pl
from jax.experimental.pallas import tpu as pltpu
from jax.sharding import Mesh
from jax.sharding import PartitionSpec as P

SIDE = 1024
EDGE = 16
CAP = 8
TRIES = 5
GROUP = 8
CLASSES = 4
BACK = 8
CHIPS = 64
LOCAL = 256
HALF = EDGE * EDGE * EDGE // 2
F32 = jnp.float32
BF16 = jnp.bfloat16
I32 = jnp.int32
LOG2E = 1.4426950408889634
KAPPA = 2.0 * 0.6931471805599453 / SIDE
PLANE = ("y", "x1", "x0")
CHIP = ("y", "x1", "x0", "z")
NEAR = ("x0", "z")


TOP = 32767.0
LOG_MID = -9.88
LOG_REACH = 9.3


def iota(shape, axis):
    return lax.broadcasted_iota(I32, shape, axis)


def ones_where(mask):
    return jnp.where(mask, 1.0, 0.0).astype(BF16)


def nt_dot(left, right):
    return lax.dot_general(left, right, (((1,), (1,)), ((), ())), preferred_element_type=F32)


def nn_dot(left, right):
    return jnp.dot(left, right, preferred_element_type=F32)


def opacity(depth):
    half = jnp.tanh(0.5 * depth)
    return 2.0 * half / (1.0 + half)


def parts_of(values, count):
    pieces = []
    rest = values
    for _ in range(count - 1):
        piece = rest.astype(BF16)
        pieces.append(piece)
        rest = rest - piece.astype(F32)
    return pieces + [rest.astype(BF16)]


def in_hbm(array):
    return pltpu.with_memory_space_constraint(array, pltpu.HBM)


def params(mib=24, semantics=None):
    return pltpu.CompilerParams(vmem_limit_bytes=mib * 1024 * 1024, dimension_semantics=semantics)


def upsample_np():
    matrix = np.zeros((2 * EDGE, EDGE), np.float32)
    for row in range(2 * EDGE):
        centre = row // 2
        beside = min(max(centre - 1 if row % 2 == 0 else centre + 1, 0), EDGE - 1)
        matrix[row, centre] += 0.75
        matrix[row, beside] += 0.25
    return matrix


def plane_weights(batch):
    up = upsample_np()
    out = np.zeros((2, 32, 8, 1 + batch, 8, 16), np.float32)
    for core in range(2):
        for sub in range(8):
            centre = 4 * batch + sub // 2
            beside = max(centre - 1, 0) if sub % 2 == 0 else centre + 1
            for m, share in ((centre, 0.75), (beside, 0.25)):
                half, y = m // 8, m % 8
                out[core, :, sub, half, y if core == 0 else 7 - y] += 0.25 * share * up
    return jnp.asarray(out.reshape(2, 256, 128 * (1 + batch)), BF16)


def split_kernel(pos_ref, bricks_ref, send_ref):
    other = 1 - pos_ref[2]
    for x in range(EDGE):
        start = pl.multiple_of(x * 256 + other * 128, 128)
        send_ref[:, x * 128 : x * 128 + 128] = bricks_ref[:, pl.ds(start, 128)]


def split_halves(pos, bricks):
    return pl.pallas_call(
        split_kernel,
        out_shape=jax.ShapeDtypeStruct((128, HALF), BF16),
        in_specs=[pl.BlockSpec(memory_space=pltpu.SMEM), pl.BlockSpec(memory_space=pltpu.VMEM)],
        out_specs=pl.BlockSpec(memory_space=pltpu.VMEM),
        compiler_params=params(),
        name="split_halves",
    )(pos, bricks)


def chip_of(cell):
    return (cell % 64) // 4 * 4 + cell // 4096


def up(values, shift):
    inside = iota(values.shape, 1) % GROUP + shift < GROUP
    return jnp.where(inside, pltpu.roll(values, 128 - shift, axis=1), pltpu.roll(values, GROUP - shift, axis=1))


def shift_of(turn, kind):
    return 1 + (turn + 2 * kind) % (GROUP - 1)


def by_class(values, kinds, turn, back):
    out = None
    for kind in range(CLASSES):
        shift = shift_of(turn, kind)
        moved = up(values, GROUP - shift if back else shift)
        out = moved if out is None else jnp.where(kinds == kind, moved, out)
    return out


def relay_plan(counts, kinds):
    over = jnp.maximum(counts - CAP, 0.0)
    taken = jnp.minimum(counts, CAP)
    begin = jnp.zeros_like(over)
    amounts, starts, bases = [], [begin], []
    for turn in range(TRIES):
        amount = jnp.minimum(over, CAP - by_class(taken, kinds, turn, False))
        bases.append(taken)
        taken = taken + by_class(amount, kinds, turn, True)
        over = over - amount
        begin = begin + amount
        amounts.append(amount)
        starts.append(begin)
    return amounts, starts, bases, over


def pack_kernel(
    pos_ref, cell_ref, bricks_ref, other_ref, out_ref, full_ref, box_ref, sems
):
    core = pos_ref[2]
    turn = pos_ref[3]
    kind = (pos_ref[0] * 4 + pos_ref[1]) % CLASSES
    dest = chip_of(cell_ref[...])
    across = jnp.broadcast_to(dest, (LOCAL, LOCAL))
    down = across.astype(F32).T.astype(I32)
    earlier = (down == across) & (iota((LOCAL, LOCAL), 0) < iota((LOCAL, LOCAL), 1))
    rank = jnp.sum(earlier.astype(I32), axis=0, keepdims=True)
    later = rank - turn * CAP
    in_turn = jnp.where((later >= 0) & (later < CAP), dest * CAP + later, -1)
    chips = iota((128, LOCAL), 0)
    counts = nt_dot(jnp.ones((8, LOCAL), BF16), ones_where(chips % CHIPS == dest))
    kinds = jnp.full((8, 128), kind, I32)
    _, starts, bases, _ = relay_plan(counts, kinds)
    rows = starts[1:] + [by_class(base, kinds, n, False) for n, base in enumerate(bases)]
    table = jnp.concatenate([row[0:1] for row in rows] + [jnp.zeros((16 - len(rows), 128), F32)], axis=0)
    found = nn_dot(table.astype(BF16), ones_where(chips == dest)).astype(I32)
    relayed = jnp.where(rank < CAP, dest * CAP + rank, -1)
    over = rank - CAP
    for n in range(TRIES):
        begin = found[n - 1 : n] if n else jnp.zeros_like(over)
        inside = (over >= begin) & (over < found[n : n + 1])
        relay = dest // GROUP * GROUP + (dest + shift_of(n, kind)) % GROUP
        relayed = jnp.where(inside, relay * CAP + found[TRIES + n : TRIES + n + 1] + over - begin, relayed)
    slot = jnp.where(turn < 0, relayed, in_turn)
    mine = pl.multiple_of(core * 128, 128)
    theirs = pl.multiple_of(128 - core * 128, 128)
    for x in range(EDGE):
        start = pl.multiple_of(x * 256 + core * 128, 128)
        full_ref[pl.ds(mine, 128), x * 128 : x * 128 + 128] = bricks_ref[:, pl.ds(start, 128)]
    full_ref[pl.ds(theirs, 128), :] = other_ref[...]
    copies = []
    for block in range(CHIPS * CAP // 128):
        pick = ones_where(iota((128, LOCAL), 0) + block * 128 == slot)
        rows = pl.ds(block * 128, 128)
        box_ref[rows, :] = nn_dot(pick, full_ref[...]).astype(BF16)
        copy = pltpu.make_async_copy(box_ref.at[rows, :], out_ref.at[rows, :], sems.at[block])
        copy.start()
        copies.append(copy)
    for copy in copies:
        copy.wait()


def pack(pos, cell_row, bricks, other):
    rows = CHIPS * CAP
    grid_spec = pltpu.PrefetchScalarGridSpec(
        num_scalar_prefetch=1,
        grid=(1,),
        in_specs=[
            pl.BlockSpec((1, LOCAL), lambda s, pos: (0, 0)),
            pl.BlockSpec((128, 2 * HALF), lambda s, pos: (0, 0)),
            pl.BlockSpec((128, HALF), lambda s, pos: (0, 0)),
        ],
        out_specs=pl.BlockSpec(memory_space=pltpu.HBM),
        scratch_shapes=[
            pltpu.VMEM((LOCAL, HALF), BF16),
            pltpu.VMEM((rows, HALF), BF16),
            pltpu.SemaphoreType.DMA((rows // 128,)),
        ],
    )
    return pl.pallas_call(
        pack_kernel,
        grid_spec=grid_spec,
        out_shape=pltpu.HBM((rows, HALF), BF16),
        compiler_params=params(),
        name="pack_outbox",
    )(pos, cell_row, bricks, other)


def index_kernel(
    pos_ref, cell_ref, place_ref, relay_place_ref, forward_ref, most_ref,
    here_ref, slot_ref, relay_ref, dest_ref, count_ref, side_ref
):
    plane, z, turn = pos_ref[0], pos_ref[1], pos_ref[3]
    me = plane * 4 + z
    mine = me % GROUP
    first = me - mine
    cell = cell_ref[...]
    gx, gz = cell % 64, cell // 64 % 64
    dest = chip_of(cell)
    dest_ref[...] = dest
    down_128 = iota((128, LOCAL), 0)
    down_chip = down_128 % CHIPS
    units = jnp.ones((8, LOCAL), BF16)

    def count(index, carry):
        row = pl.ds(index, 1)
        count_ref[row, :] = nt_dot(units, ones_where(down_chip == dest_ref[row, :]))[0:1]
        return carry

    lax.fori_loop(0, CHIPS, count, 0, unroll=8)
    counts = count_ref[...]
    most_ref[0] = jnp.max(counts).astype(I32)
    kinds = iota((CHIPS, 128), 0) % CLASSES
    amounts, starts, bases, left = relay_plan(counts, kinds)
    sources = ones_where(iota((CHIPS, CHIPS), 1) < iota((CHIPS, CHIPS), 0))
    lane = iota((CHIPS, 128), 1)

    def column(values, chip):
        return jnp.sum(jnp.where(lane == chip, values, 0.0), axis=1, keepdims=True)

    for_me = dest == me
    before = ones_where(iota((LOCAL, LOCAL), 0) < iota((LOCAL, LOCAL), 1))
    rank = nn_dot(ones_where(for_me), before).astype(I32)
    over = rank - CAP
    slots = CHIPS * CAP
    spread = jnp.where(iota((CHIPS, slots), 1) // CAP == iota((CHIPS, slots), 0), 1.0, 0.0)
    along = lambda col: jnp.sum(col * spread, axis=0, keepdims=True).astype(I32)
    slot_lane = iota((1, slots), 1) % CAP
    relay = jnp.full((CHIPS, LOCAL), -1, I32)
    handed = jnp.full((1, slots), -1, I32)
    for shift in range(1, GROUP):
        amount = jnp.zeros((CHIPS, 128), F32)
        begin = amount
        base = amount
        for kind in range(CLASSES):
            for n in range(TRIES):
                if shift_of(n, kind) == shift:
                    amount = jnp.where(kinds == kind, amounts[n], amount)
                    begin = jnp.where(kinds == kind, starts[n], begin)
                    base = jnp.where(kinds == kind, bases[n], base)
        prefix = nn_dot(sources, amount.astype(BF16))
        left = left + jnp.maximum(jnp.sum(amount, axis=0, keepdims=True) - BACK, 0.0)
        order = over - column(begin, me).astype(I32)
        at = (mine + shift) % GROUP * BACK + column(prefix, me).astype(I32) + order
        relay = jnp.where((order >= 0) & (order < column(amount, me).astype(I32)), at, relay)
        near = (mine + GROUP - shift) % GROUP
        order = slot_lane - along(column(base, me))
        at = near * BACK + order + along(column(prefix, first + near))
        handed = jnp.where((order >= 0) & (order < along(column(amount, first + near))), at, handed)
    forward_ref[...] = ones_where(iota((GROUP * BACK, slots), 0) == handed)
    most_ref[1] = jnp.max(left).astype(I32)
    relay_ref[...] = jnp.where(for_me & (turn < 0), relay, -1)
    group = iota((CHIPS, LOCAL), 0) % (128 // CAP)
    later = rank - jnp.maximum(turn, 0) * CAP
    slot_ref[...] = jnp.where(for_me & (later >= 0) & (later < CAP), later + group * CAP, -1)
    here_ref[...] = jnp.where(for_me, gz * 4 + gx % 4, -1)
    down_256 = iota((LOCAL, LOCAL), 0)
    side_ref[...] = jnp.zeros((LOCAL, 128), F32)
    for part in range(slots // 128):

        def source(index, place):
            row = pl.ds(part * (128 // CAP) + index, 1)
            here = ones_where(down_256 == here_ref[row, :])
            wanted = jnp.concatenate(
                [ones_where(down_128 == slot_ref[row, :]), ones_where(down_128 == relay_ref[row, :])], axis=0
            )
            both = nt_dot(here, wanted)
            side_ref[...] += both[:, 128:]
            return place + both[:, :128]

        place = lax.fori_loop(0, 128 // CAP, source, jnp.zeros((LOCAL, 128), F32), unroll=4)
        place_ref[:, part * 128 : part * 128 + 128] = place.astype(BF16)
    relay_place_ref[...] = side_ref[...].astype(BF16)


def index_maps(pos, cell):
    vmem = pl.BlockSpec(memory_space=pltpu.VMEM)
    return pl.pallas_call(
        index_kernel,
        out_shape=(
            pltpu.HBM((LOCAL, CHIPS * CAP), BF16),
            pltpu.HBM((LOCAL, 128), BF16),
            jax.ShapeDtypeStruct((GROUP * BACK, CHIPS * CAP), BF16),
            jax.ShapeDtypeStruct((2,), I32),
        ),
        in_specs=[pl.BlockSpec(memory_space=pltpu.SMEM), vmem],
        grid=(1,),
        out_specs=(
            pl.BlockSpec((LOCAL, CHIPS * CAP), lambda s: (0, 0)),
            pl.BlockSpec((LOCAL, 128), lambda s: (0, 0)),
            pl.BlockSpec((GROUP * BACK, CHIPS * CAP), lambda s: (0, 0)),
            pl.BlockSpec(memory_space=pltpu.SMEM),
        ),
        scratch_shapes=[pltpu.VMEM((CHIPS, LOCAL), I32)] * 4
        + [pltpu.VMEM((CHIPS, 128), F32), pltpu.VMEM((LOCAL, 128), F32)],
        compiler_params=params(),
        cost_estimate=pl.CostEstimate(flops=10**10, bytes_accessed=10**6, transcendentals=0),
        name="index_maps",
    )(pos, cell)


def key_kernel(pos_ref, cell_ref, key_z_ref, key_x_ref, kz_col_ref, kz_row_ref, kx_col_ref, kx_row_ref, here_ref, there_ref):
    plane, z = pos_ref[0], pos_ref[1]
    cell = cell_ref[...]
    gx, gz, gy = cell % 64, cell // 64 % 64, cell // 4096
    here_ref[...] = jnp.where((gy == z) & (gx // 4 == plane), gz * 4 + gx % 4, -1)
    there_ref[...] = jnp.where((gy == z) & (gz // 4 == plane), gx // 4 * 16 + gz % 4 * 4 + gx % 4, -1)
    down = iota((LOCAL, LOCAL), 0)
    byte = iota((8, LOCAL), 0)

    def key_bytes(row):
        return jnp.where(
            byte == 0, row % 256, jnp.where(byte == 1, row // 256 % 256, jnp.where(byte == 2, row // 65536, 0))
        ).astype(F32).astype(BF16)

    def source(index, sums):
        row = pl.ds(index, 1)
        return (
            sums[0] + nt_dot(ones_where(down == here_ref[row, :]), key_bytes(key_z_ref[row, :])),
            sums[1] + nt_dot(ones_where(down == there_ref[row, :]), key_bytes(key_x_ref[row, :])),
        )

    nothing = jnp.zeros((LOCAL, 8), F32)
    sums = lax.fori_loop(0, CHIPS, source, (nothing, nothing), unroll=4)
    for part, col_ref, row_ref in ((sums[0], kz_col_ref, kz_row_ref), (sums[1], kx_col_ref, kx_row_ref)):
        col = part[:, 0:1] + 256.0 * part[:, 1:2] + 65536.0 * part[:, 2:3]
        wide = jnp.broadcast_to(col, (LOCAL, 128))
        col_ref[...] = wide
        row_ref[...] = wide.T[0:8]


def order_keys(pos, cell, key_z, key_x):
    vmem = pl.BlockSpec(memory_space=pltpu.VMEM)
    col = jax.ShapeDtypeStruct((LOCAL, 128), F32)
    row = jax.ShapeDtypeStruct((8, LOCAL), F32)
    return pl.pallas_call(
        key_kernel,
        out_shape=(col, row, col, row),
        in_specs=[pl.BlockSpec(memory_space=pltpu.SMEM), vmem, vmem, vmem],
        out_specs=(vmem,) * 4,
        scratch_shapes=[pltpu.VMEM((CHIPS, LOCAL), I32)] * 2,
        compiler_params=params(),
        cost_estimate=pl.CostEstimate(flops=10**10, bytes_accessed=10**6, transcendentals=0),
        name="order_keys",
    )(pos, cell, key_z, key_x)


def forward_kernel(forward_ref, recv_ref, out_ref):
    out_ref[...] = nn_dot(forward_ref[...], recv_ref[...]).astype(BF16)


def forward(maps, received):
    vmem = pl.BlockSpec(memory_space=pltpu.VMEM)
    handed = pl.pallas_call(
        forward_kernel,
        out_shape=jax.ShapeDtypeStruct((GROUP * BACK, HALF), BF16),
        in_specs=[vmem, vmem],
        out_specs=vmem,
        compiler_params=params(),
        cost_estimate=pl.CostEstimate(flops=10**8, bytes_accessed=10**6, transcendentals=0),
        name="hand_on",
    )(maps, received)
    sent = lax.all_to_all(handed.reshape(GROUP, BACK, HALF), NEAR, split_axis=0, concat_axis=0, tiled=True)
    return sent.reshape(GROUP * BACK, HALF)


def unpack_kernel(place_ref, relay_ref, recv_ref, back_ref, cells_ref):
    cells = nn_dot(place_ref[...], recv_ref[...]) + nn_dot(relay_ref[:, : GROUP * BACK], back_ref[...])
    cells_ref[...] = cells.astype(BF16)


def unpack(place, relay_place, received, back):
    rows, lanes = received.shape
    width = 512
    return pl.pallas_call(
        unpack_kernel,
        grid=(lanes // width,),
        out_shape=pltpu.HBM((LOCAL, lanes), BF16),
        in_specs=[
            pl.BlockSpec((LOCAL, rows), lambda s: (0, 0)),
            pl.BlockSpec((LOCAL, 128), lambda s: (0, 0)),
            pl.BlockSpec((rows, width), lambda s: (0, s)),
            pl.BlockSpec((GROUP * BACK, width), lambda s: (0, s)),
        ],
        out_specs=pl.BlockSpec((LOCAL, width), lambda s: (0, s)),
        compiler_params=params(semantics=("arbitrary",)),
        cost_estimate=pl.CostEstimate(flops=10**9, bytes_accessed=3 * 10**6, transcendentals=0),
        name="unpack_inbox",
    )(in_hbm(place), in_hbm(relay_place), received, back)


def render_kernel(batch, pos_ref, transfer_ref, *refs):
    halves, (weights_ref, tile_x_ref, tile_z_ref, plane_ref, state_ref) = refs[: 1 + batch], refs[1 + batch :]
    weights = weights_ref[pos_ref[2]]
    for x in range(EDGE):
        operand = jnp.concatenate([ref[:, x * 128 : x * 128 + 128] for ref in halves], axis=1)
        plane_ref[x] = nt_dot(weights, operand).reshape(32, 8, 128)
    slope = [transfer_ref[0, 0] * LOG2E] + [0.5 * transfer_ref[0, c] for c in (1, 2, 3)]
    offset = [transfer_ref[1, 0] * LOG2E] + [0.5 * transfer_ref[1, c] for c in (1, 2, 3)]
    zero = jnp.zeros((8, 128), F32)
    one = jnp.ones((8, 128), F32)
    state_ref[0] = jnp.ones((32, 8, 128), F32)
    for n in range(1, 5):
        state_ref[n] = jnp.zeros((32, 8, 128), F32)

    def classify(sample):
        grown = jnp.exp2(slope[0] * sample + offset[0])
        above = 1.0 + grown
        dense = jnp.log2(above) * (grown * pl.reciprocal(above - 1.0, approx=True))
        alpha = dense * (KAPPA - dense * (KAPPA * KAPPA / 2 - dense * (KAPPA * KAPPA * KAPPA / 6)))
        return dense, alpha, [jnp.tanh(slope[c] * sample + offset[c]) for c in (1, 2, 3)]

    def advance(state, values):
        dense, alpha, colours = values
        weight = alpha * state[0]
        return (
            state[0] - weight,
            state[1] + colours[0] * weight,
            state[2] + colours[1] * weight,
            state[3] + colours[2] * weight,
            state[4] + dense,
        )

    def result(state):
        depth = KAPPA * state[4]
        half = 0.5 * opacity(depth)
        return [half + 0.5 * state[1], half + 0.5 * state[2], half + 0.5 * state[3], depth]

    def coded(state):
        depth = KAPPA * state[4]
        scale = TOP / opacity(depth)
        codes = [jnp.floor(scale * state[c] + 0.5) for c in (1, 2, 3)]
        codes.append(jnp.floor((jnp.log2(depth) - LOG_MID) * (TOP / LOG_REACH) + 0.5))
        return [jnp.clip(code, -TOP, TOP) for code in codes]

    def slab(x, carry):
        left = jnp.maximum(x - 1, 0)
        right = jnp.minimum(x + 1, EDGE - 1)

        def columns(view_even, view_odd):
            for k in range(32):
                centre = 3.0 * plane_ref[x, k]
                even = classify(centre + plane_ref[left, k])
                odd = classify(centre + plane_ref[right, k])
                view_even = advance(view_even, even)
                view_odd = advance(view_odd, odd)
                state = tuple(state_ref[n, k] for n in range(5))
                state = advance(advance(state, even), odd)
                for n in range(5):
                    state_ref[n, k] = state[n]
            return view_even, view_odd

        start = (one, zero, zero, zero, zero)
        views = columns(start, start)
        for odd in range(2):
            values = result(views[odd])
            for c in range(4):
                tile_z_ref[c, 2 * x + odd] = values[c]
        return carry

    lax.fori_loop(0, EDGE, slab, 0)
    values = coded([state_ref[n] for n in range(5)])
    for c in range(4):
        tile_x_ref[:, c * 256 : c * 256 + 256] = values[c].reshape(256, 128).T.astype(I32).astype(jnp.int16)


def render(pos, transfer, weights, *halves):
    smem = pl.BlockSpec(memory_space=pltpu.SMEM)
    return pl.pallas_call(
        functools.partial(render_kernel, len(halves) - 1),
        grid=(2,),
        in_specs=[smem, smem]
        + [pl.BlockSpec((128, HALF), lambda g: (g, 0))] * len(halves)
        + [pl.BlockSpec(weights.shape, lambda g: (0, 0, 0))],
        out_specs=(
            pl.BlockSpec((128, 1024), lambda g: (g, 0)),
            pl.BlockSpec((4, 32, 8, 128), lambda g: (0, 0, 0, g)),
        ),
        scratch_shapes=[pltpu.VMEM((EDGE, 32, 8, 128), F32), pltpu.VMEM((5, 32, 8, 128), F32)],
        out_shape=(pltpu.HBM((LOCAL, 1024), jnp.int16), pltpu.HBM((4, 32, 8, LOCAL), F32)),
        compiler_params=params(semantics=("arbitrary",)),
        cost_estimate=pl.CostEstimate(flops=10**10, bytes_accessed=10**7, transcendentals=10**7),
        name="render_bricks",
    )(pos, transfer, *[in_hbm(half) for half in halves], in_hbm(weights))


def to_frame(core, sums):
    rows = iota((8, 256), 0)
    rows = jnp.where(core == 0, rows, 7 - rows)
    keep = iota((8, 256), 1) % 8 == rows
    picture = jnp.zeros((64, 128), F32)
    for tile in range(4):
        lines = []
        for c in range(4):
            for batch in range(2):
                line = jnp.where(core == 0, sums[batch][c], sums[1 - batch][c])[tile : tile + 1]
                lines.append(jnp.where(keep, line, 0.0))
        spread = ones_where(iota((256, 128), 0) // 8 + 32 * tile == iota((256, 128), 1))
        for piece in parts_of(jnp.concatenate(lines, axis=0), 3):
            picture += nn_dot(piece, spread)
    return jnp.concatenate([picture[:48], opacity(picture[48:])], axis=0).reshape(4, 16, 128)


def compose_z_kernel(pos_ref, col_ref, row_ref, first_ref, second_ref, out_ref):
    here = iota((LOCAL, LOCAL), 0)
    there = iota((LOCAL, LOCAL), 1)
    col = jnp.concatenate([col_ref[...], col_ref[...]], axis=1)
    ahead = ones_where((col < row_ref[0:1, :]) & (here % 4 == there % 4))
    group = ones_where(iota((8, LOCAL), 0) == iota((8, LOCAL), 1) % 4)
    sums = []
    for tile_ref in (first_ref, second_ref):
        depth = tile_ref[3].reshape(256, LOCAL)
        pieces = parts_of(depth, 3)
        through = jnp.exp(-sum(nn_dot(piece, ahead) for piece in pieces))
        values = [parts_of(tile_ref[c].reshape(256, LOCAL) * through, 3) for c in range(3)] + [pieces]
        sums.append([sum(nt_dot(group, piece) for piece in pieces) for pieces in values])
    out_ref[...] = to_frame(pos_ref[2], sums)


FRAME = jax.ShapeDtypeStruct((4, 16, 128), F32)


def compose_z(pos, col, row, first, second):
    return pl.pallas_call(
        compose_z_kernel,
        out_shape=FRAME,
        in_specs=[pl.BlockSpec(memory_space=pltpu.SMEM)] + [pl.BlockSpec(memory_space=pltpu.VMEM)] * 4,
        out_specs=pl.BlockSpec(memory_space=pltpu.VMEM),
        compiler_params=params(),
        cost_estimate=pl.CostEstimate(flops=10**9, bytes_accessed=4 * 10**6, transcendentals=10**5),
        name="compose_z",
    )(pos, col, row, first, second)


def compose_x_kernel(last, pos_ref, col_ref, row_ref, tile_ref, *refs):
    here = iota((LOCAL, LOCAL), 0)
    there = iota((LOCAL, LOCAL), 1)
    col = jnp.concatenate([col_ref[...], col_ref[...]], axis=1)
    ahead = ones_where((row_ref[0:1, :] < col) & (here // 4 % 4 == there // 4 % 4))
    group = ones_where(iota((8, LOCAL), 0) == iota((8, LOCAL), 1) // 4 % 4)
    codes = [tile_ref[:, c * 256 : c * 256 + 256].astype(I32).astype(F32) for c in range(4)]
    depth = jnp.exp2(codes[3] * (LOG_REACH / TOP) + LOG_MID)
    pieces = parts_of(depth, 3)
    through = jnp.exp(-sum(nn_dot(ahead, piece) for piece in pieces))
    scale = (0.5 * opacity(depth)) * through
    values = [parts_of(scale + scale * (codes[c] * (1.0 / TOP)), 3) for c in range(3)] + [pieces]
    sums = [sum(nn_dot(group, piece) for piece in pieces) for pieces in values]
    if last:
        earlier_ref, out_ref = refs
        earlier = [earlier_ref[:, c * 256 : c * 256 + 256] for c in range(4)]
        out_ref[...] = to_frame(pos_ref[2], [earlier, sums])
    else:
        (out_ref,) = refs
        for c in range(4):
            out_ref[:, c * 256 : c * 256 + 256] = sums[c]


def compose_x(pos, col, row, tiles, *earlier):
    return pl.pallas_call(
        functools.partial(compose_x_kernel, len(earlier) > 0),
        out_shape=FRAME if earlier else jax.ShapeDtypeStruct((8, 1024), F32),
        in_specs=[pl.BlockSpec(memory_space=pltpu.SMEM)]
        + [pl.BlockSpec(memory_space=pltpu.VMEM)] * (3 + len(earlier)),
        out_specs=pl.BlockSpec(memory_space=pltpu.VMEM),
        compiler_params=params(),
        cost_estimate=pl.CostEstimate(flops=10**9, bytes_accessed=10**6, transcendentals=10**5),
        name="compose_x",
    )(pos, col, row, tiles, *earlier)


def swap_cores(values):
    return lax.ppermute(values, "c", [(0, 1), (1, 0)])


def send_bricks(outbox):
    lanes = outbox.shape[1]
    sent = lax.all_to_all(outbox.reshape(CHIPS, CAP, lanes), CHIP, split_axis=0, concat_axis=0, tiled=True)
    return sent.reshape(CHIPS * CAP, lanes)


def send_tiles(tiles):
    sent = lax.all_to_all(tiles.reshape(16, 16, 1024), PLANE, split_axis=0, concat_axis=0, tiled=True)
    return sent.reshape(LOCAL, 1024)


def body(bricks, transfer, assignment, brick_cell, depth_rank):
    plane = lax.axis_index(PLANE)
    z = lax.axis_index("z")
    core = lax.axis_index("c")
    chip = plane * 4 + z

    def position(turn):
        return jnp.stack([plane, z, core, turn]).astype(I32)

    start = position(jnp.int32(-1))
    cell = brick_cell.reshape(CHIPS, LOCAL)
    cell_row = lax.dynamic_slice_in_dim(brick_cell, chip * LOCAL, LOCAL).reshape(1, LOCAL)
    major = assignment.reshape(CHIPS, LOCAL) * 16384
    key_z = major + depth_rank[0].reshape(CHIPS, LOCAL)
    key_x = major + depth_rank[1].reshape(CHIPS, LOCAL)
    weights = [plane_weights(0), plane_weights(1)]
    other = swap_cores(split_halves(start, bricks))

    inbox = send_bricks(pack(start, cell_row, bricks, other))
    place, relay_place, handing, most = index_maps(start, cell)
    keys = order_keys(start, cell, key_z, key_x)
    handing, keys = lax.optimization_barrier((handing, keys))
    cells = unpack(place, relay_place, inbox, forward(handing, inbox))

    def frames_of(cells):
        other_half = swap_cores(cells)
        tile_x, first_z = render(start, transfer, weights[0], cells)
        landed = [send_tiles(tile_x)]
        tile_x, later_z = render(start, transfer, weights[1], cells, other_half)
        landed.append(send_tiles(tile_x))
        kz_col, kz_row, kx_col, kx_row = keys
        frame_z = compose_z(start, kz_col, kz_row, first_z, later_z)
        first_x = compose_x(start, kx_col, kx_row, landed[0])
        return frame_z, compose_x(start, kx_col, kx_row, landed[1], first_x)

    def in_rounds(carry):
        rounds = (most[0] + CAP - 1) // CAP

        def next_round(carry):
            turn, cells = carry
            pos = position(turn)
            place = index_maps(pos, cell)[0]
            inbox = send_bricks(pack(pos, cell_row, bricks, other))
            return turn + 1, cells + unpack(place, relay_place, inbox, jnp.zeros((GROUP * BACK, HALF), BF16))

        nothing = (jnp.int32(0), jnp.zeros((LOCAL, HALF), BF16))
        _, cells = lax.while_loop(lambda carry: carry[0] < rounds, next_round, nothing)
        return (jnp.zeros_like(carry[0]),) + frames_of(cells)

    carry = (most[1],) + frames_of(cells)
    return lax.while_loop(lambda carry: carry[0] > 0, in_rounds, carry)[1:]


def solution(mesh):
    fine = Mesh(mesh.devices.reshape(4, 2, 2, 4, 2), CHIP + ("c",))
    in_specs = (P(CHIP + ("c",), None), P(), P(), P(), P())
    out_specs = (P(None, ("z", "c"), PLANE), P(None, ("z", "c"), PLANE))
    return jax.shard_map(body, mesh=fine, in_specs=in_specs, out_specs=out_specs, check_vma=False)
```

time: 159 us -> 124 us (0.78)
  waiting for transfers between devices: 43.1 us -> 17 us
  blocking collectives: 0 us -> 10.1 us
  local copies, waits for them, and re-layouts: 10.7 us -> 4.58 us
  Pallas kernels: 72.9 us -> 66.8 us
  starting transfers between devices: 28.2 us -> 22.7 us
    all_to_all x3, waiting for transfers between devices: 40.8 us -> 16.9 us  [the longest x1 10.5 us: send_bricks(): lax.all_to_all(outbox.reshape(CHIPS, CAP, lanes), CHIP, split_axis=0, con...]
    all_to_all x0 -> x1, blocking collectives: none -> 10.1 us  [forward(): lax.all_to_all(handed.reshape(GROUP, BACK, HALF), NEAR, split_axis=0, con...]
    unnamed x26 -> x18, local copies, waits for them, and re-layouts: 8 us -> 1.01 us
    pallas_call x8 -> x10, Pallas kernels: 71.5 us -> 65.3 us  [the longest x2 31.4 us: render(): pl.pallas_call(functools.partial(render_kernel, len(halves) - 1), grid=(2...]
    all_to_all x3, starting transfers between devices: 27.9 us -> 22.7 us  [the longest x1 11.5 us: send_bricks(): lax.all_to_all(outbox.reshape(CHIPS, CAP, lanes), CHIP, split_axis=0, con...]
    ppermute x2, waiting for transfers between devices: 2.35 us -> 0.01 us  [swap_cores(): return lax.ppermute(values, 'c', [(0, 1), (1, 0)])]
  transfers between devices with their start and end apart: 5 -> 5, of which waited for: 4 -> 2; matrix products, arithmetic and copies ran while one was open for 2% -> 3% of each run, Pallas kernels for 27% -> 45%
where the time goes in v2:
time: 124 us; the launch traced here: 123 us
  Pallas kernels  66.8 us (54%)
  starting transfers between devices  22.7 us (18%)
  waiting for transfers between devices  17 us (14%)
  blocking collectives  10.1 us (8%)
  local copies, waits for them, and re-layouts  4.58 us (4%)
    pallas_call x2, Pallas kernels, render(): pl.pallas_call(functools.partial(render_kernel, len(halves) - 1), grid=(2...  31.4 us
    all_to_all x1, starting transfers between devices, send_bricks(): lax.all_to_all(outbox.reshape(CHIPS, CAP, lanes), CHIP, split_axis=0, con...  11.5 us
    all_to_all x2, starting transfers between devices, send_tiles(): lax.all_to_all(tiles.reshape(16, 16, 1024), PLANE, split_axis=0, concat_a...  11.1 us
    pallas_call x1, Pallas kernels, index_maps(): pl.pallas_call(index_kernel, out_shape=(pltpu.HBM((LOCAL, CHIPS * CAP), B...  10.8 us
    all_to_all x1, waiting for transfers between devices, send_bricks(): lax.all_to_all(outbox.reshape(CHIPS, CAP, lanes), CHIP, split_axis=0, con...  10.5 us
    all_to_all x1, blocking collectives, forward(): lax.all_to_all(handed.reshape(GROUP, BACK, HALF), NEAR, split_axis=0, con...  10.1 us
    pallas_call x1, Pallas kernels, order_keys(): pl.pallas_call(key_kernel, out_shape=(col, row, col, row), in_specs=[pl.B...  8.93 us
    all_to_all x2, waiting for transfers between devices, send_tiles(): lax.all_to_all(tiles.reshape(16, 16, 1024), PLANE, split_axis=0, concat_a...  6.47 us
  transfers between devices with their start and end apart: 5, of which 2 were waited for; matrix products, arithmetic and copies ran while one was open for 3% of the time, Pallas kernels for 45%

profile of v2, /device:TPU:0, one launch (start us, length us, event | category | flops | bytes accessed | tf_op | source)
XLA Modules:
  0.0 123.1 jit_solution(13492579298598682407)
XLA Ops:
  0.6 0.0 copy-start.5
  0.6 0.0 copy-start.8
  0.7 0.1 pad_add_fusion.1.pos_ref
  0.7 1.4 %split_halves.1 = bf16[128,2048]{1,0:T(8,128)(2,1)S(1)} custom-call(s32[4]{0:T(128)S(1)} %pad_add_fusion.1.pos_ref, bf16[128,4096]{1,0:T(8,128)(2,1)} %bricks_ref.3), custom_call_target="tpu_custom_call" | custom-call | tf_op jit(solution)/shard_map/split_halves/pallas_call | solution.py:107
  2.2 0.1 collective-permute-start.1
  2.3 0.9 reshape.57.cell_ref
  3.2 0.8 dynamic_slice.3
  3.9 1.3 %slice_reduce_fusion = (s32[16384]{0:T(1024)S(1)}, s32[16384]{0:T(1024)S(1)}) fusion(s32[2,16384]{1,0:T(2,128)} %param.15), kind=kLoop, calls=%fused_computation.1 | loop fusion | bytes 262144 | tf_op jit(solution)/shard_map/slice | solution.py:638
  5.3 0.0 copy-done.8
  5.3 0.2 multiply_reduce_fusion
  5.5 0.0 collective-permute-done.1.other_ref
  5.5 0.0 copy-start.7
  5.5 0.0 copy-done.5
  5.5 3.3 %pack_outbox.2 = bf16[512,2048]{1,0:T(8,128)(2,1)} custom-call(s32[4]{0:T(128)S(1)} %pad_add_fusion.1.pos_ref, s32[1,256]{1,0:T(1,128)S(1)} %bitcast.50, bf16[128,4096]{1,0:T(8,128)(2,1)S(1)} %copy-done.5, bf16[128,2048]{1,0:T(8,128)(2,1)S(1)} %collective-permute-done.1.other_ref), custom_call_target="tpu_custom_call" | custom-call | tf_op jit(solution)/shard_map/pack_outbox/pallas_call | solution.py:218
  8.8 0.0 copy-done.7
  8.8 11.5 %all-to-all-start.3 = ((bf16[64,8,2048]{2,1,0:T(8,128)(2,1)}), bf16[64,8,2048]{2,1,0:T(8,128)(2,1)S(1)}, u32[]{:S(2)}, u32[]{:S(2)}) async-start(bf16[64,8,2048]{2,1,0:T(8,128)(2,1)} %bitcast.49), calls=%async_computation.3 | async-start | bytes 4194304 | tf_op jit(solution)/shard_map/all_to_all | solution.py:615
  20.4 10.8 %index_maps.2 = (bf16[256,512]{1,0:T(8,128)(2,1)}, bf16[256,128]{1,0:T(8,128)(2,1)}, bf16[64,512]{1,0:T(8,128)(2,1)S(1)}, s32[2]{0:T(128)S(1)}) custom-call(s32[4]{0:T(128)S(1)} %pad_add_fusion.1.pos_ref, s32[64,256]{1,0:T(8,128)S(1)} %reshape.57.cell_ref), custom_call_target="tpu_custom_call" | custom-call | flops 10000000000 | bytes 1000000 | tf_op jit(solution)/shard_map/index_maps/pallas_call | solution.py:316
  31.2 8.9 %order_keys.1 = (f32[256,128]{1,0:T(8,128)S(1)}, f32[8,256]{1,0:T(8,128)}, f32[256,128]{1,0:T(8,128)S(1)}, f32[8,256]{1,0:T(8,128)}) custom-call(s32[4]{0:T(128)S(1)} %pad_add_fusion.1.pos_ref, s32[64,256]{1,0:T(8,128)S(1)} %reshape.57.cell_ref, s32[64,256]{1,0:T(8,128)S(1)} %get-tuple-element.325.key_z_ref, s32[64,256]{1,0:T(8,128)S(1)} %get-tuple-element.324.key_x_ref), custom_call_target="tpu_custom_call" | custom-call | flops 10000000000 | bytes 1000000 | tf_op jit(solution)/shard_map/order_keys/pallas_call | solution.py:374
  40.1 10.5 %all-to-all-done.3 = bf16[64,8,2048]{2,1,0:T(8,128)(2,1)S(1)} async-done(((bf16[64,8,2048]{2,1,0:T(8,128)(2,1)}), bf16[64,8,2048]{2,1,0:T(8,128)(2,1)S(1)}, u32[]{:S(2)}, u32[]{:S(2)}) %all-to-all-start.3) | async-done | bytes 2097184 | tf_op jit(solution)/shard_map/all_to_all | solution.py:615
  50.6 0.5 hand_on.1
  51.1 0.0 copy-start.10
  51.1 10.1 %all_to_all.38 = bf16[8,8,2048]{2,1,0:T(8,128)(2,1)S(1)} all-to-all(bf16[8,8,2048]{2,1,0:T(8,128)(2,1)S(1)} %bitcast.43), channel_id=1, replica_groups=mesh['y'=4,'x1'=2,'x0'=2,'z'=4,'c'=2] {'x0','z'}, dimensions={0} | all-to-all | bytes 524288 | tf_op jit(solution)/shard_map/all_to_all | solution.py:401
  61.2 3.6 %unpack_inbox.2.refs_0_ = bf16[256,2048]{1,0:T(8,128)(2,1)} custom-call(bf16[256,512]{1,0:T(8,128)(2,1)} %get-tuple-element.190.place_ref, bf16[256,128]{1,0:T(8,128)(2,1)} %get-tuple-element.464.relay_ref, bf16[512,2048]{1,0:T(8,128)(2,1)S(1)} %bitcast.39, bf16[64,2048]{1,0:T(8,128)(2,1)S(1)} %bitcast.42), custom_call_target="tpu_custom_call" | custom-call | flops 1000000000 | bytes 3000000 | tf_op jit(solution)/shard_map/unpack_inbox/pallas_call | solution.py:413
  64.8 0.0 collective-permute-start.2
  64.8 0.0 copy-done.10
  64.8 15.3 %render_bricks.4 = (s16[256,1024]{1,0:T(8,128)(2,1)}, f32[4,32,8,256]{3,2,1,0:T(8,128)}) custom-call(s32[4]{0:T(128)S(1)} %pad_add_fusion.1.pos_ref, f32[2,4]{1,0:T(2,128)S(1)} %copy-done.10, bf16[256,2048]{1,0:T(8,128)(2,1)} %unpack_inbox.2.refs_0_, bf16[2,256,128]{2,1,0:T(8,128)(2,1)} %constant.66.clone.refs_1_), custom_call_target="tpu_custom_call" | custom-call | flops 10000000000 | bytes 10000000 | tf_op jit(solution)/shard_map/render_bricks/pallas_call | solution.py:507
  80.1 3.9 %all-to-all-start.6 = ((s16[16,16,1024]{2,1,0:T(8,128)(2,1)}), s16[16,16,1024]{2,1,0:T(8,128)(2,1)S(1)}, u32[]{:S(2)}, u32[]{:S(2)}) async-start(s16[16,16,1024]{2,1,0:T(8,128)(2,1)} %bitcast.53), calls=%async_computation.6 | async-start | bytes 1048576 | tf_op jit(solution)/shard_map/all_to_all | solution.py:620
  84.0 0.0 copy-start.14
  84.0 0.0 collective-permute-done.2.refs_1_
  84.0 0.0 copy-start.9
  84.0 1.0 copy-done.9
  85.0 16.1 %render_bricks.5 = (s16[256,1024]{1,0:T(8,128)(2,1)}, f32[4,32,8,256]{3,2,1,0:T(8,128)}) custom-call(s32[4]{0:T(128)S(1)} %pad_add_fusion.1.pos_ref, f32[2,4]{1,0:T(2,128)S(1)} %copy-done.10, bf16[256,2048]{1,0:T(8,128)(2,1)} %unpack_inbox.2.refs_0_, bf16[256,2048]{1,0:T(8,128)(2,1)} %copy-done.9, bf16[2,256,256]{2,1,0:T(8,128)(2,1)} %constant.67.clone.refs_2_), custom_call_target="tpu_custom_call" | custom-call | flops 10000000000 | bytes 10000000 | tf_op jit(solution)/shard_map/render_bricks/pallas_call | solution.py:507
  101.1 0.0 all-to-all-done.6
  101.1 7.2 %all-to-all-start.5 = ((s16[16,16,1024]{2,1,0:T(8,128)(2,1)}), s16[16,16,1024]{2,1,0:T(8,128)(2,1)S(1)}, u32[]{:S(2)}, u32[]{:S(2)}) async-start(s16[16,16,1024]{2,1,0:T(8,128)(2,1)} %bitcast.52), calls=%async_computation.5 | async-start | bytes 1048576 | tf_op jit(solution)/shard_map/all_to_all | solution.py:620
  108.3 0.0 copy-start
  108.4 0.0 copy-start.2
  108.4 0.0 copy-start.12
  108.4 0.6 slice.12
  109.0 0.0 copy-done.14
  109.0 1.5 %compose_x.4.refs_0_ = f32[8,1024]{1,0:T(8,128)S(1)} custom-call(s32[4]{0:T(128)S(1)} %pad_add_fusion.1.pos_ref, f32[256,128]{1,0:T(8,128)S(1)} %get-tuple-element.469.col_ref, f32[8,256]{1,0:T(8,128)S(1)} %copy-done.14, s16[256,1024]{1,0:T(8,128)(2,1)S(1)} %bitcast.44), custom_call_target="tpu_custom_call" | custom-call | flops 1000000000 | bytes 1000000 | tf_op jit(solution)/shard_map/compose_x/pallas_call | solution.py:597
  110.4 0.0 copy-done
  110.4 0.0 copy-done.2
  110.4 0.0 copy-done.12
  110.5 3.0 %compose_z.2 = f32[4,16,128]{2,1,0:T(8,128)} custom-call(s32[4]{0:T(128)S(1)} %pad_add_fusion.1.pos_ref, f32[256,128]{1,0:T(8,128)S(1)} %get-tuple-element.467.col_ref, f32[8,256]{1,0:T(8,128)S(1)} %copy-done.12, f32[4,32,8,256]{3,2,1,0:T(8,128)S(1)} %copy-done, f32[4,32,8,256]{3,2,1,0:T(8,128)S(1)} %copy-done.2), custom_call_target="tpu_custom_call" | custom-call | flops 1000000000 | bytes 4000000 | tf_op jit(solution)/shard_map/compose_z/pallas_call | solution.py:562
  113.5 6.5 %all-to-all-done.5 = s16[16,16,1024]{2,1,0:T(8,128)(2,1)S(1)} async-done(((s16[16,16,1024]{2,1,0:T(8,128)(2,1)}), s16[16,16,1024]{2,1,0:T(8,128)(2,1)S(1)}, u32[]{:S(2)}, u32[]{:S(2)}) %all-to-all-start.5) | async-done | bytes 524320 | tf_op jit(solution)/shard_map/all_to_all | solution.py:620
  120.0 2.3 %compose_x.5 = f32[4,16,128]{2,1,0:T(8,128)} custom-call(s32[4]{0:T(128)S(1)} %pad_add_fusion.1.pos_ref, f32[256,128]{1,0:T(8,128)S(1)} %get-tuple-element.469.col_ref, f32[8,256]{1,0:T(8,128)S(1)} %copy-done.14, s16[256,1024]{1,0:T(8,128)(2,1)S(1)} %bitcast.45, f32[8,1024]{1,0:T(8,128)S(1)} %compose_x.4.refs_0_), custom_call_target="tpu_custom_call" | custom-call | flops 1000000000 | bytes 1000000 | tf_op jit(solution)/shard_map/compose_x/pallas_call | solution.py:597
  122.3 0.6 while.23
  (4 shorter events, 0.1 us)
Async XLA Ops:
  0.6 4.9 %copy-start.5 = (bf16[128,4096]{1,0:T(8,128)(2,1)S(1)}, bf16[128,4096]{1,0:T(8,128)(2,1)}, u32[]{:S(2)}) copy-start(bf16[128,4096]{1,0:T(8,128)(2,1)} %bricks_ref.3) | copy-start | bytes 3145732
  0.6 4.6 %copy-start.8 = (s32[16384,1]{0,1:T(1,128)S(1)}, s32[16384,1]{0,1:T(1,128)}, u32[]{:S(2)}) copy-start(s32[16384,1]{0,1:T(1,128)} %param.13) | copy-start | bytes 196612
  2.2 3.3 %collective-permute-start.1 = (bf16[128,2048]{1,0:T(8,128)(2,1)S(1)}, bf16[128,2048]{1,0:T(8,128)(2,1)S(1)}, u32[]{:S(2)}, u32[]{:S(2)}) collective-permute-start(bf16[128,2048]{1,0:T(8,128)(2,1)S(1)} %split_halves.1), channel_id=1, source_target_pairs={{0,1},{1,0},{2,3},{3,2},{4,5},{5,4},{6,7},{7,6},{8,9},{9,8},{10,11... | collective-permute-start | bytes 1572872 | tf_op jit(solution)/shard_map/ppermute | solution.py:610
  5.5 3.3 %copy-start.7 = (bf16[128,2048]{1,0:T(8,128)(2,1)}, bf16[128,2048]{1,0:T(8,128)(2,1)S(1)}, u32[]{:S(2)}) copy-start(bf16[128,2048]{1,0:T(8,128)(2,1)S(1)} %collective-permute-done.1.other_ref) | copy-start | bytes 1572868
  8.8 41.8 %all-to-all-start.3 = ((bf16[64,8,2048]{2,1,0:T(8,128)(2,1)}), bf16[64,8,2048]{2,1,0:T(8,128)(2,1)S(1)}, u32[]{:S(2)}, u32[]{:S(2)}) async-start(bf16[64,8,2048]{2,1,0:T(8,128)(2,1)} %bitcast.49), calls=%async_computation.3 | async-start | bytes 4194304 | tf_op jit(solution)/shard_map/all_to_all | solution.py:615
  51.1 13.7 %copy-start.10 = (f32[2,4]{1,0:T(2,128)S(1)}, f32[2,4]{1,0:T(2,128)}, u32[]{:S(2)}) copy-start(f32[2,4]{1,0:T(2,128)} %transfer_ref.3) | copy-start | bytes 100
  64.8 19.3 %collective-permute-start.2 = (bf16[256,2048]{1,0:T(8,128)(2,1)}, bf16[256,2048]{1,0:T(8,128)(2,1)S(1)}, u32[]{:S(2)}, u32[]{:S(2)}) collective-permute-start(bf16[256,2048]{1,0:T(8,128)(2,1)} %unpack_inbox.2.refs_0_), channel_id=1, source_target_pairs={{0,1},{1,0},{2,3},{3,2},{4,5},{5,4},{6,7},{7,6},{8,9},{9,8},{10,11... | collective-permute-start | bytes 3145736 | tf_op jit(solution)/shard_map/ppermute | solution.py:610
  80.1 21.0 %all-to-all-start.6 = ((s16[16,16,1024]{2,1,0:T(8,128)(2,1)}), s16[16,16,1024]{2,1,0:T(8,128)(2,1)S(1)}, u32[]{:S(2)}, u32[]{:S(2)}) async-start(s16[16,16,1024]{2,1,0:T(8,128)(2,1)} %bitcast.53), calls=%async_computation.6 | async-start | bytes 1048576 | tf_op jit(solution)/shard_map/all_to_all | solution.py:620
  84.0 25.0 %copy-start.14 = (f32[8,256]{1,0:T(8,128)S(1)}, f32[8,256]{1,0:T(8,128)}, u32[]{:S(2)}) copy-start(f32[8,256]{1,0:T(8,128)} %get-tuple-element.470.row_ref) | copy-start | bytes 24580
  84.0 1.0 copy-start.9
  101.1 18.9 %all-to-all-start.5 = ((s16[16,16,1024]{2,1,0:T(8,128)(2,1)}), s16[16,16,1024]{2,1,0:T(8,128)(2,1)S(1)}, u32[]{:S(2)}, u32[]{:S(2)}) async-start(s16[16,16,1024]{2,1,0:T(8,128)(2,1)} %bitcast.52), calls=%async_computation.5 | async-start | bytes 1048576 | tf_op jit(solution)/shard_map/all_to_all | solution.py:620
  108.3 2.1 %copy-start = (f32[4,32,8,256]{3,2,1,0:T(8,128)S(1)}, f32[4,32,8,256]{3,2,1,0:T(8,128)}, u32[]{:S(2)}) copy-start(f32[4,32,8,256]{3,2,1,0:T(8,128)} %get-tuple-element.193.first_ref) | copy-start | bytes 3145732
  108.4 2.1 %copy-start.2 = (f32[4,32,8,256]{3,2,1,0:T(8,128)S(1)}, f32[4,32,8,256]{3,2,1,0:T(8,128)}, u32[]{:S(2)}) copy-start(f32[4,32,8,256]{3,2,1,0:T(8,128)} %get-tuple-element.194.second_ref) | copy-start | bytes 3145732
  108.4 2.1 %copy-start.12 = (f32[8,256]{1,0:T(8,128)S(1)}, f32[8,256]{1,0:T(8,128)}, u32[]{:S(2)}) copy-start(f32[8,256]{1,0:T(8,128)} %get-tuple-element.468.row_ref) | copy-start | bytes 24580

commit v3 on v2

--- a/solution.py
+++ b/solution.py
@@ -19,6 +19,7 @@
 CHIPS = 64
 LOCAL = 256
 HALF = EDGE * EDGE * EDGE // 2
+PIECE = 512
 F32 = jnp.float32
 BF16 = jnp.bfloat16
 I32 = jnp.int32
@@ -94,24 +95,6 @@
                 half, y = m // 8, m % 8
                 out[core, :, sub, half, y if core == 0 else 7 - y] += 0.25 * share * up
     return jnp.asarray(out.reshape(2, 256, 128 * (1 + batch)), BF16)
-
-
-def split_kernel(pos_ref, bricks_ref, send_ref):
-    other = 1 - pos_ref[2]
-    for x in range(EDGE):
-        start = pl.multiple_of(x * 256 + other * 128, 128)
-        send_ref[:, x * 128 : x * 128 + 128] = bricks_ref[:, pl.ds(start, 128)]
-
-
-def split_halves(pos, bricks):
-    return pl.pallas_call(
-        split_kernel,
-        out_shape=jax.ShapeDtypeStruct((128, HALF), BF16),
-        in_specs=[pl.BlockSpec(memory_space=pltpu.SMEM), pl.BlockSpec(memory_space=pltpu.VMEM)],
-        out_specs=pl.BlockSpec(memory_space=pltpu.VMEM),
-        compiler_params=params(),
-        name="split_halves",
-    )(pos, bricks)
 
 
 def chip_of(cell):
@@ -152,10 +135,7 @@
     return amounts, starts, bases, over
 
 
-def pack_kernel(
-    pos_ref, cell_ref, bricks_ref, other_ref, out_ref, full_ref, box_ref, sems
-):
-    core = pos_ref[2]
+def plan_kernel(pos_ref, cell_ref, slot_ref):
     turn = pos_ref[3]
     kind = (pos_ref[0] * 4 + pos_ref[1]) % CLASSES
     dest = chip_of(cell_ref[...])
@@ -179,53 +159,60 @@
         inside = (over >= begin) & (over < found[n : n + 1])
         relay = dest // GROUP * GROUP + (dest + shift_of(n, kind)) % GROUP
         relayed = jnp.where(inside, relay * CAP + found[TRIES + n : TRIES + n + 1] + over - begin, relayed)
-    slot = jnp.where(turn < 0, relayed, in_turn)
-    mine = pl.multiple_of(core * 128, 128)
-    theirs = pl.multiple_of(128 - core * 128, 128)
-    for x in range(EDGE):
-        start = pl.multiple_of(x * 256 + core * 128, 128)
-        full_ref[pl.ds(mine, 128), x * 128 : x * 128 + 128] = bricks_ref[:, pl.ds(start, 128)]
-    full_ref[pl.ds(theirs, 128), :] = other_ref[...]
+    slot_ref[...] = jnp.where(turn < 0, relayed, in_turn)
+
+
+def plan_slots(pos, cell_row):
+    return pl.pallas_call(
+        plan_kernel,
+        out_shape=jax.ShapeDtypeStruct((1, LOCAL), I32),
+        in_specs=[pl.BlockSpec(memory_space=pltpu.SMEM), pl.BlockSpec(memory_space=pltpu.VMEM)],
+        out_specs=pl.BlockSpec(memory_space=pltpu.VMEM),
+        compiler_params=params(),
+        cost_estimate=pl.CostEstimate(flops=10**9, bytes_accessed=10**6, transcendentals=0),
+        name="plan_slots",
+    )(pos, cell_row)
+
+
+def pack_kernel(pos_ref, slot_ref, bricks_ref, other_ref, out_ref, full_ref, box_ref, sems):
+    core = pos_ref[2]
+    slot = slot_ref[...]
+    for n, ref in enumerate((bricks_ref, other_ref)):
+        rows = pl.ds(pl.multiple_of((core + n) % 2 * 128, 128), 128)
+        for x in range(EDGE):
+            start = pl.multiple_of(x * 256 + core * 128, 128)
+            full_ref[rows, x * 128 : x * 128 + 128] = ref[:, pl.ds(start, 128)]
+    pick = ones_where(iota((CHIPS * CAP, LOCAL), 0) == slot)
     copies = []
-    for block in range(CHIPS * CAP // 128):
-        pick = ones_where(iota((128, LOCAL), 0) + block * 128 == slot)
-        rows = pl.ds(block * 128, 128)
-        box_ref[rows, :] = nn_dot(pick, full_ref[...]).astype(BF16)
-        copy = pltpu.make_async_copy(box_ref.at[rows, :], out_ref.at[rows, :], sems.at[block])
+    for at in range(HALF // PIECE):
+        lanes = pl.ds(at * PIECE, PIECE)
+        box_ref[:, lanes] = nn_dot(pick, full_ref[:, lanes]).astype(BF16)
+        copy = pltpu.make_async_copy(box_ref.at[:, lanes], out_ref.at[:, lanes], sems.at[at])
         copy.start()
         copies.append(copy)
     for copy in copies:
         copy.wait()
 
 
-def pack(pos, cell_row, bricks, other):
+def pack(pos, slot, bricks, other):
     rows = CHIPS * CAP
-    grid_spec = pltpu.PrefetchScalarGridSpec(
-        num_scalar_prefetch=1,
-        grid=(1,),
-        in_specs=[
-            pl.BlockSpec((1, LOCAL), lambda s, pos: (0, 0)),
-            pl.BlockSpec((128, 2 * HALF), lambda s, pos: (0, 0)),
-            pl.BlockSpec((128, HALF), lambda s, pos: (0, 0)),
-        ],
+    return pl.pallas_call(
+        pack_kernel,
+        in_specs=[pl.BlockSpec(memory_space=pltpu.SMEM)] + [pl.BlockSpec(memory_space=pltpu.VMEM)] * 3,
         out_specs=pl.BlockSpec(memory_space=pltpu.HBM),
         scratch_shapes=[
             pltpu.VMEM((LOCAL, HALF), BF16),
             pltpu.VMEM((rows, HALF), BF16),
-            pltpu.SemaphoreType.DMA((rows // 128,)),
+            pltpu.SemaphoreType.DMA((HALF // PIECE,)),
         ],
-    )
-    return pl.pallas_call(
-        pack_kernel,
-        grid_spec=grid_spec,
         out_shape=pltpu.HBM((rows, HALF), BF16),
         compiler_params=params(),
         name="pack_outbox",
-    )(pos, cell_row, bricks, other)
+    )(pos, slot, bricks, other)
 
 
 def index_kernel(
-    pos_ref, cell_ref, place_ref, relay_place_ref, forward_ref, most_ref,
+    pos_ref, cell_ref, place_ref, relay_place_ref, forward_ref, most_ref, left_ref,
     here_ref, slot_ref, relay_ref, dest_ref, count_ref, side_ref
 ):
     plane, z, turn = pos_ref[0], pos_ref[1], pos_ref[3]
@@ -286,7 +273,7 @@
         at = near * BACK + order + along(column(prefix, first + near))
         handed = jnp.where((order >= 0) & (order < along(column(amount, first + near))), at, handed)
     forward_ref[...] = ones_where(iota((GROUP * BACK, slots), 0) == handed)
-    most_ref[1] = jnp.max(left).astype(I32)
+    left_ref[0] = jnp.max(left).astype(I32)
     relay_ref[...] = jnp.where(for_me & (turn < 0), relay, -1)
     group = iota((CHIPS, LOCAL), 0) % (128 // CAP)
     later = rank - jnp.maximum(turn, 0) * CAP
@@ -319,7 +306,8 @@
             pltpu.HBM((LOCAL, CHIPS * CAP), BF16),
             pltpu.HBM((LOCAL, 128), BF16),
             jax.ShapeDtypeStruct((GROUP * BACK, CHIPS * CAP), BF16),
-            jax.ShapeDtypeStruct((2,), I32),
+            jax.ShapeDtypeStruct((1,), I32),
+            jax.ShapeDtypeStruct((1,), I32),
         ),
         in_specs=[pl.BlockSpec(memory_space=pltpu.SMEM), vmem],
         grid=(1,),
@@ -328,6 +316,7 @@
             pl.BlockSpec((LOCAL, 128), lambda s: (0, 0)),
             pl.BlockSpec((GROUP * BACK, CHIPS * CAP), lambda s: (0, 0)),
             pl.BlockSpec(memory_space=pltpu.SMEM),
+            pl.BlockSpec(memory_space=pltpu.SMEM),
         ),
         scratch_shapes=[pltpu.VMEM((CHIPS, LOCAL), I32)] * 4
         + [pltpu.VMEM((CHIPS, 128), F32), pltpu.VMEM((LOCAL, 128), F32)],
@@ -337,7 +326,7 @@
     )(pos, cell)
 
 
-def key_kernel(pos_ref, cell_ref, key_z_ref, key_x_ref, kz_col_ref, kz_row_ref, kx_col_ref, kx_row_ref, here_ref, there_ref):
+def key_kernel(pos_ref, cell_ref, key_z_ref, key_x_ref, ahead_z_ref, ahead_x_ref, here_ref, there_ref):
     plane, z = pos_ref[0], pos_ref[1]
     cell = cell_ref[...]
     gx, gz, gy = cell % 64, cell // 64 % 64, cell // 4096
@@ -360,22 +349,24 @@
 
     nothing = jnp.zeros((LOCAL, 8), F32)
     sums = lax.fori_loop(0, CHIPS, source, (nothing, nothing), unroll=4)
-    for part, col_ref, row_ref in ((sums[0], kz_col_ref, kz_row_ref), (sums[1], kx_col_ref, kx_row_ref)):
-        col = part[:, 0:1] + 256.0 * part[:, 1:2] + 65536.0 * part[:, 2:3]
-        wide = jnp.broadcast_to(col, (LOCAL, 128))
-        col_ref[...] = wide
-        row_ref[...] = wide.T[0:8]
+    across = iota((LOCAL, LOCAL), 1)
+
+    def key_of(part):
+        return jnp.broadcast_to(part[:, 0:1] + 256.0 * part[:, 1:2] + 65536.0 * part[:, 2:3], (LOCAL, LOCAL))
+
+    key_z, key_x = key_of(sums[0]), key_of(sums[1])
+    ahead_z_ref[...] = ones_where((key_z < key_z.T) & (down % 4 == across % 4))
+    ahead_x_ref[...] = ones_where((key_x.T < key_x) & (down // 4 % 4 == across // 4 % 4))
 
 
 def order_keys(pos, cell, key_z, key_x):
     vmem = pl.BlockSpec(memory_space=pltpu.VMEM)
-    col = jax.ShapeDtypeStruct((LOCAL, 128), F32)
-    row = jax.ShapeDtypeStruct((8, LOCAL), F32)
+    ahead = jax.ShapeDtypeStruct((LOCAL, LOCAL), BF16)
     return pl.pallas_call(
         key_kernel,
-        out_shape=(col, row, col, row),
+        out_shape=(ahead, ahead),
         in_specs=[pl.BlockSpec(memory_space=pltpu.SMEM), vmem, vmem, vmem],
-        out_specs=(vmem,) * 4,
+        out_specs=(vmem,) * 2,
         scratch_shapes=[pltpu.VMEM((CHIPS, LOCAL), I32)] * 2,
         compiler_params=params(),
         cost_estimate=pl.CostEstimate(flops=10**10, bytes_accessed=10**6, transcendentals=0),
@@ -402,44 +393,46 @@
     return sent.reshape(GROUP * BACK, HALF)
 
 
-def unpack_kernel(place_ref, relay_ref, recv_ref, back_ref, cells_ref):
-    cells = nn_dot(place_ref[...], recv_ref[...]) + nn_dot(relay_ref[:, : GROUP * BACK], back_ref[...])
-    cells_ref[...] = cells.astype(BF16)
+def unpack_kernel(place_ref, relay_ref, recv_ref, back_ref, out_ref, cells_ref, sems):
+    copies = []
+    for at in range(HALF // PIECE):
+        lanes = pl.ds(at * PIECE, PIECE)
+        cells = nn_dot(place_ref[...], recv_ref[:, lanes]) + nn_dot(relay_ref[:, : GROUP * BACK], back_ref[:, lanes])
+        cells_ref[:, lanes] = cells.astype(BF16)
+        copies.append(pltpu.make_async_copy(cells_ref.at[:, lanes], out_ref.at[:, lanes], sems.at[at]))
+        copies[-1].start()
+    for copy in copies:
+        copy.wait()
 
 
 def unpack(place, relay_place, received, back):
-    rows, lanes = received.shape
-    width = 512
+    vmem = pl.BlockSpec(memory_space=pltpu.VMEM)
     return pl.pallas_call(
         unpack_kernel,
-        grid=(lanes // width,),
-        out_shape=pltpu.HBM((LOCAL, lanes), BF16),
-        in_specs=[
-            pl.BlockSpec((LOCAL, rows), lambda s: (0, 0)),
-            pl.BlockSpec((LOCAL, 128), lambda s: (0, 0)),
-            pl.BlockSpec((rows, width), lambda s: (0, s)),
-            pl.BlockSpec((GROUP * BACK, width), lambda s: (0, s)),
-        ],
-        out_specs=pl.BlockSpec((LOCAL, width), lambda s: (0, s)),
-        compiler_params=params(semantics=("arbitrary",)),
+        out_shape=pltpu.HBM((LOCAL, HALF), BF16),
+        in_specs=[vmem] * 4,
+        out_specs=pl.BlockSpec(memory_space=pltpu.HBM),
+        scratch_shapes=[pltpu.VMEM((LOCAL, HALF), BF16), pltpu.SemaphoreType.DMA((HALF // PIECE,))],
+        compiler_params=params(),
         cost_estimate=pl.CostEstimate(flops=10**9, bytes_accessed=3 * 10**6, transcendentals=0),
         name="unpack_inbox",
-    )(in_hbm(place), in_hbm(relay_place), received, back)
-
-
-def render_kernel(batch, pos_ref, transfer_ref, *refs):
-    halves, (weights_ref, tile_x_ref, tile_z_ref, plane_ref, state_ref) = refs[: 1 + batch], refs[1 + batch :]
-    weights = weights_ref[pos_ref[2]]
+    )(place, relay_place, received, back)
+
+
+def render_group(views, pos_ref, transfer_ref, halves, weights_ref, tile_x_ref, tile_z_ref, plane_ref, state_ref):
+    with_x, with_z = "x" in views, "z" in views
+
     for x in range(EDGE):
         operand = jnp.concatenate([ref[:, x * 128 : x * 128 + 128] for ref in halves], axis=1)
-        plane_ref[x] = nt_dot(weights, operand).reshape(32, 8, 128)
+        plane_ref[x] = nt_dot(weights_ref[pos_ref[2]], operand).reshape(32, 8, 128)
     slope = [transfer_ref[0, 0] * LOG2E] + [0.5 * transfer_ref[0, c] for c in (1, 2, 3)]
     offset = [transfer_ref[1, 0] * LOG2E] + [0.5 * transfer_ref[1, c] for c in (1, 2, 3)]
     zero = jnp.zeros((8, 128), F32)
     one = jnp.ones((8, 128), F32)
-    state_ref[0] = jnp.ones((32, 8, 128), F32)
-    for n in range(1, 5):
-        state_ref[n] = jnp.zeros((32, 8, 128), F32)
+    if with_x:
+        state_ref[0] = jnp.ones((32, 8, 128), F32)
+        for n in range(1, 5):
+            state_ref[n] = jnp.zeros((32, 8, 128), F32)
 
     def classify(sample):
         grown = jnp.exp2(slope[0] * sample + offset[0])
@@ -480,46 +473,67 @@
                 centre = 3.0 * plane_ref[x, k]
                 even = classify(centre + plane_ref[left, k])
                 odd = classify(centre + plane_ref[right, k])
-                view_even = advance(view_even, even)
-                view_odd = advance(view_odd, odd)
-                state = tuple(state_ref[n, k] for n in range(5))
-                state = advance(advance(state, even), odd)
-                for n in range(5):
-                    state_ref[n, k] = state[n]
+                if with_z:
+                    view_even = advance(view_even, even)
+                    view_odd = advance(view_odd, odd)
+                if with_x:
+                    state = tuple(state_ref[n, k] for n in range(5))
+                    state = advance(advance(state, even), odd)
+                    for n in range(5):
+                        state_ref[n, k] = state[n]
             return view_even, view_odd
 
         start = (one, zero, zero, zero, zero)
-        views = columns(start, start)
-        for odd in range(2):
-            values = result(views[odd])
+        pixels = columns(start, start)
+        for odd in range(2 if with_z else 0):
+            values = result(pixels[odd])
             for c in range(4):
                 tile_z_ref[c, 2 * x + odd] = values[c]
         return carry
 
     lax.fori_loop(0, EDGE, slab, 0)
-    values = coded([state_ref[n] for n in range(5)])
-    for c in range(4):
-        tile_x_ref[:, c * 256 : c * 256 + 256] = values[c].reshape(256, 128).T.astype(I32).astype(jnp.int16)
-
-
-def render(pos, transfer, weights, *halves):
+    if with_x:
+        values = coded([state_ref[n] for n in range(5)])
+        for c in range(4):
+            tile_x_ref[:, c * 256 : c * 256 + 256] = values[c].reshape(256, 128).T.astype(I32).astype(jnp.int16)
+
+
+def render_kernel(views, count, pos_ref, transfer_ref, *refs):
+    halves, weights_ref, rest = refs[:count], refs[count], list(refs[count + 1 :])
+    tile_x_ref = rest.pop(0) if "x" in views[0] else None
+    tile_z_ref, plane_ref, state_ref = rest
+    for g, wanted in enumerate(views):
+        if len(set(views)) == 1:
+            if g == 0:
+                render_group(wanted, pos_ref, transfer_ref, halves, weights_ref, tile_x_ref, tile_z_ref, plane_ref, state_ref)
+        else:
+
+            @pl.when(pl.program_id(0) == g)
+            def _():
+                render_group(wanted, pos_ref, transfer_ref, halves, weights_ref, tile_x_ref, tile_z_ref, plane_ref, state_ref)
+
+
+def render(views, first, pos, transfer, weights, *halves):
     smem = pl.BlockSpec(memory_space=pltpu.SMEM)
-    return pl.pallas_call(
-        functools.partial(render_kernel, len(halves) - 1),
-        grid=(2,),
+    groups_z = sum("z" in wanted for wanted in views)
+    out_specs = [pl.BlockSpec((4, 32, 8, 128), lambda g: (0, 0, 0, jnp.minimum(g, groups_z - 1)))]
+    out_shape = [pltpu.HBM((4, 32, 8, 128 * groups_z), F32)]
+    if "x" in views[0]:
+        out_specs.insert(0, pl.BlockSpec((128, 1024), lambda g: (g, 0)))
+        out_shape.insert(0, pltpu.HBM((128 * len(views), 1024), jnp.int16))
+    return pl.pallas_call(
+        functools.partial(render_kernel, views, len(halves)),
+        grid=(len(views),),
         in_specs=[smem, smem]
-        + [pl.BlockSpec((128, HALF), lambda g: (g, 0))] * len(halves)
+        + [pl.BlockSpec((128, HALF), lambda g: (g + first, 0))] * len(halves)
         + [pl.BlockSpec(weights.shape, lambda g: (0, 0, 0))],
-        out_specs=(
-            pl.BlockSpec((128, 1024), lambda g: (g, 0)),
-            pl.BlockSpec((4, 32, 8, 128), lambda g: (0, 0, 0, g)),
-        ),
+        out_specs=out_specs,
         scratch_shapes=[pltpu.VMEM((EDGE, 32, 8, 128), F32), pltpu.VMEM((5, 32, 8, 128), F32)],
-        out_shape=(pltpu.HBM((LOCAL, 1024), jnp.int16), pltpu.HBM((4, 32, 8, LOCAL), F32)),
+        out_shape=out_shape,
         compiler_params=params(semantics=("arbitrary",)),
         cost_estimate=pl.CostEstimate(flops=10**10, bytes_accessed=10**7, transcendentals=10**7),
-        name="render_bricks",
-    )(pos, transfer, *[in_hbm(half) for half in halves], in_hbm(weights))
+        name="render_" + "_".join(views),
+    )(pos, transfer, in_hbm(halves[0]), *halves[1:], weights)
 
 
 def to_frame(core, sums):
@@ -534,23 +548,22 @@
                 line = jnp.where(core == 0, sums[batch][c], sums[1 - batch][c])[tile : tile + 1]
                 lines.append(jnp.where(keep, line, 0.0))
         spread = ones_where(iota((256, 128), 0) // 8 + 32 * tile == iota((256, 128), 1))
-        for piece in parts_of(jnp.concatenate(lines, axis=0), 3):
-            picture += nn_dot(piece, spread)
+        stacked = nn_dot(jnp.concatenate(parts_of(jnp.concatenate(lines, axis=0), 3), axis=0), spread)
+        picture += stacked[:64] + stacked[64:128] + stacked[128:]
     return jnp.concatenate([picture[:48], opacity(picture[48:])], axis=0).reshape(4, 16, 128)
 
 
-def compose_z_kernel(pos_ref, col_ref, row_ref, first_ref, second_ref, out_ref):
-    here = iota((LOCAL, LOCAL), 0)
-    there = iota((LOCAL, LOCAL), 1)
-    col = jnp.concatenate([col_ref[...], col_ref[...]], axis=1)
-    ahead = ones_where((col < row_ref[0:1, :]) & (here % 4 == there % 4))
+def compose_z_kernel(pos_ref, ahead_ref, first_ref, second_ref, third_ref, out_ref):
+    ahead = ahead_ref[...]
     group = ones_where(iota((8, LOCAL), 0) == iota((8, LOCAL), 1) % 4)
     sums = []
-    for tile_ref in (first_ref, second_ref):
-        depth = tile_ref[3].reshape(256, LOCAL)
+    first = [first_ref[c] for c in range(4)]
+    second = [jnp.concatenate([second_ref[c], third_ref[c]], axis=2) for c in range(4)]
+    for tile in (first, second):
+        depth = tile[3].reshape(256, LOCAL)
         pieces = parts_of(depth, 3)
         through = jnp.exp(-sum(nn_dot(piece, ahead) for piece in pieces))
-        values = [parts_of(tile_ref[c].reshape(256, LOCAL) * through, 3) for c in range(3)] + [pieces]
+        values = [parts_of(tile[c].reshape(256, LOCAL) * through, 3) for c in range(3)] + [pieces]
         sums.append([sum(nt_dot(group, piece) for piece in pieces) for pieces in values])
     out_ref[...] = to_frame(pos_ref[2], sums)
 
@@ -558,7 +571,7 @@
 FRAME = jax.ShapeDtypeStruct((4, 16, 128), F32)
 
 
-def compose_z(pos, col, row, first, second):
+def compose_z(pos, ahead, *tiles):
     return pl.pallas_call(
         compose_z_kernel,
         out_shape=FRAME,
@@ -567,22 +580,20 @@
         compiler_params=params(),
         cost_estimate=pl.CostEstimate(flops=10**9, bytes_accessed=4 * 10**6, transcendentals=10**5),
         name="compose_z",
-    )(pos, col, row, first, second)
-
-
-def compose_x_kernel(last, pos_ref, col_ref, row_ref, tile_ref, *refs):
-    here = iota((LOCAL, LOCAL), 0)
-    there = iota((LOCAL, LOCAL), 1)
-    col = jnp.concatenate([col_ref[...], col_ref[...]], axis=1)
-    ahead = ones_where((row_ref[0:1, :] < col) & (here // 4 % 4 == there // 4 % 4))
-    group = ones_where(iota((8, LOCAL), 0) == iota((8, LOCAL), 1) // 4 % 4)
+    )(pos, ahead, *tiles)
+
+
+def compose_x_kernel(last, pos_ref, ahead_ref, tile_ref, *refs):
+    ahead = ahead_ref[...]
     codes = [tile_ref[:, c * 256 : c * 256 + 256].astype(I32).astype(F32) for c in range(4)]
     depth = jnp.exp2(codes[3] * (LOG_REACH / TOP) + LOG_MID)
     pieces = parts_of(depth, 3)
     through = jnp.exp(-sum(nn_dot(ahead, piece) for piece in pieces))
     scale = (0.5 * opacity(depth)) * through
-    values = [parts_of(scale + scale * (codes[c] * (1.0 / TOP)), 3) for c in range(3)] + [pieces]
-    sums = [sum(nn_dot(group, piece) for piece in pieces) for pieces in values]
+    values = [scale + scale * (codes[c] * (1.0 / TOP)) for c in range(3)] + [depth]
+    group = ones_where(iota((8, 48), 0) == iota((8, 48), 1) % 16 // 4)
+    folded = [jnp.sum(value.reshape(16, 16, 256), axis=0) for value in values]
+    sums = [nn_dot(group, jnp.concatenate(parts_of(fold, 3), axis=0)) for fold in folded]
     if last:
         earlier_ref, out_ref = refs
         earlier = [earlier_ref[:, c * 256 : c * 256 + 256] for c in range(4)]
@@ -593,17 +604,17 @@
             out_ref[:, c * 256 : c * 256 + 256] = sums[c]
 
 
-def compose_x(pos, col, row, tiles, *earlier):
+def compose_x(pos, ahead, tiles, *earlier):
     return pl.pallas_call(
         functools.partial(compose_x_kernel, len(earlier) > 0),
         out_shape=FRAME if earlier else jax.ShapeDtypeStruct((8, 1024), F32),
         in_specs=[pl.BlockSpec(memory_space=pltpu.SMEM)]
-        + [pl.BlockSpec(memory_space=pltpu.VMEM)] * (3 + len(earlier)),
+        + [pl.BlockSpec(memory_space=pltpu.VMEM)] * (2 + len(earlier)),
         out_specs=pl.BlockSpec(memory_space=pltpu.VMEM),
         compiler_params=params(),
         cost_estimate=pl.CostEstimate(flops=10**9, bytes_accessed=10**6, transcendentals=10**5),
         name="compose_x",
-    )(pos, col, row, tiles, *earlier)
+    )(pos, ahead, tiles, *earlier)
 
 
 def swap_cores(values):
@@ -631,46 +642,50 @@
         return jnp.stack([plane, z, core, turn]).astype(I32)
 
     start = position(jnp.int32(-1))
+    cell_row = lax.dynamic_slice_in_dim(brick_cell, chip * LOCAL, LOCAL).reshape(1, LOCAL)
+    weights = [plane_weights(0), plane_weights(1)]
+    other = swap_cores(bricks)
+
+    outbox = pack(start, plan_slots(start, cell_row), bricks, other)
+    outbox, brick_cell, assignment, depth_rank = lax.optimization_barrier((outbox, brick_cell, assignment, depth_rank))
+    inbox = send_bricks(outbox)
     cell = brick_cell.reshape(CHIPS, LOCAL)
-    cell_row = lax.dynamic_slice_in_dim(brick_cell, chip * LOCAL, LOCAL).reshape(1, LOCAL)
     major = assignment.reshape(CHIPS, LOCAL) * 16384
     key_z = major + depth_rank[0].reshape(CHIPS, LOCAL)
     key_x = major + depth_rank[1].reshape(CHIPS, LOCAL)
-    weights = [plane_weights(0), plane_weights(1)]
-    other = swap_cores(split_halves(start, bricks))
-
-    inbox = send_bricks(pack(start, cell_row, bricks, other))
-    place, relay_place, handing, most = index_maps(start, cell)
+    place, relay_place, handing, most, left = index_maps(start, cell)
     keys = order_keys(start, cell, key_z, key_x)
     handing, keys = lax.optimization_barrier((handing, keys))
     cells = unpack(place, relay_place, inbox, forward(handing, inbox))
 
     def frames_of(cells):
         other_half = swap_cores(cells)
-        tile_x, first_z = render(start, transfer, weights[0], cells)
+        tile_x, first_z = render(("xz", "xz"), 0, start, transfer, weights[0], cells)
         landed = [send_tiles(tile_x)]
-        tile_x, later_z = render(start, transfer, weights[1], cells, other_half)
+        tile_x, near_z = render(("xz", "x"), 0, start, transfer, weights[1], cells, other_half)
+        cells, tile_x, landed[0] = lax.optimization_barrier((cells, tile_x, landed[0]))
         landed.append(send_tiles(tile_x))
-        kz_col, kz_row, kx_col, kx_row = keys
-        frame_z = compose_z(start, kz_col, kz_row, first_z, later_z)
-        first_x = compose_x(start, kx_col, kx_row, landed[0])
-        return frame_z, compose_x(start, kx_col, kx_row, landed[1], first_x)
+        (far_z,) = render(("z",), 1, start, transfer, weights[1], cells, other_half)
+        ahead_z, ahead_x = keys
+        frame_z = compose_z(start, ahead_z, first_z, near_z, far_z)
+        first_x = compose_x(start, ahead_x, landed[0])
+        return frame_z, compose_x(start, ahead_x, landed[1], first_x)
 
     def in_rounds(carry):
-        rounds = (most[0] + CAP - 1) // CAP
+        rounds = (most.reshape(()) + CAP - 1) // CAP
 
         def next_round(carry):
             turn, cells = carry
             pos = position(turn)
             place = index_maps(pos, cell)[0]
-            inbox = send_bricks(pack(pos, cell_row, bricks, other))
+            inbox = send_bricks(pack(pos, plan_slots(pos, cell_row), bricks, other))
             return turn + 1, cells + unpack(place, relay_place, inbox, jnp.zeros((GROUP * BACK, HALF), BF16))
 
         nothing = (jnp.int32(0), jnp.zeros((LOCAL, HALF), BF16))
         _, cells = lax.while_loop(lambda carry: carry[0] < rounds, next_round, nothing)
         return (jnp.zeros_like(carry[0]),) + frames_of(cells)
 
-    carry = (most[1],) + frames_of(cells)
+    carry = (left.reshape(()),) + frames_of(cells)
     return lax.while_loop(lambda carry: carry[0] > 0, in_rounds, carry)[1:]
 
 

time: 124 us -> 119 us (0.960)
  waiting for transfers between devices: 17 us -> 11 us
  Pallas kernels: 66.8 us -> 70.2 us
  local copies, waits for them, and re-layouts: 4.58 us -> 1.62 us
    all_to_all x2, waiting for transfers between devices: 6.47 us -> 0.01 us  [send_tiles(): lax.all_to_all(tiles.reshape(16, 16, 1024), PLANE, split_axis=0, concat_a...]
    pallas_call x6 -> x7, Pallas kernels: 48.6 us -> 52.6 us  [the longest x3 37.6 us: render(): pl.pallas_call(functools.partial(render_kernel, views, len(halves)), grid...]
  transfers between devices with their start and end apart: 5 -> 5, of which waited for: 2 -> 2; matrix products, arithmetic and copies ran while one was open for 3% -> 1% of each run, Pallas kernels for 45% -> 53%
where the time goes in v3:
time: 119 us; the launch traced here: 118 us
  Pallas kernels  70.2 us (59%)
  starting transfers between devices  22.7 us (19%)
  waiting for transfers between devices  11 us (9%)
  blocking collectives  10.2 us (9%)
  local copies, waits for them, and re-layouts  1.62 us (1%)
    pallas_call x3, Pallas kernels, render(): pl.pallas_call(functools.partial(render_kernel, views, len(halves)), grid...  37.6 us
    all_to_all x1, starting transfers between devices, send_bricks(): lax.all_to_all(outbox.reshape(CHIPS, CAP, lanes), CHIP, split_axis=0, con...  11.5 us
    all_to_all x2, starting transfers between devices, send_tiles(): lax.all_to_all(tiles.reshape(16, 16, 1024), PLANE, split_axis=0, concat_a...  11 us
    pallas_call x1, Pallas kernels, index_maps(): pl.pallas_call(index_kernel, out_shape=(pltpu.HBM((LOCAL, CHIPS * CAP), B...  10.8 us
    all_to_all x1, waiting for transfers between devices, send_bricks(): lax.all_to_all(outbox.reshape(CHIPS, CAP, lanes), CHIP, split_axis=0, con...  10.7 us
    all_to_all x1, blocking collectives, forward(): lax.all_to_all(handed.reshape(GROUP, BACK, HALF), NEAR, split_axis=0, con...  10.2 us
    pallas_call x1, Pallas kernels, order_keys(): pl.pallas_call(key_kernel, out_shape=(ahead, ahead), in_specs=[pl.BlockSp...  8.38 us
    pallas_call x2, Pallas kernels, compose_x(): pl.pallas_call(functools.partial(compose_x_kernel, len(earlier) > 0), out...  3.34 us
  transfers between devices with their start and end apart: 5, of which 2 were waited for; matrix products, arithmetic and copies ran while one was open for 1% of the time, Pallas kernels for 53%

profile of v3, /device:TPU:0, one launch (start us, length us, event | category | flops | bytes accessed | tf_op | source)
XLA Modules:
  0.0 117.7 jit_solution(6465259153671578958)
XLA Ops:
  0.6 0.0 copy-start.13
  0.6 0.1 collective-permute-start.1
  0.7 0.8 dynamic_slice.3
  1.6 0.1 pad_add_fusion.1.pos_ref
  1.7 1.5 %plan_slots.2.slot_ref = s32[1,256]{1,0:T(1,128)S(1)} custom-call(s32[4]{0:T(128)S(1)} %pad_add_fusion.1.pos_ref, s32[1,256]{1,0:T(1,128)S(1)} %bitcast.51), custom_call_target="tpu_custom_call" | custom-call | flops 1000000000 | bytes 1000000 | tf_op jit(solution)/shard_map/plan_slots/pallas_call | solution.py:166
  3.2 0.0 copy-start.15
  3.2 0.0 copy-start.17
  3.2 0.0 copy-start.16
  3.2 0.4 collective-permute-done.1.other_ref
  3.6 0.0 copy-done.13
  3.6 2.4 %pack_outbox.2 = bf16[512,2048]{1,0:T(8,128)(2,1)} custom-call(s32[4]{0:T(128)S(1)} %pad_add_fusion.1.pos_ref, s32[1,256]{1,0:T(1,128)S(1)} %plan_slots.2.slot_ref, bf16[128,4096]{1,0:T(8,128)(2,1)S(1)} %copy-done.13, bf16[128,4096]{1,0:T(8,128)(2,1)S(1)} %collective-permute-done.1.other_ref), custom_call_target="tpu_custom_call" | custom-call | tf_op jit(solution)/shard_map/pack_outbox/pallas_call | solution.py:199
  6.0 0.0 copy-done.14
  6.1 0.0 copy-done.15
  6.1 0.3 slice_reduce_fusion
  6.4 0.0 copy-done.17
  6.4 0.2 multiply_reduce_fusion
  6.7 0.0 copy-done.16
  6.7 11.5 %all-to-all-start.3 = ((bf16[64,8,2048]{2,1,0:T(8,128)(2,1)}), bf16[64,8,2048]{2,1,0:T(8,128)(2,1)S(1)}, u32[]{:S(2)}, u32[]{:S(2)}) async-start(bf16[64,8,2048]{2,1,0:T(8,128)(2,1)} %bitcast.48), calls=%async_computation.3 | async-start | bytes 4194304 | tf_op jit(solution)/shard_map/all_to_all | solution.py:626
  18.2 10.8 %index_maps.2 = (bf16[256,512]{1,0:T(8,128)(2,1)}, bf16[256,128]{1,0:T(8,128)(2,1)}, bf16[64,512]{1,0:T(8,128)(2,1)S(1)}, s32[1]{0:T(128)}, s32[1]{0:T(128)}) custom-call(s32[4]{0:T(128)S(1)} %pad_add_fusion.1.pos_ref, s32[64,256]{1,0:T(8,128)S(1)} %reshape.62.cell_ref), custom_call_target="tpu_custom_call" | custom-call | flops 10000000000 | bytes 1000000 | tf_op jit(solution)/shard_map/index_maps/pallas_call | solution.py:303
  29.0 8.4 %order_keys.1 = (bf16[256,256]{1,0:T(8,128)(2,1)S(1)}, bf16[256,256]{1,0:T(8,128)(2,1)S(1)}) custom-call(s32[4]{0:T(128)S(1)} %pad_add_fusion.1.pos_ref, s32[64,256]{1,0:T(8,128)S(1)} %reshape.62.cell_ref, s32[64,256]{1,0:T(8,128)S(1)} %get-tuple-element.322.key_z_ref, s32[64,256]{1,0:T(8,128)S(1)} %get-tuple-element.321.key_x_ref), custom_call_target="tpu_custom_call" | custom-call | flops 10000000000 | bytes 1000000 | tf_op jit(solution)/shard_map/order_keys/pallas_call | solution.py:365
  37.4 0.0 copy-start.1
  37.4 10.7 %all-to-all-done.3 = bf16[64,8,2048]{2,1,0:T(8,128)(2,1)S(1)} async-done(((bf16[64,8,2048]{2,1,0:T(8,128)(2,1)}), bf16[64,8,2048]{2,1,0:T(8,128)(2,1)S(1)}, u32[]{:S(2)}, u32[]{:S(2)}) %all-to-all-start.3) | async-done | bytes 2097184 | tf_op jit(solution)/shard_map/all_to_all | solution.py:626
  48.1 0.5 hand_on.1
  48.6 0.0 copy-start.4
  48.6 0.0 copy-start.20
  48.6 10.2 %all_to_all.38 = bf16[8,8,2048]{2,1,0:T(8,128)(2,1)S(1)} all-to-all(bf16[8,8,2048]{2,1,0:T(8,128)(2,1)S(1)} %bitcast.42), channel_id=1, replica_groups=mesh['y'=4,'x1'=2,'x0'=2,'z'=4,'c'=2] {'x0','z'}, dimensions={0} | all-to-all | bytes 524288 | tf_op jit(solution)/shard_map/all_to_all | solution.py:392
  58.8 0.0 copy-done.1
  58.8 2.6 %unpack_inbox.2.refs_0_ = bf16[256,2048]{1,0:T(8,128)(2,1)} custom-call(bf16[256,512]{1,0:T(8,128)(2,1)S(1)} %copy-done.1, bf16[256,128]{1,0:T(8,128)(2,1)} %get-tuple-element.459.relay_ref, bf16[512,2048]{1,0:T(8,128)(2,1)S(1)} %bitcast.38, bf16[64,2048]{1,0:T(8,128)(2,1)S(1)} %bitcast.41), custom_call_target="tpu_custom_call" | custom-call | flops 1000000000 | bytes 3000000 | tf_op jit(solution)/shard_map/unpack_inbox/pallas_call | solution.py:410
  61.4 0.0 copy-start.2
  61.4 0.1 collective-permute-start.2
  61.5 0.0 copy-done.4
  61.5 0.0 copy-done.20
  61.5 15.4 %render_xz_xz.2 = (s16[256,1024]{1,0:T(8,128)(2,1)}, f32[4,32,8,256]{3,2,1,0:T(8,128)}) custom-call(s32[4]{0:T(128)S(1)} %pad_add_fusion.1.pos_ref, f32[2,4]{1,0:T(2,128)S(1)} %copy-done.20, bf16[256,2048]{1,0:T(8,128)(2,1)} %unpack_inbox.2.refs_0_, bf16[2,256,128]{2,1,0:T(8,128)(2,1)S(1)} %copy-done.4), custom_call_target="tpu_custom_call" | custom-call | flops 10000000000 | bytes 10000000 | tf_op jit(solution)/shard_map/render_xz_xz/pallas_call | solution.py:524
  76.9 3.8 %all-to-all-start.5 = ((s16[16,16,1024]{2,1,0:T(8,128)(2,1)}), s16[16,16,1024]{2,1,0:T(8,128)(2,1)S(1)}, u32[]{:S(2)}, u32[]{:S(2)}) async-start(s16[16,16,1024]{2,1,0:T(8,128)(2,1)} %bitcast.50), calls=%async_computation.5 | async-start | bytes 1048576 | tf_op jit(solution)/shard_map/all_to_all | solution.py:631
  80.7 0.0 collective-permute-done.2.refs_1_
  80.7 0.0 copy-done.2
  80.7 14.8 %render_xz_x.2 = (s16[256,1024]{1,0:T(8,128)(2,1)}, f32[4,32,8,128]{3,2,1,0:T(8,128)}) custom-call(s32[4]{0:T(128)S(1)} %pad_add_fusion.1.pos_ref, f32[2,4]{1,0:T(2,128)S(1)} %copy-done.20, bf16[256,2048]{1,0:T(8,128)(2,1)} %unpack_inbox.2.refs_0_, bf16[256,2048]{1,0:T(8,128)(2,1)S(1)} %collective-permute-done.2.refs_1_, bf16[2,256,256]{2,1,0:T(8,128)(2,1)S(1)} %copy-done.2), custom_call_target="tpu_custom_call" | custom-call | flops 10000000000 | bytes 10000000 | tf_op jit(solution)/shard_map/render_xz_x/pallas_call | solution.py:524
  95.5 0.0 all-to-all-done.5
  95.6 7.2 %all-to-all-start.6 = ((s16[16,16,1024]{2,1,0:T(8,128)(2,1)}), s16[16,16,1024]{2,1,0:T(8,128)(2,1)S(1)}, u32[]{:S(2)}, u32[]{:S(2)}) async-start(s16[16,16,1024]{2,1,0:T(8,128)(2,1)} %bitcast.49), calls=%async_computation.6 | async-start | bytes 1048576 | tf_op jit(solution)/shard_map/all_to_all | solution.py:631
  102.8 7.5 %render_z.2.third_ref = f32[4,32,8,128]{3,2,1,0:T(8,128)} custom-call(s32[4]{0:T(128)S(1)} %pad_add_fusion.1.pos_ref, f32[2,4]{1,0:T(2,128)S(1)} %copy-done.20, bf16[256,2048]{1,0:T(8,128)(2,1)} %unpack_inbox.2.refs_0_, bf16[256,2048]{1,0:T(8,128)(2,1)S(1)} %collective-permute-done.2.refs_1_, bf16[2,256,256]{2,1,0:T(8,128)(2,1)S(1)} %copy-done.2), custom_call_target="tpu_custom_call" | custom-call | flops 10000000000 | bytes 10000000 | tf_op jit(solution)/shard_map/render_z/pallas_call | solution.py:524
  110.2 1.2 compose_x.4.refs_0_
  111.4 0.1 copy-done.7
  111.5 0.1 copy-done.9
  111.6 0.2 copy-done.11
  111.7 3.0 %compose_z.2 = f32[4,16,128]{2,1,0:T(8,128)} custom-call(s32[4]{0:T(128)S(1)} %pad_add_fusion.1.pos_ref, bf16[256,256]{1,0:T(8,128)(2,1)S(1)} %get-tuple-element.462.ahead_ref, f32[4,32,8,256]{3,2,1,0:T(8,128)S(1)} %copy-done.7, f32[4,32,8,128]{3,2,1,0:T(8,128)S(1)} %copy-done.9, f32[4,32,8,128]{3,2,1,0:T(8,128)S(1)} %copy-done.11), custom_call_target="tpu_custom_call" | custom-call | flops 1000000000 | bytes 4000000 | tf_op jit(solution)/shard_map/compose_z/pallas_call | solution.py:575
  114.8 0.0 all-to-all-done.6
  114.8 2.2 %compose_x.5 = f32[4,16,128]{2,1,0:T(8,128)} custom-call(s32[4]{0:T(128)S(1)} %pad_add_fusion.1.pos_ref, bf16[256,256]{1,0:T(8,128)(2,1)S(1)} %get-tuple-element.463.ahead_ref, s16[256,1024]{1,0:T(8,128)(2,1)S(1)} %bitcast.44, f32[8,1024]{1,0:T(8,128)S(1)} %compose_x.4.refs_0_), custom_call_target="tpu_custom_call" | custom-call | flops 1000000000 | bytes 1000000 | tf_op jit(solution)/shard_map/compose_x/pallas_call | solution.py:608
  116.9 0.6 while.23
  (9 shorter events, 0.1 us)
Async XLA Ops:
  0.6 3.0 %copy-start.13 = (bf16[128,4096]{1,0:T(8,128)(2,1)S(1)}, bf16[128,4096]{1,0:T(8,128)(2,1)}, u32[]{:S(2)}) copy-start(bf16[128,4096]{1,0:T(8,128)(2,1)} %bricks_ref.1) | copy-start | bytes 3145732
  0.6 3.0 %collective-permute-start.1 = (bf16[128,4096]{1,0:T(8,128)(2,1)}, bf16[128,4096]{1,0:T(8,128)(2,1)S(1)}, u32[]{:S(2)}, u32[]{:S(2)}) collective-permute-start(bf16[128,4096]{1,0:T(8,128)(2,1)} %bricks_ref.1), channel_id=1, source_target_pairs={{0,1},{1,0},{2,3},{3,2},{4,5},{5,4},{6,7},{7,6},{8,9},{9,8},{10,11... | collective-permute-start | bytes 3145736 | tf_op jit(solution)/shard_map/ppermute | solution.py:621
  3.2 2.9 %copy-start.15 = (s32[2,16384]{1,0:T(2,128)S(1)}, s32[2,16384]{1,0:T(2,128)}, u32[]{:S(2)}) copy-start(s32[2,16384]{1,0:T(2,128)} %param.15) | copy-start | bytes 393220
  3.2 3.2 %copy-start.17 = (s32[16384,1]{0,1:T(1,128)S(1)}, s32[16384,1]{0,1:T(1,128)}, u32[]{:S(2)}) copy-start(s32[16384,1]{0,1:T(1,128)} %param.13) | copy-start | bytes 196612
  3.2 3.4 %copy-start.16 = (s32[16384]{0:T(1024)S(1)}, s32[16384]{0:T(1024)}, u32[]{:S(2)}) copy-start(s32[16384]{0:T(1024)} %param.14) | copy-start | bytes 196612
  3.6 2.4 %copy-start.14 = (bf16[128,4096]{1,0:T(8,128)(2,1)}, bf16[128,4096]{1,0:T(8,128)(2,1)S(1)}, u32[]{:S(2)}) copy-start(bf16[128,4096]{1,0:T(8,128)(2,1)S(1)} %collective-permute-done.1.other_ref) | copy-start | bytes 3145732
  6.7 41.4 %all-to-all-start.3 = ((bf16[64,8,2048]{2,1,0:T(8,128)(2,1)}), bf16[64,8,2048]{2,1,0:T(8,128)(2,1)S(1)}, u32[]{:S(2)}, u32[]{:S(2)}) async-start(bf16[64,8,2048]{2,1,0:T(8,128)(2,1)} %bitcast.48), calls=%async_computation.3 | async-start | bytes 4194304 | tf_op jit(solution)/shard_map/all_to_all | solution.py:626
  37.4 21.4 %copy-start.1 = (bf16[256,512]{1,0:T(8,128)(2,1)S(1)}, bf16[256,512]{1,0:T(8,128)(2,1)}, u32[]{:S(2)}) copy-start(bf16[256,512]{1,0:T(8,128)(2,1)} %get-tuple-element.187.place_ref) | copy-start | bytes 786436
  48.6 12.9 %copy-start.4 = (bf16[2,256,128]{2,1,0:T(8,128)(2,1)S(1)}, bf16[2,256,128]{2,1,0:T(8,128)(2,1)}, u32[]{:S(2)}) copy-start(bf16[2,256,128]{2,1,0:T(8,128)(2,1)} %constant.66.clone.refs_1_) | copy-start | bytes 393220
  48.6 12.9 %copy-start.20 = (f32[2,4]{1,0:T(2,128)S(1)}, f32[2,4]{1,0:T(2,128)}, u32[]{:S(2)}) copy-start(f32[2,4]{1,0:T(2,128)} %transfer_ref.5) | copy-start | bytes 100
  61.4 19.3 %copy-start.2 = (bf16[2,256,256]{2,1,0:T(8,128)(2,1)S(1)}, bf16[2,256,256]{2,1,0:T(8,128)(2,1)}, u32[]{:S(2)}) copy-start(bf16[2,256,256]{2,1,0:T(8,128)(2,1)} %constant.67.clone.refs_2_) | copy-start | bytes 786436
  61.4 19.3 %collective-permute-start.2 = (bf16[256,2048]{1,0:T(8,128)(2,1)}, bf16[256,2048]{1,0:T(8,128)(2,1)S(1)}, u32[]{:S(2)}, u32[]{:S(2)}) collective-permute-start(bf16[256,2048]{1,0:T(8,128)(2,1)} %unpack_inbox.2.refs_0_), channel_id=1, source_target_pairs={{0,1},{1,0},{2,3},{3,2},{4,5},{5,4},{6,7},{7,6},{8,9},{9,8},{10,11... | collective-permute-start | bytes 3145736 | tf_op jit(solution)/shard_map/ppermute | solution.py:621
  76.9 18.6 %all-to-all-start.5 = ((s16[16,16,1024]{2,1,0:T(8,128)(2,1)}), s16[16,16,1024]{2,1,0:T(8,128)(2,1)S(1)}, u32[]{:S(2)}, u32[]{:S(2)}) async-start(s16[16,16,1024]{2,1,0:T(8,128)(2,1)} %bitcast.50), calls=%async_computation.5 | async-start | bytes 1048576 | tf_op jit(solution)/shard_map/all_to_all | solution.py:631
  95.6 19.2 %all-to-all-start.6 = ((s16[16,16,1024]{2,1,0:T(8,128)(2,1)}), s16[16,16,1024]{2,1,0:T(8,128)(2,1)S(1)}, u32[]{:S(2)}, u32[]{:S(2)}) async-start(s16[16,16,1024]{2,1,0:T(8,128)(2,1)} %bitcast.49), calls=%async_computation.6 | async-start | bytes 1048576 | tf_op jit(solution)/shard_map/all_to_all | solution.py:631
  110.2 1.2 %copy-start.7 = (f32[4,32,8,256]{3,2,1,0:T(8,128)S(1)}, f32[4,32,8,256]{3,2,1,0:T(8,128)}, u32[]{:S(2)}) copy-start(f32[4,32,8,256]{3,2,1,0:T(8,128)} %get-tuple-element.191.first_ref) | copy-start | bytes 3145732
  110.2 1.4 %copy-start.9 = (f32[4,32,8,128]{3,2,1,0:T(8,128)S(1)}, f32[4,32,8,128]{3,2,1,0:T(8,128)}, u32[]{:S(2)}) copy-start(f32[4,32,8,128]{3,2,1,0:T(8,128)} %get-tuple-element.192.second_ref) | copy-start | bytes 1572868
  110.2 1.5 %copy-start.11 = (f32[4,32,8,128]{3,2,1,0:T(8,128)S(1)}, f32[4,32,8,128]{3,2,1,0:T(8,128)}, u32[]{:S(2)}) copy-start(f32[4,32,8,128]{3,2,1,0:T(8,128)} %render_z.2.third_ref) | copy-start | bytes 1572868

commit v4 on v3

--- a/solution.py
+++ b/solution.py
@@ -498,42 +498,39 @@
             tile_x_ref[:, c * 256 : c * 256 + 256] = values[c].reshape(256, 128).T.astype(I32).astype(jnp.int16)
 
 
-def render_kernel(views, count, pos_ref, transfer_ref, *refs):
-    halves, weights_ref, rest = refs[:count], refs[count], list(refs[count + 1 :])
-    tile_x_ref = rest.pop(0) if "x" in views[0] else None
-    tile_z_ref, plane_ref, state_ref = rest
-    for g, wanted in enumerate(views):
-        if len(set(views)) == 1:
-            if g == 0:
-                render_group(wanted, pos_ref, transfer_ref, halves, weights_ref, tile_x_ref, tile_z_ref, plane_ref, state_ref)
-        else:
-
-            @pl.when(pl.program_id(0) == g)
-            def _():
-                render_group(wanted, pos_ref, transfer_ref, halves, weights_ref, tile_x_ref, tile_z_ref, plane_ref, state_ref)
-
-
-def render(views, first, pos, transfer, weights, *halves):
+def render_kernel(views, count, kept, pos_ref, transfer_ref, *refs):
+    halves, weights_ref, rest = refs[:count], refs[count], list(refs[count + 1 + kept :])
+    tile_x_ref = rest.pop(0) if "x" in views else None
+    tile_z_ref = rest.pop(0) if "z" in views else None
+    plane_ref, state_ref = rest
+    render_group(views, pos_ref, transfer_ref, halves, weights_ref, tile_x_ref, tile_z_ref, plane_ref, state_ref)
+
+
+def render(views, pos, transfer, weights, *halves, before=()):
     smem = pl.BlockSpec(memory_space=pltpu.SMEM)
-    groups_z = sum("z" in wanted for wanted in views)
-    out_specs = [pl.BlockSpec((4, 32, 8, 128), lambda g: (0, 0, 0, jnp.minimum(g, groups_z - 1)))]
-    out_shape = [pltpu.HBM((4, 32, 8, 128 * groups_z), F32)]
-    if "x" in views[0]:
-        out_specs.insert(0, pl.BlockSpec((128, 1024), lambda g: (g, 0)))
-        out_shape.insert(0, pltpu.HBM((128 * len(views), 1024), jnp.int16))
-    return pl.pallas_call(
-        functools.partial(render_kernel, views, len(halves)),
-        grid=(len(views),),
+    batch = len(before)
+    out_specs, out_shape = [], []
+    if "x" in views:
+        out_specs.append(pl.BlockSpec((128, 1024), lambda g: (g, batch)))
+        out_shape.append(pltpu.HBM((LOCAL, 2048), jnp.int16))
+    if "z" in views:
+        out_specs.append(pl.BlockSpec((4, 32, 8, 128), lambda g: (0, 0, 0, g)))
+        out_shape.append(pltpu.HBM((4, 32, 8, LOCAL), F32))
+    return pl.pallas_call(
+        functools.partial(render_kernel, views, len(halves), batch),
+        grid=(2,),
         in_specs=[smem, smem]
-        + [pl.BlockSpec((128, HALF), lambda g: (g + first, 0))] * len(halves)
-        + [pl.BlockSpec(weights.shape, lambda g: (0, 0, 0))],
+        + [pl.BlockSpec((128, HALF), lambda g: (g, 0))] * len(halves)
+        + [pl.BlockSpec(weights.shape, lambda g: (0, 0, 0))]
+        + [pl.BlockSpec(memory_space=pl.ANY)] * batch,
         out_specs=out_specs,
+        input_output_aliases={3 + len(halves): 0} if before else {},
         scratch_shapes=[pltpu.VMEM((EDGE, 32, 8, 128), F32), pltpu.VMEM((5, 32, 8, 128), F32)],
         out_shape=out_shape,
         compiler_params=params(semantics=("arbitrary",)),
         cost_estimate=pl.CostEstimate(flops=10**10, bytes_accessed=10**7, transcendentals=10**7),
-        name="render_" + "_".join(views),
-    )(pos, transfer, in_hbm(halves[0]), *halves[1:], weights)
+        name="render_" + views,
+    )(pos, transfer, in_hbm(halves[0]), *halves[1:], weights, *before)
 
 
 def to_frame(core, sums):
@@ -553,13 +550,11 @@
     return jnp.concatenate([picture[:48], opacity(picture[48:])], axis=0).reshape(4, 16, 128)
 
 
-def compose_z_kernel(pos_ref, ahead_ref, first_ref, second_ref, third_ref, out_ref):
+def compose_z_kernel(pos_ref, ahead_ref, first_ref, second_ref, out_ref):
     ahead = ahead_ref[...]
     group = ones_where(iota((8, LOCAL), 0) == iota((8, LOCAL), 1) % 4)
     sums = []
-    first = [first_ref[c] for c in range(4)]
-    second = [jnp.concatenate([second_ref[c], third_ref[c]], axis=2) for c in range(4)]
-    for tile in (first, second):
+    for tile in (first_ref, second_ref):
         depth = tile[3].reshape(256, LOCAL)
         pieces = parts_of(depth, 3)
         through = jnp.exp(-sum(nn_dot(piece, ahead) for piece in pieces))
@@ -575,7 +570,7 @@
     return pl.pallas_call(
         compose_z_kernel,
         out_shape=FRAME,
-        in_specs=[pl.BlockSpec(memory_space=pltpu.SMEM)] + [pl.BlockSpec(memory_space=pltpu.VMEM)] * 4,
+        in_specs=[pl.BlockSpec(memory_space=pltpu.SMEM)] + [pl.BlockSpec(memory_space=pltpu.VMEM)] * 3,
         out_specs=pl.BlockSpec(memory_space=pltpu.VMEM),
         compiler_params=params(),
         cost_estimate=pl.CostEstimate(flops=10**9, bytes_accessed=4 * 10**6, transcendentals=10**5),
@@ -583,38 +578,34 @@
     )(pos, ahead, *tiles)
 
 
-def compose_x_kernel(last, pos_ref, ahead_ref, tile_ref, *refs):
+def compose_x_kernel(pos_ref, ahead_ref, tile_ref, out_ref):
     ahead = ahead_ref[...]
-    codes = [tile_ref[:, c * 256 : c * 256 + 256].astype(I32).astype(F32) for c in range(4)]
-    depth = jnp.exp2(codes[3] * (LOG_REACH / TOP) + LOG_MID)
-    pieces = parts_of(depth, 3)
-    through = jnp.exp(-sum(nn_dot(ahead, piece) for piece in pieces))
-    scale = (0.5 * opacity(depth)) * through
-    values = [scale + scale * (codes[c] * (1.0 / TOP)) for c in range(3)] + [depth]
     group = ones_where(iota((8, 48), 0) == iota((8, 48), 1) % 16 // 4)
-    folded = [jnp.sum(value.reshape(16, 16, 256), axis=0) for value in values]
-    sums = [nn_dot(group, jnp.concatenate(parts_of(fold, 3), axis=0)) for fold in folded]
-    if last:
-        earlier_ref, out_ref = refs
-        earlier = [earlier_ref[:, c * 256 : c * 256 + 256] for c in range(4)]
-        out_ref[...] = to_frame(pos_ref[2], [earlier, sums])
-    else:
-        (out_ref,) = refs
+    sums = []
+    for batch in range(2):
+        codes = []
         for c in range(4):
-            out_ref[:, c * 256 : c * 256 + 256] = sums[c]
-
-
-def compose_x(pos, ahead, tiles, *earlier):
-    return pl.pallas_call(
-        functools.partial(compose_x_kernel, len(earlier) > 0),
-        out_shape=FRAME if earlier else jax.ShapeDtypeStruct((8, 1024), F32),
-        in_specs=[pl.BlockSpec(memory_space=pltpu.SMEM)]
-        + [pl.BlockSpec(memory_space=pltpu.VMEM)] * (2 + len(earlier)),
+            at = batch * 1024 + c * 256
+            codes.append(tile_ref[:, at : at + 256].astype(I32).astype(F32))
+        depth = jnp.exp2(codes[3] * (LOG_REACH / TOP) + LOG_MID)
+        through = jnp.exp(-sum(nn_dot(ahead, piece) for piece in parts_of(depth, 3)))
+        scale = (0.5 * opacity(depth)) * through
+        values = [scale + scale * (codes[c] * (1.0 / TOP)) for c in range(3)] + [depth]
+        folded = [jnp.sum(value.reshape(16, 16, 256), axis=0) for value in values]
+        sums.append([nn_dot(group, jnp.concatenate(parts_of(fold, 3), axis=0)) for fold in folded])
+    out_ref[...] = to_frame(pos_ref[2], sums)
+
+
+def compose_x(pos, ahead, tiles):
+    return pl.pallas_call(
+        compose_x_kernel,
+        out_shape=FRAME,
+        in_specs=[pl.BlockSpec(memory_space=pltpu.SMEM)] + [pl.BlockSpec(memory_space=pltpu.VMEM)] * 2,
         out_specs=pl.BlockSpec(memory_space=pltpu.VMEM),
         compiler_params=params(),
         cost_estimate=pl.CostEstimate(flops=10**9, bytes_accessed=10**6, transcendentals=10**5),
         name="compose_x",
-    )(pos, ahead, tiles, *earlier)
+    )(pos, ahead, tiles)
 
 
 def swap_cores(values):
@@ -628,8 +619,8 @@
 
 
 def send_tiles(tiles):
-    sent = lax.all_to_all(tiles.reshape(16, 16, 1024), PLANE, split_axis=0, concat_axis=0, tiled=True)
-    return sent.reshape(LOCAL, 1024)
+    sent = lax.all_to_all(tiles.reshape(16, 16, 2048), PLANE, split_axis=0, concat_axis=0, tiled=True)
+    return sent.reshape(LOCAL, 2048)
 
 
 def body(bricks, transfer, assignment, brick_cell, depth_rank):
@@ -660,16 +651,13 @@
 
     def frames_of(cells):
         other_half = swap_cores(cells)
-        tile_x, first_z = render(("xz", "xz"), 0, start, transfer, weights[0], cells)
-        landed = [send_tiles(tile_x)]
-        tile_x, near_z = render(("xz", "x"), 0, start, transfer, weights[1], cells, other_half)
-        cells, tile_x, landed[0] = lax.optimization_barrier((cells, tile_x, landed[0]))
-        landed.append(send_tiles(tile_x))
-        (far_z,) = render(("z",), 1, start, transfer, weights[1], cells, other_half)
+        tile_x, first_z = render("xz", start, transfer, weights[0], cells)
+        (tile_x,) = render("x", start, transfer, weights[1], cells, other_half, before=(tile_x,))
+        cells, tile_x = lax.optimization_barrier((cells, tile_x))
+        landed = send_tiles(tile_x)
+        (later_z,) = render("z", start, transfer, weights[1], cells, other_half)
         ahead_z, ahead_x = keys
-        frame_z = compose_z(start, ahead_z, first_z, near_z, far_z)
-        first_x = compose_x(start, ahead_x, landed[0])
-        return frame_z, compose_x(start, ahead_x, landed[1], first_x)
+        return compose_z(start, ahead_z, first_z, later_z), compose_x(start, ahead_x, landed)
 
     def in_rounds(carry):
         rounds = (most.reshape(()) + CAP - 1) // CAP

time: 119 us -> 118 us (level)
  starting transfers between devices: 22.7 us -> 15.5 us
  Pallas kernels: 70.2 us -> 74 us
  waiting for transfers between devices: 11 us -> 12.6 us
    all_to_all x2 -> x1, starting transfers between devices: 11 us -> 3.87 us  [send_tiles(): lax.all_to_all(tiles.reshape(16, 16, 2048), PLANE, split_axis=0, concat_a...]
    pallas_call x5 -> x4, Pallas kernels: 41 us -> 44.7 us  [the longest x3 42 us: render(): pl.pallas_call(functools.partial(render_kernel, views, len(halves), batch...]
    all_to_all x2 -> x1, waiting for transfers between devices: 0.01 us -> 1.43 us  [send_tiles(): lax.all_to_all(tiles.reshape(16, 16, 2048), PLANE, split_axis=0, concat_a...]
  transfers between devices with their start and end apart: 5 -> 4, of which waited for: 2 -> 3; matrix products, arithmetic and copies ran while one was open for 1% -> 1% of each run, Pallas kernels for 53% -> 45%
where the time goes in v4:
time: 118 us; the launch traced here: 117 us
  Pallas kernels  74 us (63%)
  starting transfers between devices  15.5 us (13%)
  waiting for transfers between devices  12.6 us (11%)
  blocking collectives  10.2 us (9%)
  local copies, waits for them, and re-layouts  2.43 us (2%)
    pallas_call x3, Pallas kernels, render(): pl.pallas_call(functools.partial(render_kernel, views, len(halves), batch...  42 us
    all_to_all x1, starting transfers between devices, send_bricks(): lax.all_to_all(outbox.reshape(CHIPS, CAP, lanes), CHIP, split_axis=0, con...  11.5 us
    pallas_call x1, Pallas kernels, index_maps(): pl.pallas_call(index_kernel, out_shape=(pltpu.HBM((LOCAL, CHIPS * CAP), B...  10.8 us
    all_to_all x1, waiting for transfers between devices, send_bricks(): lax.all_to_all(outbox.reshape(CHIPS, CAP, lanes), CHIP, split_axis=0, con...  10.6 us
    all_to_all x1, blocking collectives, forward(): lax.all_to_all(handed.reshape(GROUP, BACK, HALF), NEAR, split_axis=0, con...  10.2 us
    pallas_call x1, Pallas kernels, order_keys(): pl.pallas_call(key_kernel, out_shape=(ahead, ahead), in_specs=[pl.BlockSp...  8.38 us
    all_to_all x1, starting transfers between devices, send_tiles(): lax.all_to_all(tiles.reshape(16, 16, 2048), PLANE, split_axis=0, concat_a...  3.87 us
    pallas_call x1, Pallas kernels, pack(): pl.pallas_call(pack_kernel, in_specs=[pl.BlockSpec(memory_space=pltpu.SME...  3.42 us
  transfers between devices with their start and end apart: 4, of which 3 were waited for; matrix products, arithmetic and copies ran while one was open for 1% of the time, Pallas kernels for 45%

profile of v4, /device:TPU:0, one launch (start us, length us, event | category | flops | bytes accessed | tf_op | source)
XLA Modules:
  0.0 116.8 jit_solution(15122138617399820888)
XLA Ops:
  0.6 0.1 collective-permute-start.1
  0.7 0.8 dynamic_slice.3
  1.5 0.1 pad_add_fusion.1.pos_ref
  1.6 1.5 %plan_slots.2.slot_ref = s32[1,256]{1,0:T(1,128)S(1)} custom-call(s32[4]{0:T(128)S(1)} %pad_add_fusion.1.pos_ref, s32[1,256]{1,0:T(1,128)S(1)} %bitcast.43), custom_call_target="tpu_custom_call" | custom-call | flops 1000000000 | bytes 1000000 | tf_op jit(solution)/shard_map/plan_slots/pallas_call | solution.py:166
  3.1 0.0 copy-start.13
  3.1 0.0 copy-start.15
  3.1 0.0 copy-start.14
  3.2 0.6 collective-permute-done.1.other_ref
  3.7 3.4 %pack_outbox.2 = bf16[512,2048]{1,0:T(8,128)(2,1)} custom-call(s32[4]{0:T(128)S(1)} %pad_add_fusion.1.pos_ref, s32[1,256]{1,0:T(1,128)S(1)} %plan_slots.2.slot_ref, bf16[128,4096]{1,0:T(8,128)(2,1)} %bricks_ref.1, bf16[128,4096]{1,0:T(8,128)(2,1)} %collective-permute-done.1.other_ref), custom_call_target="tpu_custom_call" | custom-call | tf_op jit(solution)/shard_map/pack_outbox/pallas_call | solution.py:199
  7.1 0.0 copy-done.13
  7.1 0.3 slice_reduce_fusion
  7.5 0.0 copy-done.15
  7.5 0.2 multiply_reduce_fusion
  7.7 0.0 copy-done.14
  7.8 11.5 %all-to-all-start.2 = ((bf16[64,8,2048]{2,1,0:T(8,128)(2,1)}), bf16[64,8,2048]{2,1,0:T(8,128)(2,1)S(1)}, u32[]{:S(2)}, u32[]{:S(2)}) async-start(bf16[64,8,2048]{2,1,0:T(8,128)(2,1)} %bitcast.41), calls=%async_computation.2 | async-start | bytes 4194304 | tf_op jit(solution)/shard_map/all_to_all | solution.py:617
  19.3 10.8 %index_maps.2 = (bf16[256,512]{1,0:T(8,128)(2,1)}, bf16[256,128]{1,0:T(8,128)(2,1)}, bf16[64,512]{1,0:T(8,128)(2,1)S(1)}, s32[1]{0:T(128)}, s32[1]{0:T(128)}) custom-call(s32[4]{0:T(128)S(1)} %pad_add_fusion.1.pos_ref, s32[64,256]{1,0:T(8,128)S(1)} %reshape.50.cell_ref), custom_call_target="tpu_custom_call" | custom-call | flops 10000000000 | bytes 1000000 | tf_op jit(solution)/shard_map/index_maps/pallas_call | solution.py:303
  30.2 8.4 %order_keys.1 = (bf16[256,256]{1,0:T(8,128)(2,1)S(1)}, bf16[256,256]{1,0:T(8,128)(2,1)S(1)}) custom-call(s32[4]{0:T(128)S(1)} %pad_add_fusion.1.pos_ref, s32[64,256]{1,0:T(8,128)S(1)} %reshape.50.cell_ref, s32[64,256]{1,0:T(8,128)S(1)} %get-tuple-element.307.key_z_ref, s32[64,256]{1,0:T(8,128)S(1)} %get-tuple-element.306.key_x_ref), custom_call_target="tpu_custom_call" | custom-call | flops 10000000000 | bytes 1000000 | tf_op jit(solution)/shard_map/order_keys/pallas_call | solution.py:365
  38.5 0.0 copy-start.1
  38.6 0.0 copy-start.11
  38.6 10.6 %all-to-all-done.2 = bf16[64,8,2048]{2,1,0:T(8,128)(2,1)S(1)} async-done(((bf16[64,8,2048]{2,1,0:T(8,128)(2,1)}), bf16[64,8,2048]{2,1,0:T(8,128)(2,1)S(1)}, u32[]{:S(2)}, u32[]{:S(2)}) %all-to-all-start.2) | async-done | bytes 2097184 | tf_op jit(solution)/shard_map/all_to_all | solution.py:617
  49.2 0.5 hand_on.1
  49.7 0.0 copy-start.4
  49.7 0.0 copy-start.18
  49.7 10.2 %all_to_all.27 = bf16[8,8,2048]{2,1,0:T(8,128)(2,1)S(1)} all-to-all(bf16[8,8,2048]{2,1,0:T(8,128)(2,1)S(1)} %bitcast.37), channel_id=1, replica_groups=mesh['y'=4,'x1'=2,'x0'=2,'z'=4,'c'=2] {'x0','z'}, dimensions={0} | all-to-all | bytes 524288 | tf_op jit(solution)/shard_map/all_to_all | solution.py:392
  59.9 0.0 copy-done.1
  59.9 0.0 copy-done.11
  59.9 1.7 %unpack_inbox.2.refs_0_ = bf16[256,2048]{1,0:T(8,128)(2,1)} custom-call(bf16[256,512]{1,0:T(8,128)(2,1)S(1)} %copy-done.1, bf16[256,128]{1,0:T(8,128)(2,1)S(1)} %copy-done.11, bf16[512,2048]{1,0:T(8,128)(2,1)S(1)} %bitcast.35, bf16[64,2048]{1,0:T(8,128)(2,1)S(1)} %bitcast.36), custom_call_target="tpu_custom_call" | custom-call | flops 1000000000 | bytes 3000000 | tf_op jit(solution)/shard_map/unpack_inbox/pallas_call | solution.py:410
  61.6 0.0 copy-start.2
  61.7 0.1 collective-permute-start.2
  61.8 0.0 copy-done.4
  61.8 0.0 copy-done.18
  61.8 15.4 %render_xz.2 = (s16[256,2048]{1,0:T(8,128)(2,1)}, f32[4,32,8,256]{3,2,1,0:T(8,128)}) custom-call(s32[4]{0:T(128)S(1)} %pad_add_fusion.1.pos_ref, f32[2,4]{1,0:T(2,128)S(1)} %copy-done.18, bf16[256,2048]{1,0:T(8,128)(2,1)} %unpack_inbox.2.refs_0_, bf16[2,256,128]{2,1,0:T(8,128)(2,1)S(1)} %copy-done.4), custom_call_target="tpu_custom_call" | custom-call | flops 10000000000 | bytes 10000000 | tf_op jit(solution)/shard_map/render_xz/pallas_call | solution.py:519
  77.2 0.0 collective-permute-done.2.refs_1_
  77.2 0.0 copy-done.2
  77.2 13.4 %render_x.2 = s16[256,2048]{1,0:T(8,128)(2,1)} custom-call(s32[4]{0:T(128)S(1)} %pad_add_fusion.1.pos_ref, f32[2,4]{1,0:T(2,128)S(1)} %copy-done.18, bf16[256,2048]{1,0:T(8,128)(2,1)} %unpack_inbox.2.refs_0_, bf16[256,2048]{1,0:T(8,128)(2,1)S(1)} %collective-permute-done.2.refs_1_, ...), custom_call_target="tpu_custom_call", output_to_operand_aliasing={{}: (5, {})} | custom-call | flops 10000000000 | bytes 10000000 | tf_op jit(solution)/shard_map/render_x/pallas_call | solution.py:519
  90.5 3.9 %all-to-all-start.4 = ((s16[16,16,2048]{2,1,0:T(8,128)(2,1)}), s16[16,16,2048]{2,1,0:T(8,128)(2,1)S(1)}, u32[]{:S(2)}, u32[]{:S(2)}) async-start(s16[16,16,2048]{2,1,0:T(8,128)(2,1)} %bitcast.42), calls=%async_computation.4 | async-start | bytes 2097152 | tf_op jit(solution)/shard_map/all_to_all | solution.py:622
  94.4 0.0 copy-start.6
  94.4 13.3 %render_z.2.second_ref = f32[4,32,8,256]{3,2,1,0:T(8,128)} custom-call(s32[4]{0:T(128)S(1)} %pad_add_fusion.1.pos_ref, f32[2,4]{1,0:T(2,128)S(1)} %copy-done.18, bf16[256,2048]{1,0:T(8,128)(2,1)} %unpack_inbox.2.refs_0_, bf16[256,2048]{1,0:T(8,128)(2,1)S(1)} %collective-permute-done.2.refs_1_, bf16[2,256,256]{2,1,0:T(8,128)(2,1)S(1)} %copy-done.2), custom_call_target="tpu_custom_call" | custom-call | flops 10000000000 | bytes 10000000 | tf_op jit(solution)/shard_map/render_z/pallas_call | solution.py:519
  107.7 0.0 copy-done.6
  107.7 0.0 copy-start.8
  107.7 1.2 %copy-done.8 = f32[4,32,8,256]{3,2,1,0:T(8,128)S(1)} copy-done((f32[4,32,8,256]{3,2,1,0:T(8,128)S(1)}, f32[4,32,8,256]{3,2,1,0:T(8,128)}, u32[]{:S(2)}) %copy-start.8) | copy-done | bytes 1048600
  108.9 3.0 %compose_z.2 = f32[4,16,128]{2,1,0:T(8,128)} custom-call(s32[4]{0:T(128)S(1)} %pad_add_fusion.1.pos_ref, bf16[256,256]{1,0:T(8,128)(2,1)S(1)} %get-tuple-element.447.ahead_ref, f32[4,32,8,256]{3,2,1,0:T(8,128)S(1)} %copy-done.6, f32[4,32,8,256]{3,2,1,0:T(8,128)S(1)} %copy-done.8), custom_call_target="tpu_custom_call" | custom-call | flops 1000000000 | bytes 4000000 | tf_op jit(solution)/shard_map/compose_z/pallas_call | solution.py:570
  111.9 1.4 %all-to-all-done.4 = s16[16,16,2048]{2,1,0:T(8,128)(2,1)S(1)} async-done(((s16[16,16,2048]{2,1,0:T(8,128)(2,1)}), s16[16,16,2048]{2,1,0:T(8,128)(2,1)S(1)}, u32[]{:S(2)}, u32[]{:S(2)}) %all-to-all-start.4) | async-done | bytes 1048608 | tf_op jit(solution)/shard_map/all_to_all | solution.py:622
  113.4 2.7 %compose_x.2 = f32[4,16,128]{2,1,0:T(8,128)} custom-call(s32[4]{0:T(128)S(1)} %pad_add_fusion.1.pos_ref, bf16[256,256]{1,0:T(8,128)(2,1)S(1)} %get-tuple-element.448.ahead_ref, s16[256,2048]{1,0:T(8,128)(2,1)S(1)} %bitcast.38), custom_call_target="tpu_custom_call" | custom-call | flops 1000000000 | bytes 1000000 | tf_op jit(solution)/shard_map/compose_x/pallas_call | solution.py:600
  116.0 0.6 while.23
  (5 shorter events, 0.1 us)
Async XLA Ops:
  0.6 3.1 %collective-permute-start.1 = (bf16[128,4096]{1,0:T(8,128)(2,1)}, bf16[128,4096]{1,0:T(8,128)(2,1)}, u32[]{:S(2)}, u32[]{:S(2)}) collective-permute-start(bf16[128,4096]{1,0:T(8,128)(2,1)} %bricks_ref.1), channel_id=1, source_target_pairs={{0,1},{1,0},{2,3},{3,2},{4,5},{5,4},{6,7},{7,6},{8,9},{9,8},{10,11... | collective-permute-start | bytes 3145736 | tf_op jit(solution)/shard_map/ppermute | solution.py:612
  3.1 4.0 %copy-start.13 = (s32[2,16384]{1,0:T(2,128)S(1)}, s32[2,16384]{1,0:T(2,128)}, u32[]{:S(2)}) copy-start(s32[2,16384]{1,0:T(2,128)} %param.15) | copy-start | bytes 393220
  3.1 4.4 %copy-start.15 = (s32[16384,1]{0,1:T(1,128)S(1)}, s32[16384,1]{0,1:T(1,128)}, u32[]{:S(2)}) copy-start(s32[16384,1]{0,1:T(1,128)} %param.13) | copy-start | bytes 196612
  3.1 4.6 %copy-start.14 = (s32[16384]{0:T(1024)S(1)}, s32[16384]{0:T(1024)}, u32[]{:S(2)}) copy-start(s32[16384]{0:T(1024)} %param.14) | copy-start | bytes 196612
  7.8 41.4 %all-to-all-start.2 = ((bf16[64,8,2048]{2,1,0:T(8,128)(2,1)}), bf16[64,8,2048]{2,1,0:T(8,128)(2,1)S(1)}, u32[]{:S(2)}, u32[]{:S(2)}) async-start(bf16[64,8,2048]{2,1,0:T(8,128)(2,1)} %bitcast.41), calls=%async_computation.2 | async-start | bytes 4194304 | tf_op jit(solution)/shard_map/all_to_all | solution.py:617
  38.5 21.4 %copy-start.1 = (bf16[256,512]{1,0:T(8,128)(2,1)S(1)}, bf16[256,512]{1,0:T(8,128)(2,1)}, u32[]{:S(2)}) copy-start(bf16[256,512]{1,0:T(8,128)(2,1)} %get-tuple-element.181.place_ref) | copy-start | bytes 786436
  38.6 21.4 %copy-start.11 = (bf16[256,128]{1,0:T(8,128)(2,1)S(1)}, bf16[256,128]{1,0:T(8,128)(2,1)}, u32[]{:S(2)}) copy-start(bf16[256,128]{1,0:T(8,128)(2,1)} %get-tuple-element.444.relay_ref) | copy-start | bytes 196612
  49.7 12.1 %copy-start.4 = (bf16[2,256,128]{2,1,0:T(8,128)(2,1)S(1)}, bf16[2,256,128]{2,1,0:T(8,128)(2,1)}, u32[]{:S(2)}) copy-start(bf16[2,256,128]{2,1,0:T(8,128)(2,1)} %constant.66.clone.refs_1_) | copy-start | bytes 393220
  49.7 12.1 %copy-start.18 = (f32[2,4]{1,0:T(2,128)S(1)}, f32[2,4]{1,0:T(2,128)}, u32[]{:S(2)}) copy-start(f32[2,4]{1,0:T(2,128)} %transfer_ref.5) | copy-start | bytes 100
  61.6 15.5 %copy-start.2 = (bf16[2,256,256]{2,1,0:T(8,128)(2,1)S(1)}, bf16[2,256,256]{2,1,0:T(8,128)(2,1)}, u32[]{:S(2)}) copy-start(bf16[2,256,256]{2,1,0:T(8,128)(2,1)} %constant.67.clone.refs_2_) | copy-start | bytes 786436
  61.7 15.5 %collective-permute-start.2 = (bf16[256,2048]{1,0:T(8,128)(2,1)}, bf16[256,2048]{1,0:T(8,128)(2,1)S(1)}, u32[]{:S(2)}, u32[]{:S(2)}) collective-permute-start(bf16[256,2048]{1,0:T(8,128)(2,1)} %unpack_inbox.2.refs_0_), channel_id=1, source_target_pairs={{0,1},{1,0},{2,3},{3,2},{4,5},{5,4},{6,7},{7,6},{8,9},{9,8},{10,11... | collective-permute-start | bytes 3145736 | tf_op jit(solution)/shard_map/ppermute | solution.py:612
  90.5 22.8 %all-to-all-start.4 = ((s16[16,16,2048]{2,1,0:T(8,128)(2,1)}), s16[16,16,2048]{2,1,0:T(8,128)(2,1)S(1)}, u32[]{:S(2)}, u32[]{:S(2)}) async-start(s16[16,16,2048]{2,1,0:T(8,128)(2,1)} %bitcast.42), calls=%async_computation.4 | async-start | bytes 2097152 | tf_op jit(solution)/shard_map/all_to_all | solution.py:622
  94.4 13.3 %copy-start.6 = (f32[4,32,8,256]{3,2,1,0:T(8,128)S(1)}, f32[4,32,8,256]{3,2,1,0:T(8,128)}, u32[]{:S(2)}) copy-start(f32[4,32,8,256]{3,2,1,0:T(8,128)} %get-tuple-element.185.first_ref) | copy-start | bytes 3145732
  107.7 1.2 %copy-start.8 = (f32[4,32,8,256]{3,2,1,0:T(8,128)S(1)}, f32[4,32,8,256]{3,2,1,0:T(8,128)}, u32[]{:S(2)}) copy-start(f32[4,32,8,256]{3,2,1,0:T(8,128)} %render_z.2.second_ref) | copy-start | bytes 3145732

commit v5 on v4

--- a/solution.py
+++ b/solution.py
@@ -545,8 +545,8 @@
                 line = jnp.where(core == 0, sums[batch][c], sums[1 - batch][c])[tile : tile + 1]
                 lines.append(jnp.where(keep, line, 0.0))
         spread = ones_where(iota((256, 128), 0) // 8 + 32 * tile == iota((256, 128), 1))
-        stacked = nn_dot(jnp.concatenate(parts_of(jnp.concatenate(lines, axis=0), 3), axis=0), spread)
-        picture += stacked[:64] + stacked[64:128] + stacked[128:]
+        stacked = nn_dot(jnp.concatenate(parts_of(jnp.concatenate(lines, axis=0), 2), axis=0), spread)
+        picture += stacked[:64] + stacked[64:]
     return jnp.concatenate([picture[:48], opacity(picture[48:])], axis=0).reshape(4, 16, 128)
 
 
@@ -556,9 +556,9 @@
     sums = []
     for tile in (first_ref, second_ref):
         depth = tile[3].reshape(256, LOCAL)
-        pieces = parts_of(depth, 3)
+        pieces = parts_of(depth, 2)
         through = jnp.exp(-sum(nn_dot(piece, ahead) for piece in pieces))
-        values = [parts_of(tile[c].reshape(256, LOCAL) * through, 3) for c in range(3)] + [pieces]
+        values = [parts_of(tile[c].reshape(256, LOCAL) * through, 2) for c in range(3)] + [pieces]
         sums.append([sum(nt_dot(group, piece) for piece in pieces) for pieces in values])
     out_ref[...] = to_frame(pos_ref[2], sums)
 
@@ -580,7 +580,7 @@
 
 def compose_x_kernel(pos_ref, ahead_ref, tile_ref, out_ref):
     ahead = ahead_ref[...]
-    group = ones_where(iota((8, 48), 0) == iota((8, 48), 1) % 16 // 4)
+    group = ones_where(iota((8, 32), 0) == iota((8, 32), 1) % 16 // 4)
     sums = []
     for batch in range(2):
         codes = []
@@ -588,11 +588,11 @@
             at = batch * 1024 + c * 256
             codes.append(tile_ref[:, at : at + 256].astype(I32).astype(F32))
         depth = jnp.exp2(codes[3] * (LOG_REACH / TOP) + LOG_MID)
-        through = jnp.exp(-sum(nn_dot(ahead, piece) for piece in parts_of(depth, 3)))
+        through = jnp.exp(-sum(nn_dot(ahead, piece) for piece in parts_of(depth, 2)))
         scale = (0.5 * opacity(depth)) * through
         values = [scale + scale * (codes[c] * (1.0 / TOP)) for c in range(3)] + [depth]
         folded = [jnp.sum(value.reshape(16, 16, 256), axis=0) for value in values]
-        sums.append([nn_dot(group, jnp.concatenate(parts_of(fold, 3), axis=0)) for fold in folded])
+        sums.append([nn_dot(group, jnp.concatenate(parts_of(fold, 2), axis=0)) for fold in folded])
     out_ref[...] = to_frame(pos_ref[2], sums)
 
 

time: 118 us -> 118 us (level)
  no operation moved by 1% of the time
where the time goes in v5:
time: 118 us; the launch traced here: 117 us
  Pallas kernels  73.4 us (62%)
  starting transfers between devices  15.5 us (13%)
  waiting for transfers between devices  13.1 us (11%)
  blocking collectives  10.2 us (9%)
  local copies, waits for them, and re-layouts  2.43 us (2%)
    pallas_call x3, Pallas kernels, render(): pl.pallas_call(functools.partial(render_kernel, views, len(halves), batch...  42 us
    all_to_all x1, starting transfers between devices, send_bricks(): lax.all_to_all(outbox.reshape(CHIPS, CAP, lanes), CHIP, split_axis=0, con...  11.5 us
    pallas_call x1, Pallas kernels, index_maps(): pl.pallas_call(index_kernel, out_shape=(pltpu.HBM((LOCAL, CHIPS * CAP), B...  10.8 us
    all_to_all x1, waiting for transfers between devices, send_bricks(): lax.all_to_all(outbox.reshape(CHIPS, CAP, lanes), CHIP, split_axis=0, con...  10.6 us
    all_to_all x1, blocking collectives, forward(): lax.all_to_all(handed.reshape(GROUP, BACK, HALF), NEAR, split_axis=0, con...  10.2 us
    pallas_call x1, Pallas kernels, order_keys(): pl.pallas_call(key_kernel, out_shape=(ahead, ahead), in_specs=[pl.BlockSp...  8.38 us
    all_to_all x1, starting transfers between devices, send_tiles(): lax.all_to_all(tiles.reshape(16, 16, 2048), PLANE, split_axis=0, concat_a...  3.87 us
    pallas_call x1, Pallas kernels, pack(): pl.pallas_call(pack_kernel, in_specs=[pl.BlockSpec(memory_space=pltpu.SME...  3.42 us
  transfers between devices with their start and end apart: 4, of which 3 were waited for; matrix products, arithmetic and copies ran while one was open for 1% of the time, Pallas kernels for 45%

profile of v5, /device:TPU:0, one launch (start us, length us, event | category | flops | bytes accessed | tf_op | source)
XLA Modules:
  0.0 116.6 jit_solution(11797999208465664226)
XLA Ops:
  0.6 0.1 collective-permute-start.1
  0.7 0.8 dynamic_slice.3
  1.5 0.1 pad_add_fusion.1.pos_ref
  1.6 1.5 %plan_slots.2.slot_ref = s32[1,256]{1,0:T(1,128)S(1)} custom-call(s32[4]{0:T(128)S(1)} %pad_add_fusion.1.pos_ref, s32[1,256]{1,0:T(1,128)S(1)} %bitcast.43), custom_call_target="tpu_custom_call" | custom-call | flops 1000000000 | bytes 1000000 | tf_op jit(solution)/shard_map/plan_slots/pallas_call | solution.py:166
  3.1 0.0 copy-start.13
  3.1 0.0 copy-start.15
  3.1 0.0 copy-start.14
  3.2 0.6 collective-permute-done.1.other_ref
  3.7 3.4 %pack_outbox.2 = bf16[512,2048]{1,0:T(8,128)(2,1)} custom-call(s32[4]{0:T(128)S(1)} %pad_add_fusion.1.pos_ref, s32[1,256]{1,0:T(1,128)S(1)} %plan_slots.2.slot_ref, bf16[128,4096]{1,0:T(8,128)(2,1)} %bricks_ref.1, bf16[128,4096]{1,0:T(8,128)(2,1)} %collective-permute-done.1.other_ref), custom_call_target="tpu_custom_call" | custom-call | tf_op jit(solution)/shard_map/pack_outbox/pallas_call | solution.py:199
  7.1 0.0 copy-done.13
  7.1 0.3 slice_reduce_fusion
  7.5 0.0 copy-done.15
  7.5 0.2 multiply_reduce_fusion
  7.7 0.0 copy-done.14
  7.8 11.5 %all-to-all-start.2 = ((bf16[64,8,2048]{2,1,0:T(8,128)(2,1)}), bf16[64,8,2048]{2,1,0:T(8,128)(2,1)S(1)}, u32[]{:S(2)}, u32[]{:S(2)}) async-start(bf16[64,8,2048]{2,1,0:T(8,128)(2,1)} %bitcast.41), calls=%async_computation.2 | async-start | bytes 4194304 | tf_op jit(solution)/shard_map/all_to_all | solution.py:617
  19.3 10.8 %index_maps.2 = (bf16[256,512]{1,0:T(8,128)(2,1)}, bf16[256,128]{1,0:T(8,128)(2,1)}, bf16[64,512]{1,0:T(8,128)(2,1)S(1)}, s32[1]{0:T(128)}, s32[1]{0:T(128)}) custom-call(s32[4]{0:T(128)S(1)} %pad_add_fusion.1.pos_ref, s32[64,256]{1,0:T(8,128)S(1)} %reshape.50.cell_ref), custom_call_target="tpu_custom_call" | custom-call | flops 10000000000 | bytes 1000000 | tf_op jit(solution)/shard_map/index_maps/pallas_call | solution.py:303
  30.2 8.4 %order_keys.1 = (bf16[256,256]{1,0:T(8,128)(2,1)S(1)}, bf16[256,256]{1,0:T(8,128)(2,1)S(1)}) custom-call(s32[4]{0:T(128)S(1)} %pad_add_fusion.1.pos_ref, s32[64,256]{1,0:T(8,128)S(1)} %reshape.50.cell_ref, s32[64,256]{1,0:T(8,128)S(1)} %get-tuple-element.307.key_z_ref, s32[64,256]{1,0:T(8,128)S(1)} %get-tuple-element.306.key_x_ref), custom_call_target="tpu_custom_call" | custom-call | flops 10000000000 | bytes 1000000 | tf_op jit(solution)/shard_map/order_keys/pallas_call | solution.py:365
  38.5 0.0 copy-start.1
  38.6 0.0 copy-start.11
  38.6 10.6 %all-to-all-done.2 = bf16[64,8,2048]{2,1,0:T(8,128)(2,1)S(1)} async-done(((bf16[64,8,2048]{2,1,0:T(8,128)(2,1)}), bf16[64,8,2048]{2,1,0:T(8,128)(2,1)S(1)}, u32[]{:S(2)}, u32[]{:S(2)}) %all-to-all-start.2) | async-done | bytes 2097184 | tf_op jit(solution)/shard_map/all_to_all | solution.py:617
  49.2 0.5 hand_on.1
  49.7 0.0 copy-start.4
  49.7 0.0 copy-start.18
  49.7 10.2 %all_to_all.27 = bf16[8,8,2048]{2,1,0:T(8,128)(2,1)S(1)} all-to-all(bf16[8,8,2048]{2,1,0:T(8,128)(2,1)S(1)} %bitcast.37), channel_id=1, replica_groups=mesh['y'=4,'x1'=2,'x0'=2,'z'=4,'c'=2] {'x0','z'}, dimensions={0} | all-to-all | bytes 524288 | tf_op jit(solution)/shard_map/all_to_all | solution.py:392
  59.9 0.0 copy-done.1
  59.9 0.0 copy-done.11
  59.9 1.7 %unpack_inbox.2.refs_0_ = bf16[256,2048]{1,0:T(8,128)(2,1)} custom-call(bf16[256,512]{1,0:T(8,128)(2,1)S(1)} %copy-done.1, bf16[256,128]{1,0:T(8,128)(2,1)S(1)} %copy-done.11, bf16[512,2048]{1,0:T(8,128)(2,1)S(1)} %bitcast.35, bf16[64,2048]{1,0:T(8,128)(2,1)S(1)} %bitcast.36), custom_call_target="tpu_custom_call" | custom-call | flops 1000000000 | bytes 3000000 | tf_op jit(solution)/shard_map/unpack_inbox/pallas_call | solution.py:410
  61.6 0.0 copy-start.2
  61.7 0.1 collective-permute-start.2
  61.8 0.0 copy-done.4
  61.8 0.0 copy-done.18
  61.8 15.4 %render_xz.2 = (s16[256,2048]{1,0:T(8,128)(2,1)}, f32[4,32,8,256]{3,2,1,0:T(8,128)}) custom-call(s32[4]{0:T(128)S(1)} %pad_add_fusion.1.pos_ref, f32[2,4]{1,0:T(2,128)S(1)} %copy-done.18, bf16[256,2048]{1,0:T(8,128)(2,1)} %unpack_inbox.2.refs_0_, bf16[2,256,128]{2,1,0:T(8,128)(2,1)S(1)} %copy-done.4), custom_call_target="tpu_custom_call" | custom-call | flops 10000000000 | bytes 10000000 | tf_op jit(solution)/shard_map/render_xz/pallas_call | solution.py:519
  77.2 0.0 collective-permute-done.2.refs_1_
  77.2 0.0 copy-done.2
  77.2 13.4 %render_x.2 = s16[256,2048]{1,0:T(8,128)(2,1)} custom-call(s32[4]{0:T(128)S(1)} %pad_add_fusion.1.pos_ref, f32[2,4]{1,0:T(2,128)S(1)} %copy-done.18, bf16[256,2048]{1,0:T(8,128)(2,1)} %unpack_inbox.2.refs_0_, bf16[256,2048]{1,0:T(8,128)(2,1)S(1)} %collective-permute-done.2.refs_1_, ...), custom_call_target="tpu_custom_call", output_to_operand_aliasing={{}: (5, {})} | custom-call | flops 10000000000 | bytes 10000000 | tf_op jit(solution)/shard_map/render_x/pallas_call | solution.py:519
  90.5 3.9 %all-to-all-start.4 = ((s16[16,16,2048]{2,1,0:T(8,128)(2,1)}), s16[16,16,2048]{2,1,0:T(8,128)(2,1)S(1)}, u32[]{:S(2)}, u32[]{:S(2)}) async-start(s16[16,16,2048]{2,1,0:T(8,128)(2,1)} %bitcast.42), calls=%async_computation.4 | async-start | bytes 2097152 | tf_op jit(solution)/shard_map/all_to_all | solution.py:622
  94.4 0.0 copy-start.6
  94.4 13.3 %render_z.2.second_ref = f32[4,32,8,256]{3,2,1,0:T(8,128)} custom-call(s32[4]{0:T(128)S(1)} %pad_add_fusion.1.pos_ref, f32[2,4]{1,0:T(2,128)S(1)} %copy-done.18, bf16[256,2048]{1,0:T(8,128)(2,1)} %unpack_inbox.2.refs_0_, bf16[256,2048]{1,0:T(8,128)(2,1)S(1)} %collective-permute-done.2.refs_1_, bf16[2,256,256]{2,1,0:T(8,128)(2,1)S(1)} %copy-done.2), custom_call_target="tpu_custom_call" | custom-call | flops 10000000000 | bytes 10000000 | tf_op jit(solution)/shard_map/render_z/pallas_call | solution.py:519
  107.7 0.0 copy-done.6
  107.7 0.0 copy-start.8
  107.7 1.2 %copy-done.8 = f32[4,32,8,256]{3,2,1,0:T(8,128)S(1)} copy-done((f32[4,32,8,256]{3,2,1,0:T(8,128)S(1)}, f32[4,32,8,256]{3,2,1,0:T(8,128)}, u32[]{:S(2)}) %copy-start.8) | copy-done | bytes 1048600
  108.9 2.5 %compose_z.2 = f32[4,16,128]{2,1,0:T(8,128)} custom-call(s32[4]{0:T(128)S(1)} %pad_add_fusion.1.pos_ref, bf16[256,256]{1,0:T(8,128)(2,1)S(1)} %get-tuple-element.447.ahead_ref, f32[4,32,8,256]{3,2,1,0:T(8,128)S(1)} %copy-done.6, f32[4,32,8,256]{3,2,1,0:T(8,128)S(1)} %copy-done.8), custom_call_target="tpu_custom_call" | custom-call | flops 1000000000 | bytes 4000000 | tf_op jit(solution)/shard_map/compose_z/pallas_call | solution.py:570
  111.5 1.9 %all-to-all-done.4 = s16[16,16,2048]{2,1,0:T(8,128)(2,1)S(1)} async-done(((s16[16,16,2048]{2,1,0:T(8,128)(2,1)}), s16[16,16,2048]{2,1,0:T(8,128)(2,1)S(1)}, u32[]{:S(2)}, u32[]{:S(2)}) %all-to-all-start.4) | async-done | bytes 1048608 | tf_op jit(solution)/shard_map/all_to_all | solution.py:622
  113.4 2.5 %compose_x.2 = f32[4,16,128]{2,1,0:T(8,128)} custom-call(s32[4]{0:T(128)S(1)} %pad_add_fusion.1.pos_ref, bf16[256,256]{1,0:T(8,128)(2,1)S(1)} %get-tuple-element.448.ahead_ref, s16[256,2048]{1,0:T(8,128)(2,1)S(1)} %bitcast.38), custom_call_target="tpu_custom_call" | custom-call | flops 1000000000 | bytes 1000000 | tf_op jit(solution)/shard_map/compose_x/pallas_call | solution.py:600
  115.8 0.6 while.23
  (5 shorter events, 0.1 us)
Async XLA Ops:
  0.6 3.1 %collective-permute-start.1 = (bf16[128,4096]{1,0:T(8,128)(2,1)}, bf16[128,4096]{1,0:T(8,128)(2,1)}, u32[]{:S(2)}, u32[]{:S(2)}) collective-permute-start(bf16[128,4096]{1,0:T(8,128)(2,1)} %bricks_ref.1), channel_id=1, source_target_pairs={{0,1},{1,0},{2,3},{3,2},{4,5},{5,4},{6,7},{7,6},{8,9},{9,8},{10,11... | collective-permute-start | bytes 3145736 | tf_op jit(solution)/shard_map/ppermute | solution.py:612
  3.1 4.0 %copy-start.13 = (s32[2,16384]{1,0:T(2,128)S(1)}, s32[2,16384]{1,0:T(2,128)}, u32[]{:S(2)}) copy-start(s32[2,16384]{1,0:T(2,128)} %param.15) | copy-start | bytes 393220
  3.1 4.4 %copy-start.15 = (s32[16384,1]{0,1:T(1,128)S(1)}, s32[16384,1]{0,1:T(1,128)}, u32[]{:S(2)}) copy-start(s32[16384,1]{0,1:T(1,128)} %param.13) | copy-start | bytes 196612
  3.1 4.6 %copy-start.14 = (s32[16384]{0:T(1024)S(1)}, s32[16384]{0:T(1024)}, u32[]{:S(2)}) copy-start(s32[16384]{0:T(1024)} %param.14) | copy-start | bytes 196612
  7.8 41.4 %all-to-all-start.2 = ((bf16[64,8,2048]{2,1,0:T(8,128)(2,1)}), bf16[64,8,2048]{2,1,0:T(8,128)(2,1)S(1)}, u32[]{:S(2)}, u32[]{:S(2)}) async-start(bf16[64,8,2048]{2,1,0:T(8,128)(2,1)} %bitcast.41), calls=%async_computation.2 | async-start | bytes 4194304 | tf_op jit(solution)/shard_map/all_to_all | solution.py:617
  38.5 21.4 %copy-start.1 = (bf16[256,512]{1,0:T(8,128)(2,1)S(1)}, bf16[256,512]{1,0:T(8,128)(2,1)}, u32[]{:S(2)}) copy-start(bf16[256,512]{1,0:T(8,128)(2,1)} %get-tuple-element.181.place_ref) | copy-start | bytes 786436
  38.6 21.4 %copy-start.11 = (bf16[256,128]{1,0:T(8,128)(2,1)S(1)}, bf16[256,128]{1,0:T(8,128)(2,1)}, u32[]{:S(2)}) copy-start(bf16[256,128]{1,0:T(8,128)(2,1)} %get-tuple-element.444.relay_ref) | copy-start | bytes 196612
  49.7 12.1 %copy-start.4 = (bf16[2,256,128]{2,1,0:T(8,128)(2,1)S(1)}, bf16[2,256,128]{2,1,0:T(8,128)(2,1)}, u32[]{:S(2)}) copy-start(bf16[2,256,128]{2,1,0:T(8,128)(2,1)} %constant.66.clone.refs_1_) | copy-start | bytes 393220
  49.7 12.1 %copy-start.18 = (f32[2,4]{1,0:T(2,128)S(1)}, f32[2,4]{1,0:T(2,128)}, u32[]{:S(2)}) copy-start(f32[2,4]{1,0:T(2,128)} %transfer_ref.5) | copy-start | bytes 100
  61.6 15.5 %copy-start.2 = (bf16[2,256,256]{2,1,0:T(8,128)(2,1)S(1)}, bf16[2,256,256]{2,1,0:T(8,128)(2,1)}, u32[]{:S(2)}) copy-start(bf16[2,256,256]{2,1,0:T(8,128)(2,1)} %constant.67.clone.refs_2_) | copy-start | bytes 786436
  61.7 15.5 %collective-permute-start.2 = (bf16[256,2048]{1,0:T(8,128)(2,1)}, bf16[256,2048]{1,0:T(8,128)(2,1)S(1)}, u32[]{:S(2)}, u32[]{:S(2)}) collective-permute-start(bf16[256,2048]{1,0:T(8,128)(2,1)} %unpack_inbox.2.refs_0_), channel_id=1, source_target_pairs={{0,1},{1,0},{2,3},{3,2},{4,5},{5,4},{6,7},{7,6},{8,9},{9,8},{10,11... | collective-permute-start | bytes 3145736 | tf_op jit(solution)/shard_map/ppermute | solution.py:612
  90.5 22.8 %all-to-all-start.4 = ((s16[16,16,2048]{2,1,0:T(8,128)(2,1)}), s16[16,16,2048]{2,1,0:T(8,128)(2,1)S(1)}, u32[]{:S(2)}, u32[]{:S(2)}) async-start(s16[16,16,2048]{2,1,0:T(8,128)(2,1)} %bitcast.42), calls=%async_computation.4 | async-start | bytes 2097152 | tf_op jit(solution)/shard_map/all_to_all | solution.py:622
  94.4 13.3 %copy-start.6 = (f32[4,32,8,256]{3,2,1,0:T(8,128)S(1)}, f32[4,32,8,256]{3,2,1,0:T(8,128)}, u32[]{:S(2)}) copy-start(f32[4,32,8,256]{3,2,1,0:T(8,128)} %get-tuple-element.185.first_ref) | copy-start | bytes 3145732
  107.7 1.2 %copy-start.8 = (f32[4,32,8,256]{3,2,1,0:T(8,128)S(1)}, f32[4,32,8,256]{3,2,1,0:T(8,128)}, u32[]{:S(2)}) copy-start(f32[4,32,8,256]{3,2,1,0:T(8,128)} %render_z.2.second_ref) | copy-start | bytes 3145732
